TPU v7x, 512 devices: a whole 4x4x16 slice. The times are simulated.
512 devices in a mesh: segment: 2 (over x_hi), lat: 8 (over y, core), lon: 32 (over x_lo, z).
Axes of the slice: x: 4 (x_hi: 2, x_lo: 2; x = x_hi * 2 + x_lo), y: 4, z: 16, core: 2. Of those that a mesh axis runs over, the one named last changes fastest.
Arguments:
- inputs: bfloat16 [2, 16, 1440, 256], P(None, 'lat', 'lon'), may hold values from -6 to 6
- cotangent: bfloat16 [2, 16, 1440, 256], P(None, 'lat', 'lon'), may hold values from -6 to 6
- weights: bfloat16 [2, 2304, 256], P('segment'), may hold values from -0.125 to 0.125
- psi: bfloat16 [9, 16, 3, 17], replicated, may hold values from -1.25 to 1.25
- band_half: int32 [16, 3], replicated, may hold values from 1 to 8, as said below
Outputs:
- sections: bfloat16 [2, 2, 16, 1440, 256], P('segment', None, 'lat', 'lon')
- weight_grads: float32 [2, 2304, 256], P('segment')
Inputs may be any that keep to these rules, and one draw needn't show every extreme that they name: `band_half`: rows 0 and 15 have the half-width 8 at every offset.
All inputs are finite; a program needn't handle non-finite values.
Results may differ from a plain program's by a relative error of at most 0.0076.
Values may be sent and summed in bfloat16 or wider, within the bound.
No kernel may reach another device: no remote copies, remote signals or barrier semaphores. Data moves between devices by JAX's collectives and lax.ppermute only.
A program may use at most 64 MiB of HBM per device.

v0:
```python
import jax
import jax.numpy as jnp
from jax import lax
from jax.sharding import PartitionSpec as P


def with_halo(cells, sides, width, closed):
    for axis, dim in sides:
        count = lax.axis_size(axis)
        ends = count if closed else count - 1
        head = lax.slice_in_dim(cells, 0, width, axis=dim)
        tail = lax.slice_in_dim(cells, cells.shape[dim] - width, cells.shape[dim], axis=dim)
        cells = jnp.concatenate(
            [
                lax.ppermute(tail, axis, [(i, (i + 1) % count) for i in range(ends)]),
                cells,
                lax.ppermute(head, axis, [((i + 1) % count, i) for i in range(ends)]),
            ],
            axis=dim,
        )
    return cells


def shifted(block, axis, distance):
    devices = range(lax.axis_size(axis))
    route = [(i - distance, i) for i in devices if i - distance in devices]
    return lax.ppermute(block, axis, route)


def tap_table(lond, width, flipped):
    shape = (lond, lond + width - 1, width)
    outer = lax.broadcasted_iota(jnp.int32, shape, 0)
    inner = lax.broadcasted_iota(jnp.int32, shape, 1)
    tapped = lax.broadcasted_iota(jnp.int32, shape, 2)
    if flipped:
        tapped = width - 1 - tapped
    return (inner - outer == tapped).astype(jnp.bfloat16)


def gelu_back(preact, incoming):
    return jax.vjp(jax.nn.gelu, preact)[1](incoming)[0]


def shards(inputs, cotangent, weights, psi, band_half):
    micro, latd, lond, chans = inputs.shape
    kernels = psi.shape[0]
    width = psi.shape[3]
    reach = (width - 1) // 2
    segment_first = lax.axis_index("segment") == 0
    lat_start = lax.axis_index("lat") * latd
    taps = lax.broadcasted_iota(jnp.int32, psi.shape, 3)
    live = jnp.abs(taps - reach) <= band_half[None, :, :, None]
    effective = jnp.where(live, psi, jnp.zeros_like(psi))
    padded = jnp.pad(effective, ((0, 0), (1, 1), (0, 0), (0, 0)))
    forward_rows = lax.dynamic_slice_in_dim(padded, lat_start + 1, latd, 1)
    toeplitz = jnp.einsum(
        "krab,ojb->kraoj",
        forward_rows,
        tap_table(lond, width, False),
        preferred_element_type=jnp.float32,
    ).astype(jnp.bfloat16)
    adjoint = jnp.stack(
        [
            jnp.einsum(
                "kib,ojb->kioj",
                lax.dynamic_slice_in_dim(padded[:, :, offset], lat_start + 2 - offset, latd, 1),
                tap_table(lond, width, True),
                preferred_element_type=jnp.float32,
            )
            for offset in range(3)
        ],
        axis=2,
    ).astype(jnp.bfloat16)
    matrix = weights[0]

    def extend(field):
        rowwise = with_halo(field, (("lat", 1),), 1, False)
        return with_halo(rowwise, (("lon", 2),), reach, True)

    def forward_windows(extended):
        return jnp.stack([extended[:, offset : offset + latd] for offset in range(3)], axis=2)

    def layer(field):
        windows = forward_windows(extend(field))
        count = field.shape[0]
        raw = jnp.einsum(
            "kiaoj,miajc->ikomc", toeplitz, windows, preferred_element_type=jnp.float32
        )
        basis = jnp.transpose(raw.astype(jnp.bfloat16), (3, 0, 2, 1, 4))
        basis = basis.reshape(count, latd, lond, kernels * chans)
        preact = jnp.einsum("mioq,qc->mioc", basis, matrix, preferred_element_type=jnp.float32)
        result = (field.astype(jnp.float32) + jax.nn.gelu(preact)).astype(jnp.bfloat16)
        return (result, basis, preact)

    out_early, basis_early, preact_early = layer(inputs)
    carried = shifted(out_early, "segment", 1)
    out_late, basis_late, preact_late = layer(carried)
    own_output = jnp.where(segment_first, out_early, out_late)
    own_basis = jnp.where(segment_first, basis_early, basis_late)
    own_preact = jnp.where(segment_first, preact_early, preact_late)
    units_last = gelu_back(own_preact, cotangent.astype(jnp.float32)).astype(jnp.bfloat16)
    mixed = jnp.einsum("miod,qd->mioq", units_last, matrix, preferred_element_type=jnp.float32)
    rowwise = with_halo(mixed.astype(jnp.bfloat16), (("lat", 1),), 1, False).astype(mixed.dtype)
    extended = with_halo(rowwise.astype(jnp.bfloat16), (("lon", 2),), reach, True).astype(
        rowwise.dtype
    )
    spread = extended.reshape(micro, latd + 2, lond + 2 * reach, kernels, chans)
    folded = jnp.einsum(
        "kiaoj,miajkc->iomc",
        adjoint.astype(jnp.float32),
        jnp.stack([spread[:, 2 - offset : 2 - offset + latd] for offset in range(3)], axis=2),
        precision=lax.Precision.HIGHEST,
    )
    back_band = jnp.transpose(folded, (2, 0, 1, 3))
    grad_first = (cotangent.astype(jnp.float32) + back_band).astype(jnp.bfloat16)
    returned = shifted(grad_first, "segment", -1)
    own_grad = jnp.where(segment_first, returned, cotangent)
    own_units = gelu_back(own_preact, own_grad.astype(jnp.float32)).astype(jnp.bfloat16)
    local_grads = lax.dot_general(
        own_basis.reshape(-1, kernels * chans),
        own_units.reshape(-1, chans),
        (((0,), (0,)), ((), ())),
        preferred_element_type=jnp.float32,
    )
    total_grads = lax.psum(local_grads, ("lat", "lon"))
    return (own_output[None], total_grads[None])


def solution(mesh):
    placed = (
        P(None, "lat", "lon", None),
        P(None, "lat", "lon", None),
        P("segment", None, None),
        P(),
        P(),
    )
    return jax.shard_map(
        shards,
        mesh=mesh,
        in_specs=placed,
        out_specs=(P("segment", None, "lat", "lon", None), P("segment", None, None)),
        check_vma=False,
    )
```

profile of v0, /device:TPU:1, one launch (start us, length us, event | category | flops | bytes accessed | tf_op | source)
XLA Modules:
  0.0 2129.0 jit_solution(506036587850112733)
XLA Ops:
  7.2 1.2 fusion.130
  8.4 4.6 collective-permute-start
  13.0 5.5 collective-permute-start.1
  18.6 0.8 copy.56
  19.3 1.0 compare_select_fusion
  20.4 1.0 constant_dynamic-update-slice_fusion.1
  21.4 9.2 collective-permute-start.3
  30.5 1.9 collective-permute-start.2
  33.5 3.9 collective-permute-done.2
  38.4 1.3 reshape.20
  39.7 2.2 fusion.64
  41.9 4.4 collective-permute-start.4
  46.3 2.2 collective-permute-done.4
  48.5 4.7 collective-permute-start.5
  53.2 1.9 collective-permute-start.6
  55.2 3.4 collective-permute-done.6
  58.6 1.9 collective-permute-start.8
  60.5 3.4 collective-permute-start.7
  63.9 3.4 collective-permute-done.7
  68.4 1.3 reshape.21
  70.2 0.7 copy-done.14
  71.6 0.9 copy-done.1
  72.5 0.8 fusion.126
  73.4 1.9 collective-permute-start.10
  75.3 3.6 collective-permute-start.9
  79.0 0.7 pad_slice_fusion.2
  80.0 3.2 collective-permute-done.10
  83.2 0.8 copy-done.13
  84.2 1.6 pad_maximum_fusion
  85.8 0.9 fusion.125
  86.7 1.9 collective-permute-start.12
  88.6 3.5 collective-permute-start.11
  92.2 1.0 fusion.10
  93.2 1.0 fusion.8
  94.2 2.3 pad_maximum_fusion.1
  96.5 2.6 reshape.38
  99.1 2.5 copy.73
  101.6 1.7 maximum_convert_fusion
  103.4 1.0 slice_bitcast_fusion.2
  104.6 2.9 fusion.22
  107.6 1.4 collective-permute-start.13
  109.0 0.9 broadcast_select_fusion
  109.9 4.7 collective-permute-done.13
  114.6 2.1 convolution_bitcast_fusion
  116.7 0.9 copy-done.10
  117.7 0.7 copy.79
  118.4 2000.6 %all-reduce.3.cloned.1.call-done = f32[1,2304,256]{2,1,0:T(8,128)} async-done(((f32[1,2304,256]{2,1,0:T(8,128)}), f32[1,2304,256]{2,1,0:T(8,128)}) %all-reduce.3.cloned.1.call-update) | async-done | bytes 2359312 | tf_op jit(solution)/shard_map/psum | solution.py:125
  2119.0 3.2 copy.142
  (72 shorter events, 5.3 us)
Async XLA Ops:
  7.2 32.5 %copy-start = (bf16[1,2304,256]{2,1,0:T(8,128)(2,1)S(1)}, bf16[1,2304,256]{2,1,0:T(8,128)(2,1)}, u32[]{:S(2)}) copy-start(bf16[1,2304,256]{2,1,0:T(8,128)(2,1)} %param.7) | copy-start | bytes 3538948
  7.2 2111.8 %all-reduce.3.cloned.1.call-start = ((), (), s32[]{:S(2)}) async-start(), calls=%async_computation | async-start | bytes 4718592 | tf_op jit(solution)/shard_map/psum | solution.py:125
  8.4 11.9 collective-permute-start
  13.0 8.3 collective-permute-start.1
  20.3 17.0 copy-start.6
  21.4 12.1 collective-permute-start.3
  30.5 6.8 collective-permute-start.2
  33.4 4.4 copy-start.11
  39.7 27.7 %copy-start.2 = (bf16[2,2,45,2304]{3,1,2,0:T(2,128)(2,1)}, bf16[2,2,45,2304]{3,1,2,0:T(2,128)(2,1)S(1)}, u32[]{:S(2)}) copy-start(bf16[2,2,45,2304]{3,1,2,0:T(2,128)(2,1)S(1)} %reshape.20) | copy-start | bytes 2488324
  39.7 27.7 %copy-start.12 = (bf16[9,2,3,45,61]{4,1,3,2,0:T(2,128)(2,1)S(1)}, bf16[9,2,3,45,61]{4,1,3,2,0:T(2,128)(2,1)}, u32[]{:S(2)}) copy-start(bf16[9,2,3,45,61]{4,1,3,2,0:T(2,128)(2,1)} %copy-done.11) | copy-start | bytes 889384
  41.9 16.7 copy-start.18
  41.9 6.6 collective-permute-start.4
  48.5 6.6 copy-start.9
  48.5 6.6 collective-permute-start.5
  53.2 5.4 collective-permute-start.6
  58.6 5.3 collective-permute-start.8
  60.5 6.8 collective-permute-start.7
  69.7 1.9 copy-start.4
  69.7 1.1 copy-start.14
  69.7 1.3 copy-start.16
  70.1 8.8 copy-start.7
  71.6 0.9 copy-start.1
  73.4 9.8 collective-permute-start.10
  75.3 8.9 collective-permute-start.9
  83.2 0.8 copy-start.13
  86.7 14.9 collective-permute-start.12
  88.6 13.0 collective-permute-start.11
  103.3 1.2 copy-start.8
  103.4 1.2 copy-start.17
  104.6 4.4 copy-start.3
  104.6 4.4 copy-start.5
  107.6 7.1 copy-start.15
  107.6 7.1 collective-permute-start.13
  116.7 0.9 copy-start.10
  116.7 0.9 copy-start.19
Sparse Core Ops, SparseCore 0:
  116.8 2002.1 all-reduce.2
where the time goes:
time: 2140 us; the launch traced here: 2130 us
  waiting for transfers between devices  2020 us (94%)
  starting transfers between devices  49.8 us (2%)
  local copies, waits for them, and re-layouts  23.4 us (1%)
    psum x1, waiting for transfers between devices, shards(): total_grads = lax.psum(local_grads, ('lat', 'lon'))  2000 us
  transfers between devices with their start and end apart: 15, of which 8 were waited for; matrix products, arithmetic and copies ran while one was open for 1% of the time, Pallas kernels for 0%

commit v1 on v0

--- a/solution.py
+++ b/solution.py
@@ -39,6 +39,41 @@
 
 def gelu_back(preact, incoming):
     return jax.vjp(jax.nn.gelu, preact)[1](incoming)[0]
+
+
+def neighbours_summed(grads):
+    lats, lons = lax.axis_size("lat"), lax.axis_size("lon")
+    rows, chans = grads.shape
+    half = rows // 2
+    depth = 16
+    planes = lons // depth
+    columns = lats // 2 * planes
+    swap = [(i, i ^ 1) for i in range(lats)]
+    near = [
+        [(2 * y + core) * lons + x * depth + z for y in range(lats // 2) for x in range(planes)]
+        for core in range(2)
+        for z in range(depth)
+    ]
+    far = [[x * depth + z for z in range(depth)] for x in range(planes)]
+    core = lax.axis_index("lat") % 2
+    halves = grads.reshape(2, half, chans)
+    keep = lax.dynamic_index_in_dim(halves, core, 0, keepdims=False)
+    give = lax.dynamic_index_in_dim(halves, 1 - core, 0, keepdims=False).astype(jnp.bfloat16)
+    own = (keep + lax.ppermute(give, "lat", swap).astype(jnp.float32)).astype(jnp.bfloat16)
+    own = own.reshape(columns, half // columns, chans)
+    own = lax.all_to_all(own, ("lat", "lon"), 0, 0, axis_index_groups=near)
+    own = jnp.sum(own.astype(jnp.float32), axis=0).astype(jnp.bfloat16)
+    own = own.reshape(depth, half // columns // depth, chans)
+    own = lax.all_to_all(own, "lon", 0, 0, axis_index_groups=far)
+    own = jnp.sum(own.astype(jnp.float32), axis=0).astype(jnp.bfloat16)
+    own = jnp.broadcast_to(own[None], (depth,) + own.shape)
+    own = lax.all_to_all(own, "lon", 0, 0, axis_index_groups=far).reshape(-1, chans)
+    own = jnp.broadcast_to(own[None], (columns,) + own.shape)
+    own = lax.all_to_all(own, ("lat", "lon"), 0, 0, axis_index_groups=near).reshape(-1, chans)
+    other = lax.ppermute(own, "lat", swap)
+    first = jnp.where(core == 0, own, other)
+    second = jnp.where(core == 0, other, own)
+    return jnp.concatenate([first, second], axis=0).astype(jnp.float32)
 
 
 def shards(inputs, cotangent, weights, psi, band_half):
@@ -122,7 +157,7 @@
         (((0,), (0,)), ((), ())),
         preferred_element_type=jnp.float32,
     )
-    total_grads = lax.psum(local_grads, ("lat", "lon"))
+    total_grads = neighbours_summed(local_grads)
     return (own_output[None], total_grads[None])
 
 

time: 2140 us -> 187 us (0.09)
  waiting for transfers between devices: 2020 us -> 23.2 us
  blocking collectives: 0 us -> 60.3 us
    psum x1 -> x0, waiting for transfers between devices: 2000 us -> none  [shards(): total_grads = lax.psum(local_grads, ('lat', 'lon'))]
    all_to_all x0 -> x4, blocking collectives: none -> 60.3 us  [the longest x1 16.9 us: neighbours_summed(): own = lax.all_to_all(own, ('lat', 'lon'), 0, 0, axis_index_groups=near)]
  transfers between devices with their start and end apart: 15 -> 16, of which waited for: 8 -> 9; matrix products, arithmetic and copies ran while one was open for 1% -> 9% of each run, Pallas kernels for 0% -> 0%
where the time goes in v1:
time: 187 us; the launch traced here: 186 us
  blocking collectives  60.3 us (32%)
  starting transfers between devices  58.8 us (31%)
  waiting for transfers between devices  23.2 us (12%)
  local copies, waits for them, and re-layouts  20.8 us (11%)
  matrix products  11.9 us (6%)
  other arithmetic  9.97 us (5%)
    ppermute x6, starting transfers between devices, with_halo(): lax.ppermute(head, axis, [((i + 1) % count, i) for i in range(ends)])  22.3 us
    ppermute x6, starting transfers between devices, with_halo(): lax.ppermute(tail, axis, [(i, (i + 1) % count) for i in range(ends)])  21.7 us
    all_to_all x1, blocking collectives, neighbours_summed(): own = lax.all_to_all(own, ('lat', 'lon'), 0, 0, axis_index_groups=near)  16.9 us
    all_to_all x1, blocking collectives, neighbours_summed(): lax.all_to_all(own, 'lon', 0, 0, axis_index_groups=far).reshape(-1, chans)  16.9 us
    all_to_all x1, blocking collectives, neighbours_summed(): own = lax.all_to_all(own, 'lon', 0, 0, axis_index_groups=far)  15.2 us
    all_to_all x1, blocking collectives, neighbours_summed(): lax.all_to_all(own, ('lat', 'lon'), 0, 0, axis_index_groups=near)  11.3 us
    ppermute x6, waiting for transfers between devices, with_halo(): lax.ppermute(tail, axis, [(i, (i + 1) % count) for i in range(ends)])  7.64 us
    ppermute x1, starting transfers between devices, neighbours_summed(): other = lax.ppermute(own, 'lat', swap)  7.2 us
  transfers between devices with their start and end apart: 16, of which 9 were waited for; matrix products, arithmetic and copies ran while one was open for 9% of the time, Pallas kernels for 0%

profile of v1, /device:TPU:1, one launch (start us, length us, event | category | flops | bytes accessed | tf_op | source)
XLA Modules:
  0.0 186.3 jit_solution(799702114511013393)
XLA Ops:
  0.6 1.2 fusion.115
  1.9 4.6 %collective-permute-start = (bf16[2,1,45,256]{3,2,0,1:T(8,128)(2,1)S(1)}, bf16[2,1,45,256]{3,2,0,1:T(8,128)(2,1)S(1)}, u32[]{:S(2)}, u32[]{:S(2)}) collective-permute-start(bf16[2,1,45,256]{3,2,0,1:T(8,128)(2,1)S(1)} %copy.131), channel_id=1, source_target_pairs={{0,32},{32,64},{64,96},{96,128},{128,160},{160,192},{192,224},{1,3... | collective-permute-start | bytes 138248 | tf_op jit(solution)/shard_map/ppermute | solution.py:15
  6.5 5.5 %collective-permute-start.1 = (bf16[2,1,45,256]{3,2,0,1:T(8,128)(2,1)S(1)}, bf16[2,1,45,256]{3,2,0,1:T(8,128)(2,1)S(1)}, u32[]{:S(2)}, u32[]{:S(2)}) collective-permute-start(bf16[2,1,45,256]{3,2,0,1:T(8,128)(2,1)S(1)} %copy.132), channel_id=1, source_target_pairs={{32,0},{64,32},{96,64},{128,96},{160,128},{192,160},{224,192},{33,... | collective-permute-start | bytes 138248 | tf_op jit(solution)/shard_map/ppermute | solution.py:17
  12.7 1.0 compare_select_fusion
  13.8 1.0 constant_dynamic-update-slice_fusion.1
  14.8 9.2 %collective-permute-start.3 = (bf16[2,4,8,256]{3,2,0,1:T(8,128)(2,1)S(1)}, bf16[2,4,8,256]{3,2,0,1:T(8,128)(2,1)S(1)}, u32[]{:S(2)}, u32[]{:S(2)}) collective-permute-start(bf16[2,4,8,256]{3,2,0,1:T(8,128)(2,1)S(1)} %get-tuple-element.29), channel_id=1, source_target_pairs={{1,0},{2,1},{3,2},{4,3},{5,4},{6,5},{7,6},{8,7},{9,8},{10,9},{11,1... | collective-permute-start | bytes 98312 | tf_op jit(solution)/shard_map/ppermute | solution.py:17
  24.0 1.9 %collective-permute-start.2 = (bf16[2,4,8,256]{3,2,0,1:T(8,128)(2,1)S(1)}, bf16[2,4,8,256]{3,2,0,1:T(8,128)(2,1)S(1)}, u32[]{:S(2)}, u32[]{:S(2)}) collective-permute-start(bf16[2,4,8,256]{3,2,0,1:T(8,128)(2,1)S(1)} %get-tuple-element.28), channel_id=1, source_target_pairs={{0,1},{1,2},{2,3},{3,4},{4,5},{5,6},{6,7},{7,8},{8,9},{9,10},{10,1... | collective-permute-start | bytes 98312 | tf_op jit(solution)/shard_map/ppermute | solution.py:15
  26.9 3.9 %collective-permute-done.2 = bf16[2,4,8,256]{3,2,0,1:T(8,128)(2,1)S(1)} collective-permute-done((bf16[2,4,8,256]{3,2,0,1:T(8,128)(2,1)S(1)}, bf16[2,4,8,256]{3,2,0,1:T(8,128)(2,1)S(1)}, u32[]{:S(2)}, u32[]{:S(2)}) %collective-permute-start.2) | collective-permute-done | bytes 32800 | tf_op jit(solution)/shard_map/ppermute | solution.py:15
  31.8 1.4 reshape.91
  33.2 2.4 %fusion.65 = (bf16[2,2,45,256]{3,2,1,0:T(8,128)(2,1)S(1)}, f32[2,2,45,256]{3,2,1,0:T(8,128)}) fusion(bf16[2,2,45,256]{3,1,2,0:T(2,128)(2,1)} %param.5, bf16[2,2,45,2304]{3,2,1,0:T(8,128)(2,1)} %reshape.91, bf16[1,2304,256]{2,1,0:T(8,128)(2,1)S(1)} %copy-done), kind=kOutput, calls=%fused_computation.90 | convolution fusion | flops 212843520 | bytes 2377728 | tf_op jit(solution)/shard_map/mioq,qc->mioc/dot_general | solution.py:126
  35.5 4.4 %collective-permute-start.4 = (bf16[2,2,45,256]{3,2,1,0:T(8,128)(2,1)S(1)}, bf16[2,2,45,256]{3,2,1,0:T(8,128)(2,1)S(1)}, u32[]{:S(2)}, u32[]{:S(2)}) collective-permute-start(bf16[2,2,45,256]{3,2,1,0:T(8,128)(2,1)S(1)} %get-tuple-element.34), channel_id=1, source_target_pairs={{0,256},{1,257},{2,258},{3,259},{4,260},{5,261},{6,262},{7,263},{8... | collective-permute-start | bytes 276488 | tf_op jit(solution)/shard_map/ppermute | solution.py:27
  39.9 2.2 %collective-permute-done.4 = bf16[2,2,45,256]{3,2,1,0:T(8,128)(2,1)S(1)} collective-permute-done((bf16[2,2,45,256]{3,2,1,0:T(8,128)(2,1)S(1)}, bf16[2,2,45,256]{3,2,1,0:T(8,128)(2,1)S(1)}, u32[]{:S(2)}, u32[]{:S(2)}) %collective-permute-start.4) | collective-permute-done | bytes 92192 | tf_op jit(solution)/shard_map/ppermute | solution.py:27
  42.1 4.7 %collective-permute-start.5 = (bf16[2,1,45,256]{3,2,1,0:T(8,128)(2,1)S(1)}, bf16[2,1,45,256]{3,2,1,0:T(8,128)(2,1)S(1)}, u32[]{:S(2)}, u32[]{:S(2)}) collective-permute-start(bf16[2,1,45,256]{3,2,1,0:T(8,128)(2,1)S(1)} %get-tuple-element.31), channel_id=1, source_target_pairs={{0,32},{32,64},{64,96},{96,128},{128,160},{160,192},{192,224},{1,3... | collective-permute-start | bytes 138248 | tf_op jit(solution)/shard_map/ppermute | solution.py:15
  46.8 1.9 %collective-permute-start.6 = (bf16[2,1,45,256]{3,2,1,0:T(8,128)(2,1)S(1)}, bf16[2,1,45,256]{3,2,1,0:T(8,128)(2,1)S(1)}, u32[]{:S(2)}, u32[]{:S(2)}) collective-permute-start(bf16[2,1,45,256]{3,2,1,0:T(8,128)(2,1)S(1)} %get-tuple-element.30), channel_id=1, source_target_pairs={{32,0},{64,32},{96,64},{128,96},{160,128},{192,160},{224,192},{33,... | collective-permute-start | bytes 138248 | tf_op jit(solution)/shard_map/ppermute | solution.py:17
  48.7 3.4 %collective-permute-done.6 = bf16[2,1,45,256]{3,2,1,0:T(8,128)(2,1)S(1)} collective-permute-done((bf16[2,1,45,256]{3,2,1,0:T(8,128)(2,1)S(1)}, bf16[2,1,45,256]{3,2,1,0:T(8,128)(2,1)S(1)}, u32[]{:S(2)}, u32[]{:S(2)}) %collective-permute-start.6) | collective-permute-done | bytes 46112 | tf_op jit(solution)/shard_map/ppermute | solution.py:17
  52.2 1.9 %collective-permute-start.8 = (bf16[2,4,8,256]{3,2,1,0:T(8,128)(2,1)S(1)}, bf16[2,4,8,256]{3,2,1,0:T(8,128)(2,1)S(1)}, u32[]{:S(2)}, u32[]{:S(2)}) collective-permute-start(bf16[2,4,8,256]{3,2,1,0:T(8,128)(2,1)S(1)} %get-tuple-element.27), channel_id=1, source_target_pairs={{1,0},{2,1},{3,2},{4,3},{5,4},{6,5},{7,6},{8,7},{9,8},{10,9},{11,1... | collective-permute-start | bytes 98312 | tf_op jit(solution)/shard_map/ppermute | solution.py:17
  54.1 3.4 %collective-permute-start.7 = (bf16[2,4,8,256]{3,2,1,0:T(8,128)(2,1)S(1)}, bf16[2,4,8,256]{3,2,1,0:T(8,128)(2,1)S(1)}, u32[]{:S(2)}, u32[]{:S(2)}) collective-permute-start(bf16[2,4,8,256]{3,2,1,0:T(8,128)(2,1)S(1)} %get-tuple-element.26), channel_id=1, source_target_pairs={{0,1},{1,2},{2,3},{3,4},{4,5},{5,6},{6,7},{7,8},{8,9},{9,10},{10,1... | collective-permute-start | bytes 98312 | tf_op jit(solution)/shard_map/ppermute | solution.py:15
  57.5 3.4 %collective-permute-done.7 = bf16[2,4,8,256]{3,2,1,0:T(8,128)(2,1)S(1)} collective-permute-done((bf16[2,4,8,256]{3,2,1,0:T(8,128)(2,1)S(1)}, bf16[2,4,8,256]{3,2,1,0:T(8,128)(2,1)S(1)}, u32[]{:S(2)}, u32[]{:S(2)}) %collective-permute-start.7) | collective-permute-done | bytes 32800 | tf_op jit(solution)/shard_map/ppermute | solution.py:15
  61.0 1.4 broadcast_select_fusion
  65.1 0.9 copy-done.1
  66.1 1.9 %collective-permute-start.10 = (bf16[2,1,45,2304]{3,2,1,0:T(8,128)(2,1)S(1)}, bf16[2,1,45,2304]{3,2,1,0:T(8,128)(2,1)S(1)}, u32[]{:S(2)}, u32[]{:S(2)}) collective-permute-start(bf16[2,1,45,2304]{3,2,1,0:T(8,128)(2,1)S(1)} %get-tuple-element.16), channel_id=1, source_target_pairs={{32,0},{64,32},{96,64},{128,96},{160,128},{192,160},{224,192},{33,... | collective-permute-start | bytes 1244168 | tf_op jit(solution)/shard_map/ppermute | solution.py:17
  68.0 3.6 %collective-permute-start.9 = (bf16[2,1,45,2304]{3,2,1,0:T(8,128)(2,1)S(1)}, bf16[2,1,45,2304]{3,2,1,0:T(8,128)(2,1)}, u32[]{:S(2)}, u32[]{:S(2)}) collective-permute-start(bf16[2,1,45,2304]{3,2,1,0:T(8,128)(2,1)S(1)} %get-tuple-element.15), channel_id=1, source_target_pairs={{0,32},{32,64},{64,96},{96,128},{128,160},{160,192},{192,224},{1,3... | collective-permute-start | bytes 1244168 | tf_op jit(solution)/shard_map/ppermute | solution.py:15
  72.0 3.6 %collective-permute-done.10 = bf16[2,1,45,2304]{3,2,1,0:T(8,128)(2,1)S(1)} collective-permute-done((bf16[2,1,45,2304]{3,2,1,0:T(8,128)(2,1)S(1)}, bf16[2,1,45,2304]{3,2,1,0:T(8,128)(2,1)S(1)}, u32[]{:S(2)}, u32[]{:S(2)}) %collective-permute-start.10) | collective-permute-done | bytes 414752 | tf_op jit(solution)/shard_map/ppermute | solution.py:17
  76.9 1.6 pad_maximum_fusion
  78.5 0.9 fusion.110
  79.4 1.9 %collective-permute-start.12 = (bf16[2,4,8,2304]{3,2,1,0:T(8,128)(2,1)}, bf16[2,4,8,2304]{3,2,1,0:T(8,128)(2,1)}, u32[]{:S(2)}, u32[]{:S(2)}) collective-permute-start(bf16[2,4,8,2304]{3,2,1,0:T(8,128)(2,1)} %get-tuple-element.12), channel_id=1, source_target_pairs={{1,0},{2,1},{3,2},{4,3},{5,4},{6,5},{7,6},{8,7},{9,8},{10,9},{11,1... | collective-permute-start | bytes 884744 | tf_op jit(solution)/shard_map/ppermute | solution.py:17
  81.3 3.5 %collective-permute-start.11 = (bf16[2,4,8,2304]{3,2,1,0:T(8,128)(2,1)}, bf16[2,4,8,2304]{3,2,1,0:T(8,128)(2,1)}, u32[]{:S(2)}, u32[]{:S(2)}) collective-permute-start(bf16[2,4,8,2304]{3,2,1,0:T(8,128)(2,1)} %get-tuple-element.11), channel_id=1, source_target_pairs={{0,1},{1,2},{2,3},{3,4},{4,5},{5,6},{6,7},{7,8},{8,9},{9,10},{10,1... | collective-permute-start | bytes 884744 | tf_op jit(solution)/shard_map/ppermute | solution.py:15
  84.8 1.1 fusion.10
  86.2 2.3 %pad_maximum_fusion.1 = bf16[9,2,3,45,61]{4,0,3,1,2:T(8,128)(2,1)} fusion(bf16[9,2,1,45,61]{4,0,3,1,2:T(8,128)(2,1)} %fusion.10, bf16[9,2,1,45,61]{4,0,3,1,2:T(8,128)(2,1)S(1)} %fusion.9, bf16[9,2,1,45,61]{4,0,3,1,2:T(8,128)(2,1)S(1)} %fusion.8), kind=kLoop, calls=%fused_computation.35 | loop fusion | flops 296460 | bytes 592920 | tf_op jit(solution)/shard_map/stack | solution.py:97
  88.5 2.6 %reshape.93 = bf16[2,4,45,9,256]{4,3,2,1,0:T(8,128)(2,1)} reshape(bf16[2,4,45,2304]{3,2,1,0:T(8,128)(2,1)S(1)} %pad_maximum_fusion) | data formatting | bytes 3317760 | tf_op jit(solution)/shard_map/concatenate | solution.py:13
  91.1 2.5 %copy.75 = bf16[2,4,45,9,256]{4,2,3,1,0:T(8,128)(2,1)S(1)} copy(bf16[2,4,45,9,256]{4,3,2,1,0:T(8,128)(2,1)} %reshape.93) | data formatting | bytes 3317760 | tf_op jit(solution)/shard_map/concatenate | solution.py:13
  93.6 1.7 maximum_convert_fusion
  95.3 1.0 slice_bitcast_fusion.2
  96.6 2.9 %fusion.23 = bf16[2,2,45,256]{3,2,1,0:T(8,128)(2,1)S(1)} fusion(f32[2,2,1,61,9,256]{5,3,4,2,1,0:T(8,128)S(1)} %get-tuple-element.9, f32[2,2,1,61,9,256]{5,3,4,2,1,0:T(8,128)S(1)} %get-tuple-element.10, f32[2,2,1,61,9,256]{5,3,4,2,1,0:T(8,128)S(1)} %get-tuple-element.8, bf16[9,2,3,45,61]{4,0,3,1,2:T(8,128)(2,1)S(1)} %copy-done.7, ...), kind=kOutput, calls=%fused_computation.34 | convolution fusion | flops 914236416 | bytes 7226892 | tf_op jit(solution)/shard_map/kiaoj,miajkc->iomc/dot_general | solution.py:143
  99.5 1.3 collective-permute-start.13
  102.0 1.2 dot_general.43
  103.2 3.3 %collective-permute-done.13 = bf16[2,2,45,256]{3,2,1,0:T(8,128)(2,1)S(1)} collective-permute-done((bf16[2,2,45,256]{3,2,1,0:T(8,128)(2,1)S(1)}, bf16[2,2,45,256]{3,2,1,0:T(8,128)(2,1)S(1)}, u32[]{:S(2)}, u32[]{:S(2)}) %collective-permute-start.13) | collective-permute-done | bytes 92192 | tf_op jit(solution)/shard_map/ppermute | solution.py:27
  107.3 1.7 fusion.26
  108.9 0.9 fusion.32
  109.8 1.9 %collective-permute-start.14 = (bf16[1152,256]{1,0:T(8,128)(2,1)}, bf16[1152,256]{1,0:T(8,128)(2,1)}, u32[]{:S(2)}, u32[]{:S(2)}) collective-permute-start(bf16[1152,256]{1,0:T(8,128)(2,1)} %fusion.32), channel_id=1, source_target_pairs={{0,32},{32,0},{64,96},{96,64},{128,160},{160,128},{192,224},{224,1... | collective-permute-start | bytes 1769480 | tf_op jit(solution)/shard_map/ppermute | solution.py:62
  111.7 2.3 %collective-permute-done.14 = bf16[1152,256]{1,0:T(8,128)(2,1)} collective-permute-done((bf16[1152,256]{1,0:T(8,128)(2,1)}, bf16[1152,256]{1,0:T(8,128)(2,1)}, u32[]{:S(2)}, u32[]{:S(2)}) %collective-permute-start.14) | collective-permute-done | bytes 589856 | tf_op jit(solution)/shard_map/ppermute | solution.py:62
  114.1 1.2 fusion.11
  115.3 16.9 %all_to_all.20 = bf16[8,144,256]{2,1,0:T(8,128)(2,1)S(1)} all-to-all(bf16[8,144,256]{2,1,0:T(8,128)(2,1)S(1)} %bitcast.151), channel_id=1, replica_groups={{0,16,64,80,128,144,192,208},{1,17,65,81,129,145,193,209},{2,18,66,82,1..., dimensions={0} | all-to-all | bytes 1179648 | tf_op jit(solution)/shard_map/all_to_all | solution.py:64
  132.3 15.2 %all_to_all.21 = bf16[16,9,256]{2,1,0:T(8,128)(2,1)S(1)} all-to-all(bf16[16,9,256]{2,1,0:T(8,128)(2,1)S(1)} %reshape.73), channel_id=1, replica_groups={{0,1,2,3,4,5,6,7,8,9,10,11,12,13,14,15},{16,17,18,19,20,21,22,23,24,25,..., dimensions={0} | all-to-all | bytes 147456 | tf_op jit(solution)/shard_map/all_to_all | solution.py:67
  147.6 16.9 %all_to_all.22 = bf16[16,9,256]{2,1,0:T(8,128)(2,1)S(1)} all-to-all(bf16[16,9,256]{2,1,0:T(8,128)(2,1)S(1)} %broadcast_in_dim.23), channel_id=1, replica_groups={{0,1,2,3,4,5,6,7,8,9,10,11,12,13,14,15},{16,17,18,19,20,21,22,23,24,25,..., dimensions={0} | all-to-all | bytes 147456 | tf_op jit(solution)/shard_map/all_to_all | solution.py:70
  164.5 11.3 %all_to_all.23 = bf16[8,144,256]{2,1,0:T(8,128)(2,1)S(1)} all-to-all(bf16[8,144,256]{2,1,0:T(8,128)(2,1)S(1)} %broadcast_in_dim.25), channel_id=1, replica_groups={{0,16,64,80,128,144,192,208},{1,17,65,81,129,145,193,209},{2,18,66,82,1..., dimensions={0} | all-to-all | bytes 1179648 | tf_op jit(solution)/shard_map/all_to_all | solution.py:72
  175.8 7.2 %collective-permute-start.15 = (bf16[1152,256]{1,0:T(8,128)(2,1)S(1)}, bf16[1152,256]{1,0:T(8,128)(2,1)S(1)}, u32[]{:S(2)}, u32[]{:S(2)}) collective-permute-start(bf16[1152,256]{1,0:T(8,128)(2,1)S(1)} %bitcast.150), channel_id=1, source_target_pairs={{0,32},{32,0},{64,96},{96,64},{128,160},{160,128},{192,224},{224,1... | collective-permute-start | bytes 1769480 | tf_op jit(solution)/shard_map/ppermute | solution.py:73
  184.7 1.6 maximum_convert_fusion.1
  (91 shorter events, 11.6 us)
Async XLA Ops:
  0.6 32.5 %copy-start = (bf16[1,2304,256]{2,1,0:T(8,128)(2,1)S(1)}, bf16[1,2304,256]{2,1,0:T(8,128)(2,1)}, u32[]{:S(2)}) copy-start(bf16[1,2304,256]{2,1,0:T(8,128)(2,1)} %param.7) | copy-start | bytes 3538948
  1.9 11.9 %collective-permute-start = (bf16[2,1,45,256]{3,2,0,1:T(8,128)(2,1)S(1)}, bf16[2,1,45,256]{3,2,0,1:T(8,128)(2,1)S(1)}, u32[]{:S(2)}, u32[]{:S(2)}) collective-permute-start(bf16[2,1,45,256]{3,2,0,1:T(8,128)(2,1)S(1)} %copy.131), channel_id=1, source_target_pairs={{0,32},{32,64},{64,96},{96,128},{128,160},{160,192},{192,224},{1,3... | collective-permute-start | bytes 138248 | tf_op jit(solution)/shard_map/ppermute | solution.py:15
  6.5 8.3 %collective-permute-start.1 = (bf16[2,1,45,256]{3,2,0,1:T(8,128)(2,1)S(1)}, bf16[2,1,45,256]{3,2,0,1:T(8,128)(2,1)S(1)}, u32[]{:S(2)}, u32[]{:S(2)}) collective-permute-start(bf16[2,1,45,256]{3,2,0,1:T(8,128)(2,1)S(1)} %copy.132), channel_id=1, source_target_pairs={{32,0},{64,32},{96,64},{128,96},{160,128},{192,160},{224,192},{33,... | collective-permute-start | bytes 138248 | tf_op jit(solution)/shard_map/ppermute | solution.py:17
  13.8 13.1 %copy-start.5 = (bf16[9,16,3,17]{3,0,2,1:T(8,128)(2,1)}, bf16[9,16,3,17]{3,0,2,1:T(8,128)(2,1)S(1)}, u32[]{:S(2)}) copy-start(bf16[9,16,3,17]{3,0,2,1:T(8,128)(2,1)S(1)} %compare_select_fusion) | copy-start | bytes 44068
  14.8 12.1 %collective-permute-start.3 = (bf16[2,4,8,256]{3,2,0,1:T(8,128)(2,1)S(1)}, bf16[2,4,8,256]{3,2,0,1:T(8,128)(2,1)S(1)}, u32[]{:S(2)}, u32[]{:S(2)}) collective-permute-start(bf16[2,4,8,256]{3,2,0,1:T(8,128)(2,1)S(1)} %get-tuple-element.29), channel_id=1, source_target_pairs={{1,0},{2,1},{3,2},{4,3},{5,4},{6,5},{7,6},{8,7},{9,8},{10,9},{11,1... | collective-permute-start | bytes 98312 | tf_op jit(solution)/shard_map/ppermute | solution.py:17
  24.0 6.8 %collective-permute-start.2 = (bf16[2,4,8,256]{3,2,0,1:T(8,128)(2,1)S(1)}, bf16[2,4,8,256]{3,2,0,1:T(8,128)(2,1)S(1)}, u32[]{:S(2)}, u32[]{:S(2)}) collective-permute-start(bf16[2,4,8,256]{3,2,0,1:T(8,128)(2,1)S(1)} %get-tuple-element.28), channel_id=1, source_target_pairs={{0,1},{1,2},{2,3},{3,4},{4,5},{5,6},{6,7},{7,8},{8,9},{9,10},{10,1... | collective-permute-start | bytes 98312 | tf_op jit(solution)/shard_map/ppermute | solution.py:15
  26.9 3.9 %copy-start.13 = (bf16[9,2,3,45,61]{4,1,3,2,0:T(2,128)(2,1)}, bf16[9,2,3,45,61]{4,1,3,2,0:T(2,128)(2,1)S(1)}, u32[]{:S(2)}) copy-start(bf16[9,2,3,45,61]{4,1,3,2,0:T(2,128)(2,1)S(1)} %copy.137) | copy-start | bytes 889384
  33.2 27.8 %copy-start.14 = (bf16[9,2,3,45,61]{4,1,3,2,0:T(2,128)(2,1)S(1)}, bf16[9,2,3,45,61]{4,1,3,2,0:T(2,128)(2,1)}, u32[]{:S(2)}) copy-start(bf16[9,2,3,45,61]{4,1,3,2,0:T(2,128)(2,1)} %copy-done.13) | copy-start | bytes 889384
  35.5 13.2 %copy-start.18 = (bf16[2,2,45,256]{3,2,1,0:T(8,128)(2,1)}, bf16[2,2,45,256]{3,2,1,0:T(8,128)(2,1)S(1)}, u32[]{:S(2)}) copy-start(bf16[2,2,45,256]{3,2,1,0:T(8,128)(2,1)S(1)} %get-tuple-element.34) | copy-start | bytes 276484
  35.5 6.6 %collective-permute-start.4 = (bf16[2,2,45,256]{3,2,1,0:T(8,128)(2,1)S(1)}, bf16[2,2,45,256]{3,2,1,0:T(8,128)(2,1)S(1)}, u32[]{:S(2)}, u32[]{:S(2)}) collective-permute-start(bf16[2,2,45,256]{3,2,1,0:T(8,128)(2,1)S(1)} %get-tuple-element.34), channel_id=1, source_target_pairs={{0,256},{1,257},{2,258},{3,259},{4,260},{5,261},{6,262},{7,263},{8... | collective-permute-start | bytes 276488 | tf_op jit(solution)/shard_map/ppermute | solution.py:27
  42.1 6.7 %copy-start.9 = (bf16[2,2,45,256]{3,2,1,0:T(8,128)(2,1)}, bf16[2,2,45,256]{3,2,1,0:T(8,128)(2,1)S(1)}, u32[]{:S(2)}) copy-start(bf16[2,2,45,256]{3,2,1,0:T(8,128)(2,1)S(1)} %collective-permute-done.4) | copy-start | bytes 276484
  42.1 6.6 %collective-permute-start.5 = (bf16[2,1,45,256]{3,2,1,0:T(8,128)(2,1)S(1)}, bf16[2,1,45,256]{3,2,1,0:T(8,128)(2,1)S(1)}, u32[]{:S(2)}, u32[]{:S(2)}) collective-permute-start(bf16[2,1,45,256]{3,2,1,0:T(8,128)(2,1)S(1)} %get-tuple-element.31), channel_id=1, source_target_pairs={{0,32},{32,64},{64,96},{96,128},{128,160},{160,192},{192,224},{1,3... | collective-permute-start | bytes 138248 | tf_op jit(solution)/shard_map/ppermute | solution.py:15
  46.8 5.4 %collective-permute-start.6 = (bf16[2,1,45,256]{3,2,1,0:T(8,128)(2,1)S(1)}, bf16[2,1,45,256]{3,2,1,0:T(8,128)(2,1)S(1)}, u32[]{:S(2)}, u32[]{:S(2)}) collective-permute-start(bf16[2,1,45,256]{3,2,1,0:T(8,128)(2,1)S(1)} %get-tuple-element.30), channel_id=1, source_target_pairs={{32,0},{64,32},{96,64},{128,96},{160,128},{192,160},{224,192},{33,... | collective-permute-start | bytes 138248 | tf_op jit(solution)/shard_map/ppermute | solution.py:17
  52.2 5.3 %collective-permute-start.8 = (bf16[2,4,8,256]{3,2,1,0:T(8,128)(2,1)S(1)}, bf16[2,4,8,256]{3,2,1,0:T(8,128)(2,1)S(1)}, u32[]{:S(2)}, u32[]{:S(2)}) collective-permute-start(bf16[2,4,8,256]{3,2,1,0:T(8,128)(2,1)S(1)} %get-tuple-element.27), channel_id=1, source_target_pairs={{1,0},{2,1},{3,2},{4,3},{5,4},{6,5},{7,6},{8,7},{9,8},{10,9},{11,1... | collective-permute-start | bytes 98312 | tf_op jit(solution)/shard_map/ppermute | solution.py:17
  54.1 6.8 %collective-permute-start.7 = (bf16[2,4,8,256]{3,2,1,0:T(8,128)(2,1)S(1)}, bf16[2,4,8,256]{3,2,1,0:T(8,128)(2,1)S(1)}, u32[]{:S(2)}, u32[]{:S(2)}) collective-permute-start(bf16[2,4,8,256]{3,2,1,0:T(8,128)(2,1)S(1)} %get-tuple-element.26), channel_id=1, source_target_pairs={{0,1},{1,2},{2,3},{3,4},{4,5},{5,6},{6,7},{7,8},{8,9},{9,10},{10,1... | collective-permute-start | bytes 98312 | tf_op jit(solution)/shard_map/ppermute | solution.py:15
  63.5 0.9 copy-start.11
  63.5 1.0 copy-start.16
  63.9 2.1 %copy-start.2 = (f32[2,2,45,256]{3,2,1,0:T(8,128)}, f32[2,2,45,256]{3,2,1,0:T(8,128)S(1)}, u32[]{:S(2)}) copy-start(f32[2,2,45,256]{3,2,1,0:T(8,128)S(1)} %fusion.13) | copy-start | bytes 552964
  64.5 7.2 %copy-start.6 = (bf16[9,16,3,17]{3,0,2,1:T(8,128)(2,1)S(1)}, bf16[9,16,3,17]{3,0,2,1:T(8,128)(2,1)}, u32[]{:S(2)}) copy-start(bf16[9,16,3,17]{3,0,2,1:T(8,128)(2,1)} %copy-done.5) | copy-start | bytes 44068
  65.1 0.9 copy-start.1
  66.1 9.6 %collective-permute-start.10 = (bf16[2,1,45,2304]{3,2,1,0:T(8,128)(2,1)S(1)}, bf16[2,1,45,2304]{3,2,1,0:T(8,128)(2,1)S(1)}, u32[]{:S(2)}, u32[]{:S(2)}) collective-permute-start(bf16[2,1,45,2304]{3,2,1,0:T(8,128)(2,1)S(1)} %get-tuple-element.16), channel_id=1, source_target_pairs={{32,0},{64,32},{96,64},{128,96},{160,128},{192,160},{224,192},{33,... | collective-permute-start | bytes 1244168 | tf_op jit(solution)/shard_map/ppermute | solution.py:17
  68.0 8.9 %collective-permute-start.9 = (bf16[2,1,45,2304]{3,2,1,0:T(8,128)(2,1)S(1)}, bf16[2,1,45,2304]{3,2,1,0:T(8,128)(2,1)}, u32[]{:S(2)}, u32[]{:S(2)}) collective-permute-start(bf16[2,1,45,2304]{3,2,1,0:T(8,128)(2,1)S(1)} %get-tuple-element.15), channel_id=1, source_target_pairs={{0,32},{32,64},{64,96},{96,128},{128,160},{160,192},{192,224},{1,3... | collective-permute-start | bytes 1244168 | tf_op jit(solution)/shard_map/ppermute | solution.py:15
  75.7 0.8 copy-start.15
  79.4 14.2 %collective-permute-start.12 = (bf16[2,4,8,2304]{3,2,1,0:T(8,128)(2,1)}, bf16[2,4,8,2304]{3,2,1,0:T(8,128)(2,1)}, u32[]{:S(2)}, u32[]{:S(2)}) collective-permute-start(bf16[2,4,8,2304]{3,2,1,0:T(8,128)(2,1)} %get-tuple-element.12), channel_id=1, source_target_pairs={{1,0},{2,1},{3,2},{4,3},{5,4},{6,5},{7,6},{8,7},{9,8},{10,9},{11,1... | collective-permute-start | bytes 884744 | tf_op jit(solution)/shard_map/ppermute | solution.py:17
  81.3 12.3 %collective-permute-start.11 = (bf16[2,4,8,2304]{3,2,1,0:T(8,128)(2,1)}, bf16[2,4,8,2304]{3,2,1,0:T(8,128)(2,1)}, u32[]{:S(2)}, u32[]{:S(2)}) collective-permute-start(bf16[2,4,8,2304]{3,2,1,0:T(8,128)(2,1)} %get-tuple-element.11), channel_id=1, source_target_pairs={{0,1},{1,2},{2,3},{3,4},{4,5},{5,6},{6,7},{7,8},{8,9},{9,10},{10,1... | collective-permute-start | bytes 884744 | tf_op jit(solution)/shard_map/ppermute | solution.py:15
  95.3 1.2 copy-start.7
  95.3 1.2 copy-start.17
  96.6 4.3 %copy-start.8 = (bf16[2,2,45,9,256]{4,2,0,3,1:T(8,128)(2,1)S(1)}, bf16[2,2,45,9,256]{4,2,0,3,1:T(8,128)(2,1)}, u32[]{:S(2)}) copy-start(bf16[2,2,45,9,256]{4,2,0,3,1:T(8,128)(2,1)} %get-tuple-element.36) | copy-start | bytes 2488324
  99.5 6.9 %collective-permute-start.13 = (bf16[2,2,45,256]{3,2,1,0:T(8,128)(2,1)S(1)}, bf16[2,2,45,256]{3,2,1,0:T(8,128)(2,1)S(1)}, u32[]{:S(2)}, u32[]{:S(2)}) collective-permute-start(bf16[2,2,45,256]{3,2,1,0:T(8,128)(2,1)S(1)} %fusion.23), channel_id=1, source_target_pairs={{256,0},{257,1},{258,2},{259,3},{260,4},{261,5},{262,6},{263,7},{2... | collective-permute-start | bytes 276488 | tf_op jit(solution)/shard_map/ppermute | solution.py:27
  101.6 4.8 %copy-start.3 = (f32[2,2,45,256]{3,2,1,0:T(8,128)S(1)}, f32[2,2,45,256]{3,2,1,0:T(8,128)}, u32[]{:S(2)}) copy-start(f32[2,2,45,256]{3,2,1,0:T(8,128)} %copy-done.2) | copy-start | bytes 552964
  101.6 4.8 %copy-start.12 = (f32[2,2,45,256]{3,2,1,0:T(8,128)S(1)}, f32[2,2,45,256]{3,2,1,0:T(8,128)}, u32[]{:S(2)}) copy-start(f32[2,2,45,256]{3,2,1,0:T(8,128)} %get-tuple-element.35) | copy-start | bytes 552964
  109.8 4.2 %collective-permute-start.14 = (bf16[1152,256]{1,0:T(8,128)(2,1)}, bf16[1152,256]{1,0:T(8,128)(2,1)}, u32[]{:S(2)}, u32[]{:S(2)}) collective-permute-start(bf16[1152,256]{1,0:T(8,128)(2,1)} %fusion.32), channel_id=1, source_target_pairs={{0,32},{32,0},{64,96},{96,64},{128,160},{160,128},{192,224},{224,1... | collective-permute-start | bytes 1769480 | tf_op jit(solution)/shard_map/ppermute | solution.py:62
  132.2 50.9 %copy-start.4 = (f32[2,2,45,256]{3,2,1,0:T(8,128)S(1)}, f32[2,2,45,256]{3,2,1,0:T(8,128)}, u32[]{:S(2)}) copy-start(f32[2,2,45,256]{3,2,1,0:T(8,128)} %copy-done.2) | copy-start | bytes 552964
  132.2 50.9 %copy-start.10 = (bf16[2,2,45,256]{3,2,1,0:T(8,128)(2,1)S(1)}, bf16[2,2,45,256]{3,2,1,0:T(8,128)(2,1)}, u32[]{:S(2)}) copy-start(bf16[2,2,45,256]{3,2,1,0:T(8,128)(2,1)} %copy-done.9) | copy-start | bytes 276484
  132.2 50.9 %copy-start.19 = (bf16[2,2,45,256]{3,2,1,0:T(8,128)(2,1)S(1)}, bf16[2,2,45,256]{3,2,1,0:T(8,128)(2,1)}, u32[]{:S(2)}) copy-start(bf16[2,2,45,256]{3,2,1,0:T(8,128)(2,1)} %copy-done.18) | copy-start | bytes 276484
  175.8 8.8 %collective-permute-start.15 = (bf16[1152,256]{1,0:T(8,128)(2,1)S(1)}, bf16[1152,256]{1,0:T(8,128)(2,1)S(1)}, u32[]{:S(2)}, u32[]{:S(2)}) collective-permute-start(bf16[1152,256]{1,0:T(8,128)(2,1)S(1)} %bitcast.150), channel_id=1, source_target_pairs={{0,32},{32,0},{64,96},{96,64},{128,160},{160,128},{192,224},{224,1... | collective-permute-start | bytes 1769480 | tf_op jit(solution)/shard_map/ppermute | solution.py:73

commit v2 on v1

v2 whole, which is shorter than its diff:
```python
import functools

import jax
import jax.numpy as jnp
from jax import lax
from jax.experimental import pallas as pl
from jax.experimental.pallas import tpu as pltpu
from jax.sharding import PartitionSpec as P

EDGE = 24
LANES = 128
SPAN = 96
CURVE = 0.7978845608028654
CUBIC = 0.044715


def routed(block, axis, distance, closed):
    count = lax.axis_size(axis)
    if closed:
        route = [(i, (i + distance) % count) for i in range(count)]
    else:
        route = [(i, i + distance) for i in range(count) if 0 <= i + distance < count]
    return lax.ppermute(block, axis, route)


def gelu_slope(x):
    squared = x * x
    bend = jnp.tanh(CURVE * (x + CUBIC * x * squared))
    inner = CURVE * (1.0 + 3.0 * CUBIC * squared)
    return 0.5 * (1.0 + bend) + 0.5 * x * (1.0 - bend * bend) * inner


def device_kernel(
    flags,
    taps,
    field,
    own_matrix,
    other_near,
    other_far,
    section,
    keep,
    give,
    table,
    matrices,
    basis0,
    basis1,
    middle,
    preact0,
    units1,
    spread,
    chosen_basis,
    chosen_units,
    grads,
):
    f32, bf16 = jnp.float32, jnp.bfloat16
    kernels = 9
    rows, chans = own_matrix.shape
    half = rows // 2
    reach = 8
    segment, core = flags[0], flags[1]
    window = kernels * SPAN
    lond = section.shape[2]
    near_start = pl.multiple_of(core * half, half)
    far_start = pl.multiple_of((1 - core) * half, half)

    def build(i, carry):
        for a in range(3):
            lanes = slice(a * LANES, (a + 1) * LANES)
            row = jnp.broadcast_to(taps[i, :, lanes], (SPAN, LANES))
            table[i, :, lanes] = pltpu.roll(
                row, LANES - reach, 1, stride=1, stride_axis=0
            ).astype(bf16)
        return carry

    lax.fori_loop(0, 6 * kernels, build, 0)

    matrices[segment] = own_matrix[...]
    matrices[1 - segment, pl.ds(near_start, half)] = other_near[...]
    matrices[1 - segment, pl.ds(far_start, half)] = other_far[...]

    def convolve(i, lines, skip, source, basis):
        m, r = lax.div(i, lines), lax.rem(i, lines)
        slab = source[m, pl.ds(r, 3)].reshape(3 * LANES, chans)
        rows_of = table[pl.ds((r + skip) * kernels, kernels)].reshape(window, 3 * LANES)
        out = jnp.dot(rows_of, slab, preferred_element_type=f32)
        start = pl.multiple_of(i * SPAN, SPAN)
        for k in range(kernels):
            basis[pl.ds(start, SPAN), k * chans : (k + 1) * chans] = out[
                k * SPAN : (k + 1) * SPAN
            ].astype(bf16)

    def first_basis(i, carry):
        convolve(i, 6, 0, field, basis0)
        return carry

    lax.fori_loop(0, 12, first_basis, 0)

    def first_mix(m, carry):
        start = pl.multiple_of(m * 6 * SPAN, 6 * SPAN)
        pre = jnp.dot(
            basis0[pl.ds(start, 6 * SPAN), :], matrices[0], preferred_element_type=f32
        )
        centre = field[m, 1:7, :SPAN].astype(f32).reshape(6 * SPAN, chans)
        out = centre + jax.nn.gelu(pre)
        middle[m, :, :SPAN] = out.astype(bf16).reshape(6, SPAN, chans)
        middle[m, :, SPAN:] = jnp.zeros((6, LANES - SPAN, chans), bf16)
        preact0[m] = pre[2 * SPAN : 4 * SPAN].reshape(2, SPAN, chans)
        return carry

    lax.fori_loop(0, 2, first_mix, 0)

    def second_basis(i, carry):
        convolve(i, 4, 1, middle, basis1)
        return carry

    lax.fori_loop(0, 8, second_basis, 0)

    def second_mix(m, carry):
        start = pl.multiple_of(m * 4 * SPAN, 4 * SPAN)
        pre = jnp.dot(
            basis1[pl.ds(start, 4 * SPAN), :], matrices[1], preferred_element_type=f32
        )
        incoming = field[m, 8:12, :SPAN].astype(f32).reshape(4 * SPAN, chans)
        units1[pl.ds(start, 4 * SPAN), :] = (incoming * gelu_slope(pre)).astype(bf16)
        for p in range(2):
            own = middle[m, p + 2, :SPAN].astype(f32)
            late = own + jax.nn.gelu(pre[(p + 1) * SPAN : (p + 2) * SPAN])
            picked = jnp.where(segment == 0, own, late)
            section[m, p] = picked[EDGE : EDGE + lond].astype(bf16)
        return carry

    lax.fori_loop(0, 2, second_mix, 0)

    column = lax.broadcasted_iota(jnp.int32, (SPAN, chans), 0)
    live = (column >= EDGE) & (column < EDGE + lond)

    @pl.when(segment == 0)
    def _():
        def unmix(k, carry):
            depth = pl.multiple_of(k * chans, chans)
            place = pl.multiple_of(k * SPAN, SPAN)
            mixed = lax.dot_general(
                units1[...],
                matrices[1, pl.ds(depth, chans), :],
                (((1,), (1,)), ((), ())),
                preferred_element_type=f32,
            ).astype(bf16)
            for m in range(2):
                for s in range(4):
                    begin = (m * 4 + s) * SPAN
                    spread[s, pl.ds(place, SPAN), m * chans : (m + 1) * chans] = mixed[
                        begin : begin + SPAN
                    ]
            return carry

        lax.fori_loop(0, kernels, unmix, 0)
        for p in range(2):
            back = jnp.zeros((LANES, 2 * chans), f32)
            for a in range(3):
                s = p + 2 - a
                rows_of = table[
                    (s + 1) * kernels : (s + 2) * kernels, :, a * LANES : (a + 1) * LANES
                ].reshape(window, LANES)
                back += lax.dot_general(
                    rows_of,
                    spread[s],
                    (((0,), (0,)), ((), ())),
                    preferred_element_type=f32,
                )
            for m in range(2):
                place = (m * 2 + p) * SPAN
                total = field[m, 9 + p, :SPAN].astype(f32) + back[
                    :SPAN, m * chans : (m + 1) * chans
                ]
                grad = total.astype(bf16).astype(f32)
                unit = grad * gelu_slope(preact0[m, p])
                chosen_units[place : place + SPAN, :] = jnp.where(live, unit, 0.0).astype(bf16)
                begin = (m * 6 + p + 2) * SPAN
                chosen_basis[place : place + SPAN, :] = basis0[begin : begin + SPAN, :]

    @pl.when(segment != 0)
    def _():
        for p in range(2):
            for m in range(2):
                place = (m * 2 + p) * SPAN
                begin = (m * 4 + p + 1) * SPAN
                unit = units1[begin : begin + SPAN, :].astype(f32)
                chosen_units[place : place + SPAN, :] = jnp.where(live, unit, 0.0).astype(bf16)
                chosen_basis[place : place + SPAN, :] = basis1[begin : begin + SPAN, :]

    for k in range(kernels):
        grads[k * chans : (k + 1) * chans, :] = lax.dot_general(
            chosen_basis[:, k * chans : (k + 1) * chans],
            chosen_units[...],
            (((0,), (0,)), ((), ())),
            preferred_element_type=f32,
        )
    keep[...] = grads[pl.ds(near_start, half), :]
    give[...] = grads[pl.ds(far_start, half), :].astype(bf16)


def on_device(flags, taps, field, own_matrix, other_near, other_far, lond):
    rows, chans = own_matrix.shape
    half = rows // 2
    bf16, f32 = jnp.bfloat16, jnp.float32
    whole = pl.BlockSpec(memory_space=pltpu.VMEM)
    return pl.pallas_call(
        device_kernel,
        out_shape=(
            jax.ShapeDtypeStruct((2, 2, lond, chans), bf16),
            jax.ShapeDtypeStruct((half, chans), f32),
            jax.ShapeDtypeStruct((half, chans), bf16),
        ),
        in_specs=[pl.BlockSpec(memory_space=pltpu.SMEM)] + [whole] * 5,
        out_specs=(whole, whole, whole),
        scratch_shapes=[
            pltpu.VMEM((54, SPAN, 3 * LANES), bf16),
            pltpu.VMEM((2, rows, chans), bf16),
            pltpu.VMEM((12 * SPAN, rows), bf16),
            pltpu.VMEM((8 * SPAN, rows), bf16),
            pltpu.VMEM((2, 6, LANES, chans), bf16),
            pltpu.VMEM((2, 2, SPAN, chans), f32),
            pltpu.VMEM((8 * SPAN, chans), bf16),
            pltpu.VMEM((4, 9 * SPAN, 2 * chans), bf16),
            pltpu.VMEM((4 * SPAN, rows), bf16),
            pltpu.VMEM((4 * SPAN, chans), bf16),
            pltpu.VMEM((rows, chans), f32),
        ],
        compiler_params=pltpu.CompilerParams(vmem_limit_bytes=52 * 1024 * 1024),
        name="sphere",
    )(flags, taps, field, own_matrix, other_near, other_far)


def gathered_sum(keep, give):
    lats, lons = lax.axis_size("lat"), lax.axis_size("lon")
    half, chans = keep.shape
    depth = 16
    planes = lons // depth
    columns = lats // 2 * planes
    swap = [(i, i ^ 1) for i in range(lats)]
    near = [
        [(2 * y + core) * lons + x * depth + z for y in range(lats // 2) for x in range(planes)]
        for core in range(2)
        for z in range(depth)
    ]
    far = [[x * depth + z for z in range(depth)] for x in range(planes)]
    core = lax.axis_index("lat") % 2
    own = (keep + lax.ppermute(give, "lat", swap).astype(jnp.float32)).astype(jnp.bfloat16)
    own = own.reshape(columns, half // columns, chans)
    own = lax.all_to_all(own, ("lat", "lon"), 0, 0, axis_index_groups=near)
    own = jnp.sum(own.astype(jnp.float32), axis=0).astype(jnp.bfloat16)
    own = own.reshape(depth, half // columns // depth, chans)
    own = lax.all_to_all(own, "lon", 0, 0, axis_index_groups=far)
    own = jnp.sum(own.astype(jnp.float32), axis=0).astype(jnp.bfloat16)
    own = jnp.broadcast_to(own[None], (depth,) + own.shape)
    own = lax.all_to_all(own, "lon", 0, 0, axis_index_groups=far).reshape(-1, chans)
    own = jnp.broadcast_to(own[None], (columns,) + own.shape)
    own = lax.all_to_all(own, ("lat", "lon"), 0, 0, axis_index_groups=near).reshape(-1, chans)
    other = lax.ppermute(own, "lat", swap)
    first = jnp.where(core == 0, own, other)
    second = jnp.where(core == 0, other, own)
    return jnp.concatenate([first, second], axis=0).astype(jnp.float32)


def tap_rows(psi, band_half, lat_start):
    kernels, lines, offsets, width = psi.shape
    taps = lax.broadcasted_iota(jnp.int32, psi.shape, 3)
    live = jnp.abs(taps - (width - 1) // 2) <= band_half[None, :, :, None]
    effective = jnp.where(live, psi, jnp.zeros_like(psi)).astype(jnp.float32)
    by_row = jnp.transpose(effective, (1, 0, 2, 3))
    by_row = jnp.pad(by_row, ((2, 2), (0, 0), (0, 0), (0, LANES - width)))
    own = lax.dynamic_slice_in_dim(by_row, lat_start, 6, 0)
    return own.reshape(6 * kernels, 1, offsets * LANES)


def widened(inputs, cotangent):
    lond = inputs.shape[2]
    both = jnp.concatenate([inputs, cotangent[:, 1:]], axis=1)
    down = routed(both, "lat", 1, False)
    both = jnp.concatenate([inputs, cotangent[:, :1]], axis=1)
    up = routed(both, "lat", -1, False)
    down_far = routed(inputs[:, 1:], "lat", 2, False)
    up_far = routed(inputs[:, :1], "lat", -2, False)
    lines = jnp.concatenate(
        [
            down_far,
            down[:, :2],
            inputs,
            up[:, :2],
            up_far,
            down[:, 2:],
            cotangent,
            up[:, 2:],
        ],
        axis=1,
    )
    left = routed(lines[:, :, lond - EDGE :], "lon", 1, True)
    right = routed(lines[:, :, :EDGE], "lon", -1, True)
    blank = jnp.zeros(lines.shape[:2] + (LANES - lond - 2 * EDGE, lines.shape[3]), lines.dtype)
    return jnp.concatenate([left, lines, right, blank], axis=2)


def shards(inputs, cotangent, weights, psi, band_half):
    lat = lax.axis_index("lat")
    core = lat % 2
    segment = lax.axis_index("segment")
    matrix = weights[0]
    half = matrix.shape[0] // 2
    mine = lax.dynamic_slice_in_dim(matrix, core * half, half, 0)
    other_near = lax.ppermute(mine, "segment", [(0, 1), (1, 0)])
    field = widened(inputs, cotangent)
    other_far = lax.ppermute(
        other_near, "lat", [(i, i ^ 1) for i in range(lax.axis_size("lat"))]
    )
    taps = tap_rows(psi, band_half, lat * inputs.shape[1])
    flags = jnp.stack([segment, core]).astype(jnp.int32)
    section, keep, give = on_device(
        flags, taps, field, matrix, other_near, other_far, inputs.shape[2]
    )
    return (section[None], gathered_sum(keep, give)[None])


def solution(mesh):
    placed = (
        P(None, "lat", "lon", None),
        P(None, "lat", "lon", None),
        P("segment", None, None),
        P(),
        P(),
    )
    return jax.shard_map(
        shards,
        mesh=mesh,
        in_specs=placed,
        out_specs=(P("segment", None, "lat", "lon", None), P("segment", None, None)),
        check_vma=False,
    )
```

time: 187 us -> 151 us (0.81)
  Pallas kernels: 0 us -> 24.1 us
  local copies, waits for them, and re-layouts: 20.8 us -> 3.48 us
  starting transfers between devices: 58.8 us -> 42.7 us
  matrix products: 11.9 us -> 0 us
  waiting for transfers between devices: 23.2 us -> 13.1 us
  other arithmetic: 9.97 us -> 5.32 us
    pallas_call x0 -> x1, Pallas kernels: none -> 24.1 us  [on_device(): pl.pallas_call(device_kernel, out_shape=(jax.ShapeDtypeStruct((2, 2, lond...]
    ppermute x16 -> x10, starting transfers between devices: 58.8 us -> 42.7 us  [the longest x6 28.3 us: routed(): return lax.ppermute(block, axis, route)]
    dot_general x11 -> x0, matrix products: 11.9 us -> none  [the longest x1 2.95 us: shards(): jnp.einsum('kiaoj,miajkc->iomc', adjoint.astype(jnp.float32), jnp.stack([...]
    ppermute x16 -> x10, waiting for transfers between devices: 23.2 us -> 13.1 us  [the longest x1 10.2 us: shards(): other_near = lax.ppermute(mine, 'segment', [(0, 1), (1, 0)])]
    concatenate x4 -> x2, local copies, waits for them, and re-layouts: 5.09 us -> 0.08 us  [the longest x1 0.08 us: widened(): return jnp.concatenate([left, lines, right, blank], axis=2)]
    unnamed x51 -> x21, local copies, waits for them, and re-layouts: 6.03 us -> 1.83 us
    reshape x6 -> x2, local copies, waits for them, and re-layouts: 3.72 us -> 0.14 us  [the longest x1 0.1 us: tap_rows(): return own.reshape(6 * kernels, 1, offsets * LANES)]
    another operation x1, other arithmetic: 2.28 us -> 0.07 us  [shards(): flags = jnp.stack([segment, core]).astype(jnp.int32)]
  transfers between devices with their start and end apart: 16 -> 10, of which waited for: 9 -> 3; matrix products, arithmetic and copies ran while one was open for 9% -> 3% of each run, Pallas kernels for 0% -> 0%
where the time goes in v2:
time: 151 us
  blocking collectives  60.9 us (40%)
  starting transfers between devices  42.7 us (28%)
  Pallas kernels  24.1 us (16%)
  waiting for transfers between devices  13.1 us (9%)
  other arithmetic  5.32 us (4%)
  local copies, waits for them, and re-layouts  3.48 us (2%)
    ppermute x6, starting transfers between devices, routed(): return lax.ppermute(block, axis, route)  28.3 us
    pallas_call x1, Pallas kernels, on_device(): pl.pallas_call(device_kernel, out_shape=(jax.ShapeDtypeStruct((2, 2, lond...  24.1 us
    all_to_all x1, blocking collectives, gathered_sum(): own = lax.all_to_all(own, 'lon', 0, 0, axis_index_groups=far)  19.7 us
    all_to_all x1, blocking collectives, gathered_sum(): lax.all_to_all(own, 'lon', 0, 0, axis_index_groups=far).reshape(-1, chans)  17.1 us
    all_to_all x1, blocking collectives, gathered_sum(): own = lax.all_to_all(own, ('lat', 'lon'), 0, 0, axis_index_groups=near)  13.2 us
    all_to_all x1, blocking collectives, gathered_sum(): lax.all_to_all(own, ('lat', 'lon'), 0, 0, axis_index_groups=near)  10.9 us
    ppermute x1, waiting for transfers between devices, shards(): other_near = lax.ppermute(mine, 'segment', [(0, 1), (1, 0)])  10.2 us
    ppermute x1, starting transfers between devices, gathered_sum(): other = lax.ppermute(own, 'lat', swap)  7.28 us
  transfers between devices with their start and end apart: 10, of which 3 were waited for; matrix products, arithmetic and copies ran while one was open for 3% of the time, Pallas kernels for 0%

profile of v2, /device:TPU:1, one launch (start us, length us, event | category | flops | bytes accessed | tf_op | source)
XLA Modules:
  0.0 150.5 jit_solution(4793928399791448457)
XLA Ops:
  0.6 0.0 copy-start.2
  0.6 0.0 copy-start
  0.7 1.0 copy.18
  1.7 1.3 collective-permute-start.3
  3.0 0.0 copy-start.1
  3.0 4.8 %collective-permute-start = (bf16[2,1,45,256]{3,2,1,0:T(8,128)(2,1)S(1)}, bf16[2,1,45,256]{3,2,1,0:T(8,128)(2,1)S(1)}, u32[]{:S(2)}, u32[]{:S(2)}) collective-permute-start(bf16[2,1,45,256]{3,2,1,0:T(8,128)(2,1)S(1)} %get-tuple-element.17), channel_id=1, source_target_pairs={{0,64},{32,96},{64,128},{96,160},{128,192},{160,224},{1,65},{33,97... | collective-permute-start | bytes 138248 | tf_op jit(solution)/shard_map/ppermute | solution.py:23
  7.8 1.1 fusion.4
  9.0 8.7 %collective-permute-start.2 = (bf16[2,3,45,256]{3,2,1,0:T(8,128)(2,1)S(1)}, bf16[2,3,45,256]{3,2,1,0:T(8,128)(2,1)S(1)}, u32[]{:S(2)}, u32[]{:S(2)}) collective-permute-start(bf16[2,3,45,256]{3,2,1,0:T(8,128)(2,1)S(1)} %get-tuple-element.18), channel_id=1, source_target_pairs={{32,0},{64,32},{96,64},{128,96},{160,128},{192,160},{224,192},{33,... | collective-permute-start | bytes 414728 | tf_op jit(solution)/shard_map/ppermute | solution.py:23
  17.7 1.9 %collective-permute-start.1 = (bf16[2,3,45,256]{3,2,1,0:T(8,128)(2,1)S(1)}, bf16[2,3,45,256]{3,2,1,0:T(8,128)(2,1)S(1)}, u32[]{:S(2)}, u32[]{:S(2)}) collective-permute-start(bf16[2,3,45,256]{3,2,1,0:T(8,128)(2,1)S(1)} %get-tuple-element.19), channel_id=1, source_target_pairs={{0,32},{32,64},{64,96},{96,128},{128,160},{160,192},{192,224},{1,3... | collective-permute-start | bytes 414728 | tf_op jit(solution)/shard_map/ppermute | solution.py:23
  19.6 0.0 copy-done
  19.6 0.0 copy-start.3
  19.6 0.0 copy-start.4
  19.7 1.9 %collective-permute-start.6 = (bf16[1152,256]{1,0:T(8,128)(2,1)S(1)}, bf16[1152,256]{1,0:T(8,128)(2,1)S(1)}, u32[]{:S(2)}, u32[]{:S(2)}) collective-permute-start(bf16[1152,256]{1,0:T(8,128)(2,1)S(1)} %dynamic-slice_bitcast_fusion), channel_id=1, source_target_pairs={{0,256},{256,0},{1,257},{257,1},{2,258},{258,2},{3,259},{259,3},{4... | collective-permute-start | bytes 1769480 | tf_op jit(solution)/shard_map/ppermute | solution.py:310
  21.6 0.0 collective-permute-done
  21.7 0.0 collective-permute-done.1
  21.7 0.0 copy-done.2
  21.7 0.0 collective-permute-done.2
  21.8 0.0 collective-permute-done.3
  21.8 0.0 copy-done.1
  21.8 0.1 fusion.2
  22.0 2.1 %collective-permute-start.4 = (bf16[2,12,24,256]{3,2,1,0:T(8,128)(2,1)S(1)}, bf16[2,12,24,256]{3,2,1,0:T(8,128)(2,1)S(1)}, u32[]{:S(2)}, u32[]{:S(2)}) collective-permute-start(bf16[2,12,24,256]{3,2,1,0:T(8,128)(2,1)S(1)} %get-tuple-element.14), channel_id=1, source_target_pairs={{0,1},{1,2},{2,3},{3,4},{4,5},{5,6},{6,7},{7,8},{8,9},{9,10},{10,1... | collective-permute-start | bytes 884744 | tf_op jit(solution)/shard_map/ppermute | solution.py:23
  24.1 9.5 %collective-permute-start.5 = (bf16[2,12,24,256]{3,2,1,0:T(8,128)(2,1)S(1)}, bf16[2,12,24,256]{3,2,1,0:T(8,128)(2,1)S(1)}, u32[]{:S(2)}, u32[]{:S(2)}) collective-permute-start(bf16[2,12,24,256]{3,2,1,0:T(8,128)(2,1)S(1)} %get-tuple-element.15), channel_id=1, source_target_pairs={{0,31},{1,0},{2,1},{3,2},{4,3},{5,4},{6,5},{7,6},{8,7},{9,8},{10,9... | collective-permute-start | bytes 884744 | tf_op jit(solution)/shard_map/ppermute | solution.py:23
  33.6 10.2 %collective-permute-done.6.other_near = bf16[1152,256]{1,0:T(8,128)(2,1)S(1)} collective-permute-done((bf16[1152,256]{1,0:T(8,128)(2,1)S(1)}, bf16[1152,256]{1,0:T(8,128)(2,1)S(1)}, u32[]{:S(2)}, u32[]{:S(2)}) %collective-permute-start.6) | collective-permute-done | bytes 589856 | tf_op jit(solution)/shard_map/ppermute | solution.py:310
  43.8 3.3 %collective-permute-start.7 = (bf16[1152,256]{1,0:T(8,128)(2,1)S(1)}, bf16[1152,256]{1,0:T(8,128)(2,1)S(1)}, u32[]{:S(2)}, u32[]{:S(2)}) collective-permute-start(bf16[1152,256]{1,0:T(8,128)(2,1)S(1)} %collective-permute-done.6.other_near), channel_id=1, source_target_pairs={{0,32},{32,0},{64,96},{96,64},{128,160},{160,128},{192,224},{224,1... | collective-permute-start | bytes 1769480 | tf_op jit(solution)/shard_map/ppermute | solution.py:312
  47.1 0.0 copy-done.3
  47.1 0.0 copy-done.4
  47.1 0.1 fusion
  47.3 0.1 reshape.49.taps
  47.4 0.1 pad.14.clone
  47.5 0.1 pad_add_fusion.flags
  47.6 0.0 collective-permute-done.4
  47.6 0.0 collective-permute-done.5
  47.6 1.8 %maximum_maximum_fusion.field = bf16[2,12,128,256]{3,2,1,0:T(8,128)(2,1)} fusion(bf16[2,12,24,256]{3,2,1,0:T(8,128)(2,1)S(1)} %collective-permute-done.5, bf16[2,12,45,256]{3,2,1,0:T(8,128)(2,1)S(1)} %slice_dynamic-update-slice_fusion.2, bf16[2,12,24,256]{3,2,1,0:T(8,128)(2,1)S(1)} %collective-permute-done.4, bf16[128]{0:T(256)(128)(2,1)S(1)} %pad.14.clone), kind=kLoop, calls=%fused_computation | loop fusion | flops 6291456 | bytes 2715904 | tf_op jit(solution)/shard_map/concatenate | solution.py:300
  49.4 0.0 collective-permute-done.7.other_far
  49.4 24.1 %sphere.1 = (bf16[2,2,45,256]{3,2,1,0:T(8,128)(2,1)S(1)}, f32[1152,256]{1,0:T(8,128)}, bf16[1152,256]{1,0:T(8,128)(2,1)S(1)}) custom-call(s32[2]{0:T(128)S(1)} %pad_add_fusion.flags, f32[54,1,384]{2,1,0:T(1,128)S(1)} %reshape.49.taps, bf16[2,12,128,256]{3,2,1,0:T(8,128)(2,1)} %maximum_maximum_fusion.field, bf16[2304,256]{1,0:T(8,128)(2,1)} %bitcast.17, ...), custom_call_target="tpu_custom_call" | custom-call | tf_op jit(solution)/shard_map/sphere/pallas_call | solution.py:207
  73.5 1.9 %collective-permute-start.8 = (bf16[1152,256]{1,0:T(8,128)(2,1)S(1)}, bf16[1152,256]{1,0:T(8,128)(2,1)S(1)}, u32[]{:S(2)}, u32[]{:S(2)}) collective-permute-start(bf16[1152,256]{1,0:T(8,128)(2,1)S(1)} %get-tuple-element.7), channel_id=1, source_target_pairs={{0,32},{32,0},{64,96},{96,64},{128,160},{160,128},{192,224},{224,1... | collective-permute-start | bytes 1769480 | tf_op jit(solution)/shard_map/ppermute | solution.py:248
  75.4 2.0 %collective-permute-done.8 = bf16[1152,256]{1,0:T(8,128)(2,1)S(1)} collective-permute-done((bf16[1152,256]{1,0:T(8,128)(2,1)S(1)}, bf16[1152,256]{1,0:T(8,128)(2,1)S(1)}, u32[]{:S(2)}, u32[]{:S(2)}) %collective-permute-start.8) | collective-permute-done | bytes 589856 | tf_op jit(solution)/shard_map/ppermute | solution.py:248
  77.3 1.4 add_convert_fusion
  78.8 13.2 %all_to_all.20 = bf16[8,144,256]{2,1,0:T(8,128)(2,1)S(1)} all-to-all(bf16[8,144,256]{2,1,0:T(8,128)(2,1)S(1)} %bitcast.19), channel_id=1, replica_groups={{0,16,64,80,128,144,192,208},{1,17,65,81,129,145,193,209},{2,18,66,82,1..., dimensions={0} | all-to-all | bytes 1179648 | tf_op jit(solution)/shard_map/all_to_all | solution.py:250
  92.0 0.1 reduce_sum.24
  92.1 19.7 %all_to_all.21 = bf16[16,9,256]{2,1,0:T(8,128)(2,1)S(1)} all-to-all(bf16[16,9,256]{2,1,0:T(8,128)(2,1)S(1)} %reshape.51), channel_id=1, replica_groups={{0,1,2,3,4,5,6,7,8,9,10,11,12,13,14,15},{16,17,18,19,20,21,22,23,24,25,..., dimensions={0} | all-to-all | bytes 147456 | tf_op jit(solution)/shard_map/all_to_all | solution.py:253
  111.8 17.1 %all_to_all.22 = bf16[16,9,256]{2,1,0:T(8,128)(2,1)S(1)} all-to-all(bf16[16,9,256]{2,1,0:T(8,128)(2,1)S(1)} %broadcast_in_dim.27), channel_id=1, replica_groups={{0,1,2,3,4,5,6,7,8,9,10,11,12,13,14,15},{16,17,18,19,20,21,22,23,24,25,..., dimensions={0} | all-to-all | bytes 147456 | tf_op jit(solution)/shard_map/all_to_all | solution.py:256
  129.0 10.9 %all_to_all.23 = bf16[8,144,256]{2,1,0:T(8,128)(2,1)S(1)} all-to-all(bf16[8,144,256]{2,1,0:T(8,128)(2,1)S(1)} %broadcast_in_dim.29), channel_id=1, replica_groups={{0,16,64,80,128,144,192,208},{1,17,65,81,129,145,193,209},{2,18,66,82,1..., dimensions={0} | all-to-all | bytes 1179648 | tf_op jit(solution)/shard_map/all_to_all | solution.py:258
  139.9 7.3 %collective-permute-start.9 = (bf16[1152,256]{1,0:T(8,128)(2,1)S(1)}, bf16[1152,256]{1,0:T(8,128)(2,1)S(1)}, u32[]{:S(2)}, u32[]{:S(2)}) collective-permute-start(bf16[1152,256]{1,0:T(8,128)(2,1)S(1)} %bitcast.18), channel_id=1, source_target_pairs={{0,32},{32,0},{64,96},{96,64},{128,160},{160,128},{192,224},{224,1... | collective-permute-start | bytes 1769480 | tf_op jit(solution)/shard_map/ppermute | solution.py:259
  147.2 0.7 copy.26
  147.9 0.9 collective-permute-done.9
  148.8 0.1 select_bitcast_fusion.1
  148.9 1.6 %maximum_convert_fusion = f32[1,2304,256]{2,1,0:T(8,128)} fusion(bf16[1,1152,256]{2,1,0:T(8,128)(2,1)S(1)} %get-tuple-element.13, bf16[1,1152,256]{2,1,0:T(8,128)(2,1)S(1)} %get-tuple-element.12), kind=kLoop, calls=%fused_computation.1 | loop fusion | flops 2359296 | bytes 3538944 | tf_op jit(solution)/shard_map/convert_element_type | solution.py:262
  (22 shorter events, 0.4 us)
Async XLA Ops:
  0.6 21.1 %copy-start.2 = (bf16[2,2,45,256]{3,1,2,0:T(2,128)(2,1)S(1)}, bf16[2,2,45,256]{3,1,2,0:T(2,128)(2,1)}, u32[]{:S(2)}) copy-start(bf16[2,2,45,256]{3,1,2,0:T(2,128)(2,1)} %param.5) | copy-start | bytes 276484
  0.6 19.0 %copy-start = (bf16[1,2304,256]{2,1,0:T(8,128)(2,1)S(1)}, bf16[1,2304,256]{2,1,0:T(8,128)(2,1)}, u32[]{:S(2)}) copy-start(bf16[1,2304,256]{2,1,0:T(8,128)(2,1)} %param.7) | copy-start | bytes 3538948
  1.7 20.1 %collective-permute-start.3 = (bf16[2,1,45,256]{3,2,1,0:T(8,128)(2,1)S(1)}, bf16[2,1,45,256]{3,2,1,0:T(8,128)(2,1)S(1)}, u32[]{:S(2)}, u32[]{:S(2)}) collective-permute-start(bf16[2,1,45,256]{3,2,1,0:T(8,128)(2,1)S(1)} %get-tuple-element.16), channel_id=1, source_target_pairs={{64,0},{96,32},{128,64},{160,96},{192,128},{224,160},{65,1},{97,33... | collective-permute-start | bytes 138248 | tf_op jit(solution)/shard_map/ppermute | solution.py:23
  3.0 18.8 %copy-start.1 = (bf16[2,2,45,256]{3,1,2,0:T(2,128)(2,1)S(1)}, bf16[2,2,45,256]{3,1,2,0:T(2,128)(2,1)}, u32[]{:S(2)}) copy-start(bf16[2,2,45,256]{3,1,2,0:T(2,128)(2,1)} %param.6) | copy-start | bytes 276484
  3.0 18.7 %collective-permute-start = (bf16[2,1,45,256]{3,2,1,0:T(8,128)(2,1)S(1)}, bf16[2,1,45,256]{3,2,1,0:T(8,128)(2,1)S(1)}, u32[]{:S(2)}, u32[]{:S(2)}) collective-permute-start(bf16[2,1,45,256]{3,2,1,0:T(8,128)(2,1)S(1)} %get-tuple-element.17), channel_id=1, source_target_pairs={{0,64},{32,96},{64,128},{96,160},{128,192},{160,224},{1,65},{33,97... | collective-permute-start | bytes 138248 | tf_op jit(solution)/shard_map/ppermute | solution.py:23
  9.0 12.7 %collective-permute-start.2 = (bf16[2,3,45,256]{3,2,1,0:T(8,128)(2,1)S(1)}, bf16[2,3,45,256]{3,2,1,0:T(8,128)(2,1)S(1)}, u32[]{:S(2)}, u32[]{:S(2)}) collective-permute-start(bf16[2,3,45,256]{3,2,1,0:T(8,128)(2,1)S(1)} %get-tuple-element.18), channel_id=1, source_target_pairs={{32,0},{64,32},{96,64},{128,96},{160,128},{192,160},{224,192},{33,... | collective-permute-start | bytes 414728 | tf_op jit(solution)/shard_map/ppermute | solution.py:23
  17.7 4.0 %collective-permute-start.1 = (bf16[2,3,45,256]{3,2,1,0:T(8,128)(2,1)S(1)}, bf16[2,3,45,256]{3,2,1,0:T(8,128)(2,1)S(1)}, u32[]{:S(2)}, u32[]{:S(2)}) collective-permute-start(bf16[2,3,45,256]{3,2,1,0:T(8,128)(2,1)S(1)} %get-tuple-element.19), channel_id=1, source_target_pairs={{0,32},{32,64},{64,96},{96,128},{128,160},{160,192},{192,224},{1,3... | collective-permute-start | bytes 414728 | tf_op jit(solution)/shard_map/ppermute | solution.py:23
  19.6 27.4 %copy-start.3 = (bf16[9,16,3,17]{3,1,2,0:T(8,128)(2,1)S(1)}, bf16[9,16,3,17]{3,1,2,0:T(8,128)(2,1)}, u32[]{:S(2)}) copy-start(bf16[9,16,3,17]{3,1,2,0:T(8,128)(2,1)} %param.8) | copy-start | bytes 44068
  19.6 27.4 %copy-start.4 = (s32[16,3]{0,1:T(4,128)S(1)}, s32[16,3]{0,1:T(4,128)}, u32[]{:S(2)}) copy-start(s32[16,3]{0,1:T(4,128)} %param.9) | copy-start | bytes 580
  19.7 24.1 %collective-permute-start.6 = (bf16[1152,256]{1,0:T(8,128)(2,1)S(1)}, bf16[1152,256]{1,0:T(8,128)(2,1)S(1)}, u32[]{:S(2)}, u32[]{:S(2)}) collective-permute-start(bf16[1152,256]{1,0:T(8,128)(2,1)S(1)} %dynamic-slice_bitcast_fusion), channel_id=1, source_target_pairs={{0,256},{256,0},{1,257},{257,1},{2,258},{258,2},{3,259},{259,3},{4... | collective-permute-start | bytes 1769480 | tf_op jit(solution)/shard_map/ppermute | solution.py:310
  22.0 25.6 %collective-permute-start.4 = (bf16[2,12,24,256]{3,2,1,0:T(8,128)(2,1)S(1)}, bf16[2,12,24,256]{3,2,1,0:T(8,128)(2,1)S(1)}, u32[]{:S(2)}, u32[]{:S(2)}) collective-permute-start(bf16[2,12,24,256]{3,2,1,0:T(8,128)(2,1)S(1)} %get-tuple-element.14), channel_id=1, source_target_pairs={{0,1},{1,2},{2,3},{3,4},{4,5},{5,6},{6,7},{7,8},{8,9},{9,10},{10,1... | collective-permute-start | bytes 884744 | tf_op jit(solution)/shard_map/ppermute | solution.py:23
  24.1 23.5 %collective-permute-start.5 = (bf16[2,12,24,256]{3,2,1,0:T(8,128)(2,1)S(1)}, bf16[2,12,24,256]{3,2,1,0:T(8,128)(2,1)S(1)}, u32[]{:S(2)}, u32[]{:S(2)}) collective-permute-start(bf16[2,12,24,256]{3,2,1,0:T(8,128)(2,1)S(1)} %get-tuple-element.15), channel_id=1, source_target_pairs={{0,31},{1,0},{2,1},{3,2},{4,3},{5,4},{6,5},{7,6},{8,7},{9,8},{10,9... | collective-permute-start | bytes 884744 | tf_op jit(solution)/shard_map/ppermute | solution.py:23
  43.8 5.6 %collective-permute-start.7 = (bf16[1152,256]{1,0:T(8,128)(2,1)S(1)}, bf16[1152,256]{1,0:T(8,128)(2,1)S(1)}, u32[]{:S(2)}, u32[]{:S(2)}) collective-permute-start(bf16[1152,256]{1,0:T(8,128)(2,1)S(1)} %collective-permute-done.6.other_near), channel_id=1, source_target_pairs={{0,32},{32,0},{64,96},{96,64},{128,160},{160,128},{192,224},{224,1... | collective-permute-start | bytes 1769480 | tf_op jit(solution)/shard_map/ppermute | solution.py:312
  73.5 3.9 %collective-permute-start.8 = (bf16[1152,256]{1,0:T(8,128)(2,1)S(1)}, bf16[1152,256]{1,0:T(8,128)(2,1)S(1)}, u32[]{:S(2)}, u32[]{:S(2)}) collective-permute-start(bf16[1152,256]{1,0:T(8,128)(2,1)S(1)} %get-tuple-element.7), channel_id=1, source_target_pairs={{0,32},{32,0},{64,96},{96,64},{128,160},{160,128},{192,224},{224,1... | collective-permute-start | bytes 1769480 | tf_op jit(solution)/shard_map/ppermute | solution.py:248
  139.9 8.9 %collective-permute-start.9 = (bf16[1152,256]{1,0:T(8,128)(2,1)S(1)}, bf16[1152,256]{1,0:T(8,128)(2,1)S(1)}, u32[]{:S(2)}, u32[]{:S(2)}) collective-permute-start(bf16[1152,256]{1,0:T(8,128)(2,1)S(1)} %bitcast.18), channel_id=1, source_target_pairs={{0,32},{32,0},{64,96},{96,64},{128,160},{160,128},{192,224},{224,1... | collective-permute-start | bytes 1769480 | tf_op jit(solution)/shard_map/ppermute | solution.py:259

commit v3 on v2

v3 whole, which is shorter than its diff:
```python
import functools

import jax
import jax.numpy as jnp
from jax import lax
from jax.experimental import pallas as pl
from jax.experimental.pallas import tpu as pltpu
from jax.sharding import PartitionSpec as P

EDGE = 24
WINDOW = 112
FIRST = 80
SECOND = 64
BLOCK = 48
REST = 32
SLAB = 64
WIDE = 256
DEEP = 640
CURVE = 0.7978845608028654
CUBIC = 0.044715


def routed(block, axis, distance, closed):
    count = lax.axis_size(axis)
    if closed:
        route = [(i, (i + distance) % count) for i in range(count)]
    else:
        route = [(i, i + distance) for i in range(count) if 0 <= i + distance < count]
    return lax.ppermute(block, axis, route)


def gelu_slope(x):
    squared = x * x
    bend = jnp.tanh(CURVE * (x + CUBIC * x * squared))
    inner = CURVE * (1.0 + 3.0 * CUBIC * squared)
    return 0.5 * (1.0 + bend) + 0.5 * x * (1.0 - bend * bend) * inner


def table_kernel(ahead, behind, table, adjoint):
    kernels = ahead.shape[1]
    bf16 = jnp.bfloat16

    def sloped(row, lines, start):
        return pltpu.roll(
            jnp.broadcast_to(row, (lines, 128)), start, 1, stride=1, stride_axis=0
        )

    def forward(r, carry):
        for k in range(kernels):
            for part in (slice(0, 128), slice(128, 256)):
                table[r * kernels + k, :, part] = sloped(
                    ahead[r, k : k + 1, part], BLOCK, 0
                ).astype(bf16)
        return carry

    lax.fori_loop(0, ahead.shape[0], forward, 0)
    low = lax.broadcasted_iota(jnp.int32, (FIRST, 128), 1) < SECOND

    def backward(i, carry):
        for pair in range(DEEP // 128):
            k = 2 * pair
            even = sloped(behind[i, k : k + 1, :], FIRST, SECOND)
            if k + 1 < kernels:
                odd = sloped(behind[i, k + 1 : k + 2, :], FIRST, 0)
            else:
                odd = jnp.zeros_like(even)
            adjoint[i, :, pair * 128 : (pair + 1) * 128] = jnp.where(low, even, odd).astype(bf16)
        return carry

    lax.fori_loop(0, behind.shape[0], backward, 0)


def band_tables(ahead, behind):
    whole = pl.BlockSpec(memory_space=pltpu.VMEM)
    lines, kernels = ahead.shape[:2]
    return pl.pallas_call(
        table_kernel,
        out_shape=(
            jax.ShapeDtypeStruct((lines * kernels, BLOCK, WIDE), jnp.bfloat16),
            jax.ShapeDtypeStruct((behind.shape[0], FIRST, DEEP), jnp.bfloat16),
        ),
        in_specs=[whole] * 2,
        out_specs=(whole, whole),
        compiler_params=pltpu.CompilerParams(vmem_limit_bytes=16 * 1024 * 1024),
        name="tables",
    )(ahead, behind)


def device_kernel(
    flags,
    table,
    adjoint,
    field,
    own_matrix,
    other_near,
    other_far,
    section,
    keep,
    give,
    matrices,
    turned,
    basis0,
    basis1,
    middle,
    preact0,
    units1,
    spread,
    chosen_basis,
    chosen_units,
    grads,
):
    f32, bf16 = jnp.float32, jnp.bfloat16
    rows, chans = own_matrix.shape
    kernels = rows // chans
    half = rows // 2
    segment, core = flags[0], flags[1]
    lond = section.shape[2]
    near_start = pl.multiple_of(core * half, half)
    far_start = pl.multiple_of((1 - core) * half, half)

    def convolve(m, r, line, source, basis, start, pieces):
        for offset, count in pieces:
            blocks = [source[m, r + min(a, 2), offset : offset + SLAB] for a in range(4)]
            slab = jnp.concatenate(blocks, axis=0)
            rows_of = table[pl.ds(line * kernels, kernels), :count].reshape(kernels * count, WIDE)
            out = jnp.dot(rows_of, slab, preferred_element_type=f32)
            place = pl.multiple_of(start + offset, 16)
            for k in range(kernels):
                basis[pl.ds(place, count), k * chans : (k + 1) * chans] = out[
                    k * count : (k + 1) * count
                ].astype(bf16)

    def first_basis(r, carry):
        for m in range(2):
            convolve(m, r, r, field, basis0, (m * 6 + r) * FIRST, ((0, BLOCK), (BLOCK, REST)))
        return carry

    lax.fori_loop(0, 6, first_basis, 0, unroll=True)

    matrices[segment] = own_matrix[...]
    matrices[1 - segment, pl.ds(near_start, half)] = other_near[...]
    matrices[1 - segment, pl.ds(far_start, half)] = other_far[...]

    for k in range(kernels):
        span = slice(k * chans, (k + 1) * chans)
        turned[:, span] = jnp.transpose(matrices[1, span, :])

    def first_mix(m, carry):
        start = pl.multiple_of(m * 6 * FIRST, 16)
        pre = jnp.dot(
            basis0[pl.ds(start, 6 * FIRST), :], matrices[0], preferred_element_type=f32
        )
        centre = field[m, 1:7].astype(f32)[:, 8 : 8 + FIRST].reshape(6 * FIRST, chans)
        out = centre + jax.nn.gelu(pre)
        middle[m, :, :FIRST] = out.astype(bf16).reshape(6, FIRST, chans)
        middle[m, :, FIRST:] = jnp.zeros((6, 16, chans), bf16)
        for p in range(2):
            preact0[m, p] = pre[(p + 2) * FIRST + 16 : (p + 3) * FIRST]
        return carry

    lax.fori_loop(0, 2, first_mix, 0, unroll=True)

    def second_basis(s, carry):
        for m in range(2):
            start = (m * 4 + s) * SECOND
            convolve(m, s, s + 1, middle, basis1, start, ((0, REST), (REST, REST)))
        return carry

    lax.fori_loop(0, 4, second_basis, 0, unroll=True)

    def second_mix(m, carry):
        start = pl.multiple_of(m * 4 * SECOND, 4 * SECOND)
        pre = jnp.dot(
            basis1[pl.ds(start, 4 * SECOND), :], matrices[1], preferred_element_type=f32
        )
        incoming = field[m, 8:12, 16 : 16 + SECOND].astype(f32).reshape(4 * SECOND, chans)
        units1[pl.ds(start, 4 * SECOND), :] = (incoming * gelu_slope(pre)).astype(bf16)
        for p in range(2):
            own = middle[m, p + 2, 16 : 16 + SECOND].astype(f32)[:lond]
            begin = (p + 1) * SECOND + 8
            late = own + jax.nn.gelu(pre[begin : begin + lond])
            section[m, p] = jnp.where(segment == 0, own, late).astype(bf16)
        return carry

    lax.fori_loop(0, 2, second_mix, 0, unroll=True)

    column = lax.broadcasted_iota(jnp.int32, (SECOND, chans), 0)

    @pl.when(segment == 0)
    def _():
        live = column < lond
        spread[:, kernels * SECOND :, :] = jnp.zeros(
            (4, DEEP - kernels * SECOND, 2 * chans), bf16
        )
        for k in range(kernels):
            mixed = lax.dot_general(
                units1[...],
                turned[:, k * chans : (k + 1) * chans],
                (((1,), (0,)), ((), ())),
                preferred_element_type=f32,
            ).astype(bf16)
            for m in range(2):
                for s in range(4):
                    begin = (m * 4 + s) * SECOND
                    spread[
                        s, k * SECOND : (k + 1) * SECOND, m * chans : (m + 1) * chans
                    ] = mixed[begin : begin + SECOND]
        for p in range(2):
            back = jnp.zeros((FIRST, 2 * chans), f32)
            for a in range(3):
                s = p + 2 - a
                back += jnp.dot(adjoint[s * 3 + a], spread[s], preferred_element_type=f32)
            for m in range(2):
                place = (m * 2 + p) * SECOND
                total = field[m, 9 + p].astype(f32)[EDGE : EDGE + SECOND] + back[
                    16 : 16 + SECOND, m * chans : (m + 1) * chans
                ]
                grad = total.astype(bf16).astype(f32)
                unit = grad * gelu_slope(preact0[m, p])
                chosen_units[place : place + SECOND, :] = jnp.where(live, unit, 0.0).astype(bf16)
                begin = (m * 6 + p + 2) * FIRST + 16
                chosen_basis[place : place + SECOND, :] = basis0[begin : begin + SECOND, :]

    @pl.when(segment != 0)
    def _():
        live = (column >= 8) & (column < 8 + lond)
        for p in range(2):
            for m in range(2):
                place = (m * 2 + p) * SECOND
                begin = (m * 4 + p + 1) * SECOND
                unit = units1[begin : begin + SECOND, :].astype(f32)
                chosen_units[place : place + SECOND, :] = jnp.where(live, unit, 0.0).astype(bf16)
                chosen_basis[place : place + SECOND, :] = basis1[begin : begin + SECOND, :]

    for k in range(kernels):
        grads[k * chans : (k + 1) * chans, :] = lax.dot_general(
            chosen_basis[:, k * chans : (k + 1) * chans],
            chosen_units[...],
            (((0,), (0,)), ((), ())),
            preferred_element_type=f32,
        )
    keep[...] = grads[pl.ds(near_start, half), :]
    give[...] = grads[pl.ds(far_start, half), :].astype(bf16)


def on_device(flags, tables, field, own_matrix, other_near, other_far, lond):
    rows, chans = own_matrix.shape
    half = rows // 2
    bf16, f32 = jnp.bfloat16, jnp.float32
    whole = pl.BlockSpec(memory_space=pltpu.VMEM)
    return pl.pallas_call(
        device_kernel,
        out_shape=(
            jax.ShapeDtypeStruct((2, 2, lond, chans), bf16),
            jax.ShapeDtypeStruct((half, chans), f32),
            jax.ShapeDtypeStruct((half, chans), bf16),
        ),
        in_specs=[pl.BlockSpec(memory_space=pltpu.SMEM)] + [whole] * 6,
        out_specs=(whole, whole, whole),
        scratch_shapes=[
            pltpu.VMEM((2, rows, chans), bf16),
            pltpu.VMEM((chans, rows), bf16),
            pltpu.VMEM((12 * FIRST, rows), bf16),
            pltpu.VMEM((8 * SECOND, rows), bf16),
            pltpu.VMEM((2, 6, FIRST + 16, chans), bf16),
            pltpu.VMEM((2, 2, SECOND, chans), f32),
            pltpu.VMEM((8 * SECOND, chans), bf16),
            pltpu.VMEM((4, DEEP, 2 * chans), bf16),
            pltpu.VMEM((4 * SECOND, rows), bf16),
            pltpu.VMEM((4 * SECOND, chans), bf16),
            pltpu.VMEM((rows, chans), f32),
        ],
        compiler_params=pltpu.CompilerParams(vmem_limit_bytes=32 * 1024 * 1024),
        name="sphere",
    )(flags, *tables, field, own_matrix, other_near, other_far)


def gathered_sum(keep, give):
    lats, lons = lax.axis_size("lat"), lax.axis_size("lon")
    half, chans = keep.shape
    depth = 16
    planes = lons // depth
    columns = lats // 2 * planes
    swap = [(i, i ^ 1) for i in range(lats)]
    near = [
        [(2 * y + core) * lons + x * depth + z for y in range(lats // 2) for x in range(planes)]
        for core in range(2)
        for z in range(depth)
    ]
    far = [[x * depth + z for z in range(depth)] for x in range(planes)]
    core = lax.axis_index("lat") % 2
    own = (keep + lax.ppermute(give, "lat", swap).astype(jnp.float32)).astype(jnp.bfloat16)
    own = own.reshape(columns, half // columns, chans)
    own = lax.all_to_all(own, ("lat", "lon"), 0, 0, axis_index_groups=near)
    own = jnp.sum(own.astype(jnp.float32), axis=0).astype(jnp.bfloat16)
    own = own.reshape(depth, half // columns // depth, chans)
    own = lax.all_to_all(own, "lon", 0, 0, axis_index_groups=far)
    own = jnp.sum(own.astype(jnp.float32), axis=0).astype(jnp.bfloat16)
    own = jnp.broadcast_to(own[None], (depth,) + own.shape)
    own = lax.all_to_all(own, "lon", 0, 0, axis_index_groups=far).reshape(-1, chans)
    own = jnp.broadcast_to(own[None], (columns,) + own.shape)
    own = lax.all_to_all(own, ("lat", "lon"), 0, 0, axis_index_groups=near).reshape(-1, chans)
    other = lax.ppermute(own, "lat", swap)
    first = jnp.where(core == 0, own, other)
    second = jnp.where(core == 0, other, own)
    return jnp.concatenate([first, second], axis=0).astype(jnp.float32)


def tap_rows(psi, band_half, lat_start):
    kernels, lines, offsets, width = psi.shape
    taps = lax.broadcasted_iota(jnp.int32, psi.shape, 3)
    live = jnp.abs(taps - (width - 1) // 2) <= band_half[None, :, :, None]
    effective = jnp.where(live, psi, jnp.zeros_like(psi)).astype(jnp.float32)
    by_row = jnp.transpose(effective, (1, 0, 2, 3))
    by_row = jnp.pad(by_row, ((2, 2), (0, 0), (0, 0), (0, 0)))
    own = lax.dynamic_slice_in_dim(by_row, lat_start, 6, 0)
    ahead = jnp.pad(own, ((0, 0), (0, 0), (0, 1), (0, SLAB - width)))
    ahead = ahead.reshape(6, kernels, WIDE)
    behind = jnp.transpose(jnp.flip(own[1:5], 3), (0, 2, 1, 3))
    start = SECOND - width + 1
    behind = jnp.pad(behind, ((0, 0), (0, 0), (0, 0), (start, 128 - width - start)))
    return ahead, behind.reshape(4 * offsets, kernels, 128)


def across():
    lons = lax.axis_size("lon")
    depth = lons // 2
    return [
        (seg * lons + x * depth + z, (1 - seg) * lons + (1 - x) * depth + z)
        for seg in range(2)
        for x in range(2)
        for z in range(depth)
    ]


def widened(inputs, cotangent):
    lond = inputs.shape[2]
    both = jnp.concatenate([inputs, cotangent[:, 1:]], axis=1)
    down = routed(both, "lat", 1, False)
    both = jnp.concatenate([inputs, cotangent[:, :1]], axis=1)
    up = routed(both, "lat", -1, False)
    down_far = routed(inputs[:, 1:], "lat", 2, False)
    up_far = routed(inputs[:, :1], "lat", -2, False)
    lines = jnp.concatenate(
        [
            down_far,
            down[:, :2],
            inputs,
            up[:, :2],
            up_far,
            down[:, 2:],
            cotangent,
            up[:, 2:],
        ],
        axis=1,
    )
    left = routed(lines[:, :, lond - EDGE :], "lon", 1, True)
    right = routed(lines[:, :, :EDGE], "lon", -1, True)
    return lines, left, right


def joined(left, lines, right):
    lond = lines.shape[2]
    blank = jnp.zeros(lines.shape[:2] + (WINDOW - lond - 2 * EDGE, lines.shape[3]), lines.dtype)
    return jnp.concatenate([left, lines, right, blank], axis=2)


def shards(inputs, cotangent, weights, psi, band_half):
    lat = lax.axis_index("lat")
    core = lat % 2
    segment = lax.axis_index("segment")
    matrix = weights[0]
    half = matrix.shape[0] // 2
    mine = lax.dynamic_slice_in_dim(matrix, core * half, half, 0)
    other_near = lax.ppermute(mine, ("segment", "lon"), across())
    lines, left, right = widened(inputs, cotangent)
    tables = band_tables(*tap_rows(psi, band_half, lat * inputs.shape[1]))
    left, right, other_near, tables = lax.optimization_barrier((left, right, other_near, tables))
    other_far = lax.ppermute(
        other_near, "lat", [(i, i ^ 1) for i in range(lax.axis_size("lat"))]
    )
    field = joined(left, lines, right)
    flags = jnp.stack([segment, core]).astype(jnp.int32)
    section, keep, give = on_device(
        flags, tables, field, matrix, other_near, other_far, inputs.shape[2]
    )
    return (section[None], gathered_sum(keep, give)[None])


def solution(mesh):
    placed = (
        P(None, "lat", "lon", None),
        P(None, "lat", "lon", None),
        P("segment", None, None),
        P(),
        P(),
    )
    return jax.shard_map(
        shards,
        mesh=mesh,
        in_specs=placed,
        out_specs=(P("segment", None, "lat", "lon", None), P("segment", None, None)),
        check_vma=False,
    )
```

time: 151 us -> 132 us (0.87)
  Pallas kernels: 24.1 us -> 9.87 us
  waiting for transfers between devices: 13.1 us -> 9.99 us
  local copies, waits for them, and re-layouts: 3.48 us -> 6.52 us
  blocking collectives: 60.9 us -> 58.7 us
    pallas_call x1, Pallas kernels: 24.1 us -> 7.65 us  [on_device(): pl.pallas_call(device_kernel, out_shape=(jax.ShapeDtypeStruct((2, 2, lond...]
    ppermute x1, waiting for transfers between devices: 10.2 us -> 0.01 us  [shards(): other_near = lax.ppermute(mine, ('segment', 'lon'), across())]
    ppermute x6, waiting for transfers between devices: 0.02 us -> 7.19 us  [routed(): return lax.ppermute(block, axis, route)]
    all_to_all x1, blocking collectives: 19.7 us -> 15.7 us  [gathered_sum(): own = lax.all_to_all(own, 'lon', 0, 0, axis_index_groups=far)]
    pallas_call x0 -> x1, Pallas kernels: none -> 2.22 us  [band_tables(): pl.pallas_call(table_kernel, out_shape=(jax.ShapeDtypeStruct((lines * ker...]
    all_to_all x1, blocking collectives: 13.2 us -> 15 us  [gathered_sum(): own = lax.all_to_all(own, ('lat', 'lon'), 0, 0, axis_index_groups=near)]
  transfers between devices with their start and end apart: 10 -> 10, of which waited for: 3 -> 4; matrix products, arithmetic and copies ran while one was open for 3% -> 5% of each run, Pallas kernels for 0% -> 2%
where the time goes in v3:
time: 132 us
  blocking collectives  58.7 us (44%)
  starting transfers between devices  41.6 us (32%)
  waiting for transfers between devices  9.99 us (8%)
  Pallas kernels  9.87 us (7%)
  local copies, waits for them, and re-layouts  6.52 us (5%)
  other arithmetic  4.02 us (3%)
    ppermute x6, starting transfers between devices, routed(): return lax.ppermute(block, axis, route)  27.6 us
    all_to_all x1, blocking collectives, gathered_sum(): lax.all_to_all(own, 'lon', 0, 0, axis_index_groups=far).reshape(-1, chans)  17.1 us
    all_to_all x1, blocking collectives, gathered_sum(): own = lax.all_to_all(own, 'lon', 0, 0, axis_index_groups=far)  15.7 us
    all_to_all x1, blocking collectives, gathered_sum(): own = lax.all_to_all(own, ('lat', 'lon'), 0, 0, axis_index_groups=near)  15 us
    all_to_all x1, blocking collectives, gathered_sum(): lax.all_to_all(own, ('lat', 'lon'), 0, 0, axis_index_groups=near)  10.9 us
    pallas_call x1, Pallas kernels, on_device(): pl.pallas_call(device_kernel, out_shape=(jax.ShapeDtypeStruct((2, 2, lond...  7.65 us
    ppermute x1, starting transfers between devices, gathered_sum(): other = lax.ppermute(own, 'lat', swap)  7.28 us
    ppermute x6, waiting for transfers between devices, routed(): return lax.ppermute(block, axis, route)  7.19 us
  transfers between devices with their start and end apart: 10, of which 4 were waited for; matrix products, arithmetic and copies ran while one was open for 5% of the time, Pallas kernels for 2%

profile of v3, /device:TPU:1, one launch (start us, length us, event | category | flops | bytes accessed | tf_op | source)
XLA Modules:
  0.0 131.8 jit_solution(2468980682400809364)
XLA Ops:
  0.6 1.0 copy.18
  1.7 0.0 copy-start.5
  1.7 1.4 %collective-permute-start.3 = (bf16[2,1,45,256]{3,2,1,0:T(8,128)(2,1)S(1)}, bf16[2,1,45,256]{3,2,1,0:T(8,128)(2,1)S(1)}, u32[]{:S(2)}, u32[]{:S(2)}) collective-permute-start(bf16[2,1,45,256]{3,2,1,0:T(8,128)(2,1)S(1)} %get-tuple-element.30), channel_id=1, source_target_pairs={{64,0},{96,32},{128,64},{160,96},{192,128},{224,160},{65,1},{97,33... | collective-permute-start | bytes 138248 | tf_op jit(solution)/shard_map/ppermute | solution.py:29
  3.1 4.7 %collective-permute-start = (bf16[2,1,45,256]{3,2,1,0:T(8,128)(2,1)S(1)}, bf16[2,1,45,256]{3,2,1,0:T(8,128)(2,1)S(1)}, u32[]{:S(2)}, u32[]{:S(2)}) collective-permute-start(bf16[2,1,45,256]{3,2,1,0:T(8,128)(2,1)S(1)} %get-tuple-element.31), channel_id=1, source_target_pairs={{0,64},{32,96},{64,128},{96,160},{128,192},{160,224},{1,65},{33,97... | collective-permute-start | bytes 138248 | tf_op jit(solution)/shard_map/ppermute | solution.py:29
  7.8 1.1 fusion.4
  8.9 0.0 copy-start.4
  9.0 8.7 %collective-permute-start.2 = (bf16[2,3,45,256]{3,2,1,0:T(8,128)(2,1)S(1)}, bf16[2,3,45,256]{3,2,1,0:T(8,128)(2,1)S(1)}, u32[]{:S(2)}, u32[]{:S(2)}) collective-permute-start(bf16[2,3,45,256]{3,2,1,0:T(8,128)(2,1)S(1)} %get-tuple-element.32), channel_id=1, source_target_pairs={{32,0},{64,32},{96,64},{128,96},{160,128},{192,160},{224,192},{33,... | collective-permute-start | bytes 414728 | tf_op jit(solution)/shard_map/ppermute | solution.py:29
  17.7 1.9 %collective-permute-start.1 = (bf16[2,3,45,256]{3,2,1,0:T(8,128)(2,1)S(1)}, bf16[2,3,45,256]{3,2,1,0:T(8,128)(2,1)S(1)}, u32[]{:S(2)}, u32[]{:S(2)}) collective-permute-start(bf16[2,3,45,256]{3,2,1,0:T(8,128)(2,1)S(1)} %get-tuple-element.33), channel_id=1, source_target_pairs={{0,32},{32,64},{64,96},{96,128},{128,160},{160,192},{192,224},{1,3... | collective-permute-start | bytes 414728 | tf_op jit(solution)/shard_map/ppermute | solution.py:29
  19.6 0.9 dynamic-slice_bitcast_fusion
  20.5 2.0 %collective-permute-start.6 = (bf16[1152,256]{1,0:T(8,128)(2,1)}, bf16[1152,256]{1,0:T(8,128)(2,1)S(1)}, u32[]{:S(2)}, u32[]{:S(2)}) collective-permute-start(bf16[1152,256]{1,0:T(8,128)(2,1)} %dynamic-slice_bitcast_fusion), channel_id=1, source_target_pairs={{0,272},{1,273},{2,274},{3,275},{4,276},{5,277},{6,278},{7,279},{8... | collective-permute-start | bytes 1769480 | tf_op jit(solution)/shard_map/ppermute | solution.py:375
  22.6 0.0 collective-permute-done
  22.6 0.0 collective-permute-done.1
  22.6 0.0 collective-permute-done.2
  22.7 0.0 collective-permute-done.3
  22.8 0.0 copy-start.3
  22.8 1.0 fusion.2
  23.8 9.0 %collective-permute-start.5 = (bf16[2,12,24,256]{3,2,1,0:T(8,128)(2,1)}, bf16[2,12,24,256]{3,2,1,0:T(8,128)(2,1)S(1)}, u32[]{:S(2)}, u32[]{:S(2)}) collective-permute-start(bf16[2,12,24,256]{3,2,1,0:T(8,128)(2,1)} %get-tuple-element.28), channel_id=1, source_target_pairs={{0,31},{1,0},{2,1},{3,2},{4,3},{5,4},{6,5},{7,6},{8,7},{9,8},{10,9... | collective-permute-start | bytes 884744 | tf_op jit(solution)/shard_map/ppermute | solution.py:29
  32.8 1.9 %collective-permute-start.4 = (bf16[2,12,24,256]{3,2,1,0:T(8,128)(2,1)}, bf16[2,12,24,256]{3,2,1,0:T(8,128)(2,1)}, u32[]{:S(2)}, u32[]{:S(2)}) collective-permute-start(bf16[2,12,24,256]{3,2,1,0:T(8,128)(2,1)} %get-tuple-element.29), channel_id=1, source_target_pairs={{0,1},{1,2},{2,3},{3,4},{4,5},{5,6},{6,7},{7,8},{8,9},{9,10},{10,1... | collective-permute-start | bytes 884744 | tf_op jit(solution)/shard_map/ppermute | solution.py:29
  34.8 0.1 fusion
  35.0 0.1 reshape.57.ahead
  35.2 0.1 rev.4
  35.3 0.1 pad.18.clone
  35.4 2.2 %tables.1 = (bf16[54,48,256]{2,1,0:T(8,128)(2,1)S(1)}, bf16[12,80,640]{2,1,0:T(8,128)(2,1)S(1)}) custom-call(f32[6,9,256]{2,1,0:T(8,128)S(1)} %reshape.57.ahead, f32[12,9,128]{2,1,0:T(8,128)S(1)} %bitcast.19), custom_call_target="tpu_custom_call" | custom-call | tf_op jit(solution)/shard_map/tables/pallas_call | solution.py:76
  37.6 0.0 copy-start.1
  37.6 1.0 copy-done.1
  38.7 1.2 collective-permute-done.5
  39.9 5.9 %collective-permute-done.4 = bf16[2,12,24,256]{3,2,1,0:T(8,128)(2,1)} collective-permute-done((bf16[2,12,24,256]{3,2,1,0:T(8,128)(2,1)}, bf16[2,12,24,256]{3,2,1,0:T(8,128)(2,1)}, u32[]{:S(2)}, u32[]{:S(2)}) %collective-permute-start.4) | collective-permute-done | bytes 294944 | tf_op jit(solution)/shard_map/ppermute | solution.py:29
  45.8 0.0 collective-permute-done.6.other_near
  45.8 2.6 %collective-permute-start.7 = (bf16[1152,256]{1,0:T(8,128)(2,1)S(1)}, bf16[1152,256]{1,0:T(8,128)(2,1)}, u32[]{:S(2)}, u32[]{:S(2)}) collective-permute-start(bf16[1152,256]{1,0:T(8,128)(2,1)S(1)} %collective-permute-done.6.other_near), channel_id=1, source_target_pairs={{0,32},{32,0},{64,96},{96,64},{128,160},{160,128},{192,224},{224,1... | collective-permute-start | bytes 1769480 | tf_op jit(solution)/shard_map/ppermute | solution.py:379
  48.5 0.0 copy-start.2
  48.5 0.1 pad.24.clone
  48.6 0.1 pad_add_fusion.flags
  48.7 1.8 %maximum_maximum_fusion.field = bf16[2,12,112,256]{3,2,1,0:T(8,128)(2,1)S(1)} fusion(bf16[2,12,24,256]{3,2,1,0:T(8,128)(2,1)S(1)} %collective-permute-done.5, bf16[2,12,45,256]{3,2,1,0:T(8,128)(2,1)} %copy-done.3, bf16[2,12,24,256]{3,2,1,0:T(8,128)(2,1)} %collective-permute-done.4, bf16[112]{0:T(256)(128)(2,1)S(1)} %pad.24.clone), kind=kLoop, calls=%fused_computation | loop fusion | flops 5505024 | bytes 2519264 | tf_op jit(solution)/shard_map/concatenate | solution.py:365
  50.5 0.0 collective-permute-done.7.other_far
  50.5 7.6 %sphere.1 = (bf16[2,2,45,256]{3,2,1,0:T(8,128)(2,1)S(1)}, f32[1152,256]{1,0:T(8,128)S(1)}, bf16[1152,256]{1,0:T(8,128)(2,1)S(1)}) custom-call(s32[2]{0:T(128)S(1)} %pad_add_fusion.flags, bf16[54,48,256]{2,1,0:T(8,128)(2,1)S(1)} %get-tuple-element.14.table, bf16[12,80,640]{2,1,0:T(8,128)(2,1)S(1)} %copy-done.2, ...), custom_call_target="tpu_custom_call" | custom-call | tf_op jit(solution)/shard_map/sphere/pallas_call | solution.py:251
  58.2 2.0 %collective-permute-start.8 = (bf16[1152,256]{1,0:T(8,128)(2,1)S(1)}, bf16[1152,256]{1,0:T(8,128)(2,1)S(1)}, u32[]{:S(2)}, u32[]{:S(2)}) collective-permute-start(bf16[1152,256]{1,0:T(8,128)(2,1)S(1)} %get-tuple-element.21), channel_id=1, source_target_pairs={{0,32},{32,0},{64,96},{96,64},{128,160},{160,128},{192,224},{224,1... | collective-permute-start | bytes 1769480 | tf_op jit(solution)/shard_map/ppermute | solution.py:292
  60.2 1.9 %collective-permute-done.8 = bf16[1152,256]{1,0:T(8,128)(2,1)S(1)} collective-permute-done((bf16[1152,256]{1,0:T(8,128)(2,1)S(1)}, bf16[1152,256]{1,0:T(8,128)(2,1)S(1)}, u32[]{:S(2)}, u32[]{:S(2)}) %collective-permute-start.8) | collective-permute-done | bytes 589856 | tf_op jit(solution)/shard_map/ppermute | solution.py:292
  62.1 0.1 add_convert_fusion
  62.2 15.0 %all_to_all.20 = bf16[8,144,256]{2,1,0:T(8,128)(2,1)S(1)} all-to-all(bf16[8,144,256]{2,1,0:T(8,128)(2,1)S(1)} %bitcast.22), channel_id=1, replica_groups={{0,16,64,80,128,144,192,208},{1,17,65,81,129,145,193,209},{2,18,66,82,1..., dimensions={0} | all-to-all | bytes 1179648 | tf_op jit(solution)/shard_map/all_to_all | solution.py:294
  77.2 0.1 reduce_sum.24
  77.3 15.7 %all_to_all.21 = bf16[16,9,256]{2,1,0:T(8,128)(2,1)S(1)} all-to-all(bf16[16,9,256]{2,1,0:T(8,128)(2,1)S(1)} %reshape.55), channel_id=1, replica_groups={{0,1,2,3,4,5,6,7,8,9,10,11,12,13,14,15},{16,17,18,19,20,21,22,23,24,25,..., dimensions={0} | all-to-all | bytes 147456 | tf_op jit(solution)/shard_map/all_to_all | solution.py:297
  93.1 17.1 %all_to_all.22 = bf16[16,9,256]{2,1,0:T(8,128)(2,1)S(1)} all-to-all(bf16[16,9,256]{2,1,0:T(8,128)(2,1)S(1)} %broadcast_in_dim.27), channel_id=1, replica_groups={{0,1,2,3,4,5,6,7,8,9,10,11,12,13,14,15},{16,17,18,19,20,21,22,23,24,25,..., dimensions={0} | all-to-all | bytes 147456 | tf_op jit(solution)/shard_map/all_to_all | solution.py:300
  110.3 10.9 %all_to_all.23 = bf16[8,144,256]{2,1,0:T(8,128)(2,1)S(1)} all-to-all(bf16[8,144,256]{2,1,0:T(8,128)(2,1)S(1)} %broadcast_in_dim.29), channel_id=1, replica_groups={{0,16,64,80,128,144,192,208},{1,17,65,81,129,145,193,209},{2,18,66,82,1..., dimensions={0} | all-to-all | bytes 1179648 | tf_op jit(solution)/shard_map/all_to_all | solution.py:302
  121.2 7.3 %collective-permute-start.9 = (bf16[1152,256]{1,0:T(8,128)(2,1)S(1)}, bf16[1152,256]{1,0:T(8,128)(2,1)S(1)}, u32[]{:S(2)}, u32[]{:S(2)}) collective-permute-start(bf16[1152,256]{1,0:T(8,128)(2,1)S(1)} %bitcast.21), channel_id=1, source_target_pairs={{0,32},{32,0},{64,96},{96,64},{128,160},{160,128},{192,224},{224,1... | collective-permute-start | bytes 1769480 | tf_op jit(solution)/shard_map/ppermute | solution.py:303
  128.5 0.7 copy.29
  129.2 0.9 collective-permute-done.9
  130.1 0.1 select_bitcast_fusion.1
  130.2 1.6 %maximum_convert_fusion = f32[1,2304,256]{2,1,0:T(8,128)} fusion(bf16[1,1152,256]{2,1,0:T(8,128)(2,1)S(1)} %get-tuple-element.27, bf16[1,1152,256]{2,1,0:T(8,128)(2,1)S(1)} %get-tuple-element.26), kind=kLoop, calls=%fused_computation.1 | loop fusion | flops 2359296 | bytes 3538944 | tf_op jit(solution)/shard_map/convert_element_type | solution.py:306
  (34 shorter events, 0.5 us)
Async XLA Ops:
  0.6 19.0 %copy-start = (bf16[1,2304,256]{2,1,0:T(8,128)(2,1)S(1)}, bf16[1,2304,256]{2,1,0:T(8,128)(2,1)}, u32[]{:S(2)}) copy-start(bf16[1,2304,256]{2,1,0:T(8,128)(2,1)} %param.7) | copy-start | bytes 3538948
  1.7 21.0 %copy-start.5 = (bf16[2,2,45,256]{3,1,2,0:T(2,128)(2,1)S(1)}, bf16[2,2,45,256]{3,1,2,0:T(2,128)(2,1)}, u32[]{:S(2)}) copy-start(bf16[2,2,45,256]{3,1,2,0:T(2,128)(2,1)} %param.5) | copy-start | bytes 276484
  1.7 21.0 %collective-permute-start.3 = (bf16[2,1,45,256]{3,2,1,0:T(8,128)(2,1)S(1)}, bf16[2,1,45,256]{3,2,1,0:T(8,128)(2,1)S(1)}, u32[]{:S(2)}, u32[]{:S(2)}) collective-permute-start(bf16[2,1,45,256]{3,2,1,0:T(8,128)(2,1)S(1)} %get-tuple-element.30), channel_id=1, source_target_pairs={{64,0},{96,32},{128,64},{160,96},{192,128},{224,160},{65,1},{97,33... | collective-permute-start | bytes 138248 | tf_op jit(solution)/shard_map/ppermute | solution.py:29
  3.1 19.5 %collective-permute-start = (bf16[2,1,45,256]{3,2,1,0:T(8,128)(2,1)S(1)}, bf16[2,1,45,256]{3,2,1,0:T(8,128)(2,1)S(1)}, u32[]{:S(2)}, u32[]{:S(2)}) collective-permute-start(bf16[2,1,45,256]{3,2,1,0:T(8,128)(2,1)S(1)} %get-tuple-element.31), channel_id=1, source_target_pairs={{0,64},{32,96},{64,128},{96,160},{128,192},{160,224},{1,65},{33,97... | collective-permute-start | bytes 138248 | tf_op jit(solution)/shard_map/ppermute | solution.py:29
  8.9 13.8 %copy-start.4 = (bf16[2,2,45,256]{3,1,2,0:T(2,128)(2,1)S(1)}, bf16[2,2,45,256]{3,1,2,0:T(2,128)(2,1)}, u32[]{:S(2)}) copy-start(bf16[2,2,45,256]{3,1,2,0:T(2,128)(2,1)} %param.6) | copy-start | bytes 276484
  9.0 13.7 %collective-permute-start.2 = (bf16[2,3,45,256]{3,2,1,0:T(8,128)(2,1)S(1)}, bf16[2,3,45,256]{3,2,1,0:T(8,128)(2,1)S(1)}, u32[]{:S(2)}, u32[]{:S(2)}) collective-permute-start(bf16[2,3,45,256]{3,2,1,0:T(8,128)(2,1)S(1)} %get-tuple-element.32), channel_id=1, source_target_pairs={{32,0},{64,32},{96,64},{128,96},{160,128},{192,160},{224,192},{33,... | collective-permute-start | bytes 414728 | tf_op jit(solution)/shard_map/ppermute | solution.py:29
  17.7 4.9 %collective-permute-start.1 = (bf16[2,3,45,256]{3,2,1,0:T(8,128)(2,1)S(1)}, bf16[2,3,45,256]{3,2,1,0:T(8,128)(2,1)S(1)}, u32[]{:S(2)}, u32[]{:S(2)}) collective-permute-start(bf16[2,3,45,256]{3,2,1,0:T(8,128)(2,1)S(1)} %get-tuple-element.33), channel_id=1, source_target_pairs={{0,32},{32,64},{64,96},{96,128},{128,160},{160,192},{192,224},{1,3... | collective-permute-start | bytes 414728 | tf_op jit(solution)/shard_map/ppermute | solution.py:29
  20.5 14.3 %copy-start.6 = (bf16[9,16,3,17]{3,1,2,0:T(8,128)(2,1)S(1)}, bf16[9,16,3,17]{3,1,2,0:T(8,128)(2,1)}, u32[]{:S(2)}) copy-start(bf16[9,16,3,17]{3,1,2,0:T(8,128)(2,1)} %param.8) | copy-start | bytes 44068
  20.5 14.3 %copy-start.7 = (s32[16,3]{0,1:T(4,128)S(1)}, s32[16,3]{0,1:T(4,128)}, u32[]{:S(2)}) copy-start(s32[16,3]{0,1:T(4,128)} %param.9) | copy-start | bytes 580
  20.5 25.3 %collective-permute-start.6 = (bf16[1152,256]{1,0:T(8,128)(2,1)}, bf16[1152,256]{1,0:T(8,128)(2,1)S(1)}, u32[]{:S(2)}, u32[]{:S(2)}) collective-permute-start(bf16[1152,256]{1,0:T(8,128)(2,1)} %dynamic-slice_bitcast_fusion), channel_id=1, source_target_pairs={{0,272},{1,273},{2,274},{3,275},{4,276},{5,277},{6,278},{7,279},{8... | collective-permute-start | bytes 1769480 | tf_op jit(solution)/shard_map/ppermute | solution.py:375
  22.8 12.2 %copy-start.3 = (bf16[2,12,45,256]{3,2,1,0:T(8,128)(2,1)}, bf16[2,12,45,256]{3,2,1,0:T(8,128)(2,1)S(1)}, u32[]{:S(2)}) copy-start(bf16[2,12,45,256]{3,2,1,0:T(8,128)(2,1)S(1)} %slice_dynamic-update-slice_fusion.2) | copy-start | bytes 1658884
  23.8 16.1 %collective-permute-start.5 = (bf16[2,12,24,256]{3,2,1,0:T(8,128)(2,1)}, bf16[2,12,24,256]{3,2,1,0:T(8,128)(2,1)S(1)}, u32[]{:S(2)}, u32[]{:S(2)}) collective-permute-start(bf16[2,12,24,256]{3,2,1,0:T(8,128)(2,1)} %get-tuple-element.28), channel_id=1, source_target_pairs={{0,31},{1,0},{2,1},{3,2},{4,3},{5,4},{6,5},{7,6},{8,7},{9,8},{10,9... | collective-permute-start | bytes 884744 | tf_op jit(solution)/shard_map/ppermute | solution.py:29
  32.8 13.0 %collective-permute-start.4 = (bf16[2,12,24,256]{3,2,1,0:T(8,128)(2,1)}, bf16[2,12,24,256]{3,2,1,0:T(8,128)(2,1)}, u32[]{:S(2)}, u32[]{:S(2)}) collective-permute-start(bf16[2,12,24,256]{3,2,1,0:T(8,128)(2,1)} %get-tuple-element.29), channel_id=1, source_target_pairs={{0,1},{1,2},{2,3},{3,4},{4,5},{5,6},{6,7},{7,8},{8,9},{9,10},{10,1... | collective-permute-start | bytes 884744 | tf_op jit(solution)/shard_map/ppermute | solution.py:29
  37.6 1.0 copy-start.1
  45.8 4.7 %collective-permute-start.7 = (bf16[1152,256]{1,0:T(8,128)(2,1)S(1)}, bf16[1152,256]{1,0:T(8,128)(2,1)}, u32[]{:S(2)}, u32[]{:S(2)}) collective-permute-start(bf16[1152,256]{1,0:T(8,128)(2,1)S(1)} %collective-permute-done.6.other_near), channel_id=1, source_target_pairs={{0,32},{32,0},{64,96},{96,64},{128,160},{160,128},{192,224},{224,1... | collective-permute-start | bytes 1769480 | tf_op jit(solution)/shard_map/ppermute | solution.py:379
  48.5 2.0 %copy-start.2 = (bf16[12,80,640]{2,1,0:T(8,128)(2,1)S(1)}, bf16[12,80,640]{2,1,0:T(8,128)(2,1)}, u32[]{:S(2)}) copy-start(bf16[12,80,640]{2,1,0:T(8,128)(2,1)} %copy-done.1) | copy-start | bytes 3686404
  58.2 3.9 %collective-permute-start.8 = (bf16[1152,256]{1,0:T(8,128)(2,1)S(1)}, bf16[1152,256]{1,0:T(8,128)(2,1)S(1)}, u32[]{:S(2)}, u32[]{:S(2)}) collective-permute-start(bf16[1152,256]{1,0:T(8,128)(2,1)S(1)} %get-tuple-element.21), channel_id=1, source_target_pairs={{0,32},{32,0},{64,96},{96,64},{128,160},{160,128},{192,224},{224,1... | collective-permute-start | bytes 1769480 | tf_op jit(solution)/shard_map/ppermute | solution.py:292
  121.2 8.9 %collective-permute-start.9 = (bf16[1152,256]{1,0:T(8,128)(2,1)S(1)}, bf16[1152,256]{1,0:T(8,128)(2,1)S(1)}, u32[]{:S(2)}, u32[]{:S(2)}) collective-permute-start(bf16[1152,256]{1,0:T(8,128)(2,1)S(1)} %bitcast.21), channel_id=1, source_target_pairs={{0,32},{32,0},{64,96},{96,64},{128,160},{160,128},{192,224},{224,1... | collective-permute-start | bytes 1769480 | tf_op jit(solution)/shard_map/ppermute | solution.py:303

commit v4 on v3

--- a/solution.py
+++ b/solution.py
@@ -287,17 +287,28 @@
         for core in range(2)
         for z in range(depth)
     ]
-    far = [[x * depth + z for z in range(depth)] for x in range(planes)]
+    hop = 4
+    beside = [[b + i for i in range(hop)] for b in range(0, lons, hop)]
+    apart = [
+        [x * depth + b + i * hop for i in range(depth // hop)]
+        for x in range(planes)
+        for b in range(hop)
+    ]
     core = lax.axis_index("lat") % 2
     own = (keep + lax.ppermute(give, "lat", swap).astype(jnp.float32)).astype(jnp.bfloat16)
     own = own.reshape(columns, half // columns, chans)
     own = lax.all_to_all(own, ("lat", "lon"), 0, 0, axis_index_groups=near)
     own = jnp.sum(own.astype(jnp.float32), axis=0).astype(jnp.bfloat16)
-    own = own.reshape(depth, half // columns // depth, chans)
-    own = lax.all_to_all(own, "lon", 0, 0, axis_index_groups=far)
+    lines, lanes = half // columns // 2, chans // 2
+    own = own.reshape(2, lines, 2, lanes).transpose(0, 2, 1, 3).reshape(hop, lines, lanes)
+    own = lax.all_to_all(own, "lon", 0, 0, axis_index_groups=beside)
     own = jnp.sum(own.astype(jnp.float32), axis=0).astype(jnp.bfloat16)
-    own = jnp.broadcast_to(own[None], (depth,) + own.shape)
-    own = lax.all_to_all(own, "lon", 0, 0, axis_index_groups=far).reshape(-1, chans)
+    own = jnp.broadcast_to(own[None], (depth // hop,) + own.shape)
+    own = lax.all_to_all(own, "lon", 0, 0, axis_index_groups=apart)
+    own = jnp.sum(own.astype(jnp.float32), axis=0).astype(jnp.bfloat16)
+    own = jnp.broadcast_to(own[None], (hop,) + own.shape)
+    own = lax.all_to_all(own, "lon", 0, 0, axis_index_groups=beside)
+    own = own.reshape(2, 2, lines, lanes).transpose(0, 2, 1, 3).reshape(2 * lines, chans)
     own = jnp.broadcast_to(own[None], (columns,) + own.shape)
     own = lax.all_to_all(own, ("lat", "lon"), 0, 0, axis_index_groups=near).reshape(-1, chans)
     other = lax.ppermute(own, "lat", swap)

time: 132 us -> 130 us (0.985)
  blocking collectives: 58.7 us -> 54.9 us
  starting transfers between devices: 41.6 us -> 43 us
    all_to_all x2 -> x3, blocking collectives: 32.8 us -> 29.3 us  [the longest x1 15.3 us: gathered_sum(): own = lax.all_to_all(own, 'lon', 0, 0, axis_index_groups=apart)]
    ppermute x1, starting transfers between devices: 7.28 us -> 8.68 us  [gathered_sum(): other = lax.ppermute(own, 'lat', swap)]
    unnamed x29 -> x30, local copies, waits for them, and re-layouts: 2.89 us -> 2.91 us
where the time goes in v4:
time: 130 us; the launch traced here: 129 us
  blocking collectives  54.9 us (42%)
  starting transfers between devices  43 us (33%)
  waiting for transfers between devices  10 us (8%)
  Pallas kernels  9.89 us (8%)
  local copies, waits for them, and re-layouts  6.54 us (5%)
  other arithmetic  4.01 us (3%)
    ppermute x6, starting transfers between devices, routed(): return lax.ppermute(block, axis, route)  27.6 us
    all_to_all x1, blocking collectives, gathered_sum(): own = lax.all_to_all(own, 'lon', 0, 0, axis_index_groups=apart)  15.3 us
    all_to_all x1, blocking collectives, gathered_sum(): own = lax.all_to_all(own, ('lat', 'lon'), 0, 0, axis_index_groups=near)  14.9 us
    all_to_all x2, blocking collectives, gathered_sum(): own = lax.all_to_all(own, 'lon', 0, 0, axis_index_groups=beside)  14 us
    all_to_all x1, blocking collectives, gathered_sum(): lax.all_to_all(own, ('lat', 'lon'), 0, 0, axis_index_groups=near)  10.7 us
    ppermute x1, starting transfers between devices, gathered_sum(): other = lax.ppermute(own, 'lat', swap)  8.68 us
    pallas_call x1, Pallas kernels, on_device(): pl.pallas_call(device_kernel, out_shape=(jax.ShapeDtypeStruct((2, 2, lond...  7.66 us
    ppermute x6, waiting for transfers between devices, routed(): return lax.ppermute(block, axis, route)  7.19 us
  transfers between devices with their start and end apart: 10, of which 4 were waited for; matrix products, arithmetic and copies ran while one was open for 5% of the time, Pallas kernels for 2%

profile of v4, /device:TPU:1, one launch (start us, length us, event | category | flops | bytes accessed | tf_op | source)
XLA Modules:
  0.0 129.5 jit_solution(12652827169134824876)
XLA Ops:
  0.6 1.0 copy.44
  1.7 0.0 copy-start.5
  1.7 1.4 %collective-permute-start.3 = (bf16[2,1,45,256]{3,2,1,0:T(8,128)(2,1)S(1)}, bf16[2,1,45,256]{3,2,1,0:T(8,128)(2,1)S(1)}, u32[]{:S(2)}, u32[]{:S(2)}) collective-permute-start(bf16[2,1,45,256]{3,2,1,0:T(8,128)(2,1)S(1)} %get-tuple-element.34), channel_id=1, source_target_pairs={{64,0},{96,32},{128,64},{160,96},{192,128},{224,160},{65,1},{97,33... | collective-permute-start | bytes 138248 | tf_op jit(solution)/shard_map/ppermute | solution.py:29
  3.1 4.7 %collective-permute-start = (bf16[2,1,45,256]{3,2,1,0:T(8,128)(2,1)S(1)}, bf16[2,1,45,256]{3,2,1,0:T(8,128)(2,1)S(1)}, u32[]{:S(2)}, u32[]{:S(2)}) collective-permute-start(bf16[2,1,45,256]{3,2,1,0:T(8,128)(2,1)S(1)} %get-tuple-element.35), channel_id=1, source_target_pairs={{0,64},{32,96},{64,128},{96,160},{128,192},{160,224},{1,65},{33,97... | collective-permute-start | bytes 138248 | tf_op jit(solution)/shard_map/ppermute | solution.py:29
  7.8 1.1 fusion.4
  8.9 0.0 copy-start.4
  9.0 8.7 %collective-permute-start.2 = (bf16[2,3,45,256]{3,2,1,0:T(8,128)(2,1)S(1)}, bf16[2,3,45,256]{3,2,1,0:T(8,128)(2,1)S(1)}, u32[]{:S(2)}, u32[]{:S(2)}) collective-permute-start(bf16[2,3,45,256]{3,2,1,0:T(8,128)(2,1)S(1)} %get-tuple-element.36), channel_id=1, source_target_pairs={{32,0},{64,32},{96,64},{128,96},{160,128},{192,160},{224,192},{33,... | collective-permute-start | bytes 414728 | tf_op jit(solution)/shard_map/ppermute | solution.py:29
  17.7 1.9 %collective-permute-start.1 = (bf16[2,3,45,256]{3,2,1,0:T(8,128)(2,1)S(1)}, bf16[2,3,45,256]{3,2,1,0:T(8,128)(2,1)S(1)}, u32[]{:S(2)}, u32[]{:S(2)}) collective-permute-start(bf16[2,3,45,256]{3,2,1,0:T(8,128)(2,1)S(1)} %get-tuple-element.37), channel_id=1, source_target_pairs={{0,32},{32,64},{64,96},{96,128},{128,160},{160,192},{192,224},{1,3... | collective-permute-start | bytes 414728 | tf_op jit(solution)/shard_map/ppermute | solution.py:29
  19.6 0.9 dynamic-slice_bitcast_fusion
  20.5 2.0 %collective-permute-start.6 = (bf16[1152,256]{1,0:T(8,128)(2,1)}, bf16[1152,256]{1,0:T(8,128)(2,1)S(1)}, u32[]{:S(2)}, u32[]{:S(2)}) collective-permute-start(bf16[1152,256]{1,0:T(8,128)(2,1)} %dynamic-slice_bitcast_fusion), channel_id=1, source_target_pairs={{0,272},{1,273},{2,274},{3,275},{4,276},{5,277},{6,278},{7,279},{8... | collective-permute-start | bytes 1769480 | tf_op jit(solution)/shard_map/ppermute | solution.py:386
  22.6 0.0 collective-permute-done
  22.6 0.0 collective-permute-done.1
  22.7 0.0 collective-permute-done.3
  22.8 1.0 fusion.2
  23.8 9.0 %collective-permute-start.5 = (bf16[2,12,24,256]{3,2,1,0:T(8,128)(2,1)}, bf16[2,12,24,256]{3,2,1,0:T(8,128)(2,1)S(1)}, u32[]{:S(2)}, u32[]{:S(2)}) collective-permute-start(bf16[2,12,24,256]{3,2,1,0:T(8,128)(2,1)} %get-tuple-element.32), channel_id=1, source_target_pairs={{0,31},{1,0},{2,1},{3,2},{4,3},{5,4},{6,5},{7,6},{8,7},{9,8},{10,9... | collective-permute-start | bytes 884744 | tf_op jit(solution)/shard_map/ppermute | solution.py:29
  32.8 1.9 %collective-permute-start.4 = (bf16[2,12,24,256]{3,2,1,0:T(8,128)(2,1)}, bf16[2,12,24,256]{3,2,1,0:T(8,128)(2,1)}, u32[]{:S(2)}, u32[]{:S(2)}) collective-permute-start(bf16[2,12,24,256]{3,2,1,0:T(8,128)(2,1)} %get-tuple-element.33), channel_id=1, source_target_pairs={{0,1},{1,2},{2,3},{3,4},{4,5},{5,6},{6,7},{7,8},{8,9},{9,10},{10,1... | collective-permute-start | bytes 884744 | tf_op jit(solution)/shard_map/ppermute | solution.py:29
  34.8 0.1 fusion
  35.0 0.1 reshape.66.ahead
  35.1 0.1 rev.4
  35.3 0.1 pad.18.clone
  35.4 2.2 %tables.1 = (bf16[54,48,256]{2,1,0:T(8,128)(2,1)S(1)}, bf16[12,80,640]{2,1,0:T(8,128)(2,1)S(1)}) custom-call(f32[6,9,256]{2,1,0:T(8,128)S(1)} %reshape.66.ahead, f32[12,9,128]{2,1,0:T(8,128)S(1)} %bitcast.29), custom_call_target="tpu_custom_call" | custom-call | tf_op jit(solution)/shard_map/tables/pallas_call | solution.py:76
  37.6 0.0 copy-start.1
  37.6 1.0 copy-done.1
  38.6 1.2 collective-permute-done.5
  39.9 5.9 %collective-permute-done.4 = bf16[2,12,24,256]{3,2,1,0:T(8,128)(2,1)} collective-permute-done((bf16[2,12,24,256]{3,2,1,0:T(8,128)(2,1)}, bf16[2,12,24,256]{3,2,1,0:T(8,128)(2,1)}, u32[]{:S(2)}, u32[]{:S(2)}) %collective-permute-start.4) | collective-permute-done | bytes 294944 | tf_op jit(solution)/shard_map/ppermute | solution.py:29
  45.8 0.0 collective-permute-done.6.other_near
  45.8 2.6 %collective-permute-start.7 = (bf16[1152,256]{1,0:T(8,128)(2,1)S(1)}, bf16[1152,256]{1,0:T(8,128)(2,1)}, u32[]{:S(2)}, u32[]{:S(2)}) collective-permute-start(bf16[1152,256]{1,0:T(8,128)(2,1)S(1)} %collective-permute-done.6.other_near), channel_id=1, source_target_pairs={{0,32},{32,0},{64,96},{96,64},{128,160},{160,128},{192,224},{224,1... | collective-permute-start | bytes 1769480 | tf_op jit(solution)/shard_map/ppermute | solution.py:390
  48.5 0.0 copy-start.2
  48.5 0.1 pad.24.clone
  48.6 0.1 pad_add_fusion.flags
  48.6 1.8 %maximum_maximum_fusion.field = bf16[2,12,112,256]{3,2,1,0:T(8,128)(2,1)S(1)} fusion(bf16[2,12,24,256]{3,2,1,0:T(8,128)(2,1)S(1)} %collective-permute-done.5, bf16[2,12,45,256]{3,2,1,0:T(8,128)(2,1)} %copy-done.3, bf16[2,12,24,256]{3,2,1,0:T(8,128)(2,1)} %collective-permute-done.4, bf16[112]{0:T(256)(128)(2,1)S(1)} %pad.24.clone), kind=kLoop, calls=%fused_computation | loop fusion | flops 5505024 | bytes 2519264 | tf_op jit(solution)/shard_map/concatenate | solution.py:376
  50.5 0.0 collective-permute-done.7.other_far
  50.5 7.7 %sphere.1 = (bf16[2,2,45,256]{3,2,1,0:T(8,128)(2,1)S(1)}, f32[1152,256]{1,0:T(8,128)S(1)}, bf16[1152,256]{1,0:T(8,128)(2,1)S(1)}) custom-call(s32[2]{0:T(128)S(1)} %pad_add_fusion.flags, bf16[54,48,256]{2,1,0:T(8,128)(2,1)S(1)} %get-tuple-element.14.table, bf16[12,80,640]{2,1,0:T(8,128)(2,1)S(1)} %copy-done.2, ...), custom_call_target="tpu_custom_call" | custom-call | tf_op jit(solution)/shard_map/sphere/pallas_call | solution.py:251
  58.2 2.0 %collective-permute-start.8 = (bf16[1152,256]{1,0:T(8,128)(2,1)S(1)}, bf16[1152,256]{1,0:T(8,128)(2,1)S(1)}, u32[]{:S(2)}, u32[]{:S(2)}) collective-permute-start(bf16[1152,256]{1,0:T(8,128)(2,1)S(1)} %get-tuple-element.21), channel_id=1, source_target_pairs={{0,32},{32,0},{64,96},{96,64},{128,160},{160,128},{192,224},{224,1... | collective-permute-start | bytes 1769480 | tf_op jit(solution)/shard_map/ppermute | solution.py:298
  60.2 1.9 %collective-permute-done.8 = bf16[1152,256]{1,0:T(8,128)(2,1)S(1)} collective-permute-done((bf16[1152,256]{1,0:T(8,128)(2,1)S(1)}, bf16[1152,256]{1,0:T(8,128)(2,1)S(1)}, u32[]{:S(2)}, u32[]{:S(2)}) %collective-permute-start.8) | collective-permute-done | bytes 589856 | tf_op jit(solution)/shard_map/ppermute | solution.py:298
  62.1 0.1 add_convert_fusion
  62.2 14.9 %all_to_all.25 = bf16[8,144,256]{2,1,0:T(8,128)(2,1)S(1)} all-to-all(bf16[8,144,256]{2,1,0:T(8,128)(2,1)S(1)} %bitcast.32), channel_id=1, replica_groups={{0,16,64,80,128,144,192,208},{1,17,65,81,129,145,193,209},{2,18,66,82,1..., dimensions={0} | all-to-all | bytes 1179648 | tf_op jit(solution)/shard_map/all_to_all | solution.py:300
  77.2 0.1 reduce_sum.36
  77.3 7.0 %all_to_all.26 = bf16[4,72,128]{2,1,0:T(8,128)(2,1)S(1)} all-to-all(bf16[4,72,128]{2,1,0:T(8,128)(2,1)S(1)} %bitcast.34), channel_id=1, replica_groups={{0,1,2,3},{4,5,6,7},{8,9,10,11},{12,13,14,15},{16,17,18,19},{20,21,22,2..., dimensions={0} | all-to-all | bytes 147456 | tf_op jit(solution)/shard_map/all_to_all | solution.py:304
  84.3 15.3 %all_to_all.27 = bf16[4,72,128]{2,1,0:T(8,128)(2,1)S(1)} all-to-all(bf16[4,72,128]{2,1,0:T(8,128)(2,1)S(1)} %broadcast_in_dim.33), channel_id=1, replica_groups={{0,4,8,12},{1,5,9,13},{2,6,10,14},{3,7,11,15},{16,20,24,28},{17,21,25,2..., dimensions={0} | all-to-all | bytes 147456 | tf_op jit(solution)/shard_map/all_to_all | solution.py:307
  99.7 7.0 %all_to_all.28 = bf16[4,72,128]{2,1,0:T(8,128)(2,1)S(1)} all-to-all(bf16[4,72,128]{2,1,0:T(8,128)(2,1)S(1)} %broadcast_in_dim.34), channel_id=1, replica_groups={{0,1,2,3},{4,5,6,7},{8,9,10,11},{12,13,14,15},{16,17,18,19},{20,21,22,2..., dimensions={0} | all-to-all | bytes 147456 | tf_op jit(solution)/shard_map/all_to_all | solution.py:310
  106.7 0.1 copy.56
  106.8 10.7 %all_to_all.29 = bf16[8,144,256]{2,1,0:T(8,128)(2,1)S(1)} all-to-all(bf16[8,144,256]{2,1,0:T(8,128)(2,1)S(1)} %broadcast_in_dim.36), channel_id=1, replica_groups={{0,16,64,80,128,144,192,208},{1,17,65,81,129,145,193,209},{2,18,66,82,1..., dimensions={0} | all-to-all | bytes 1179648 | tf_op jit(solution)/shard_map/all_to_all | solution.py:313
  117.5 8.7 %collective-permute-start.9 = (bf16[1152,256]{1,0:T(8,128)(2,1)S(1)}, bf16[1152,256]{1,0:T(8,128)(2,1)S(1)}, u32[]{:S(2)}, u32[]{:S(2)}) collective-permute-start(bf16[1152,256]{1,0:T(8,128)(2,1)S(1)} %bitcast.31), channel_id=1, source_target_pairs={{0,32},{32,0},{64,96},{96,64},{128,160},{160,128},{192,224},{224,1... | collective-permute-start | bytes 1769480 | tf_op jit(solution)/shard_map/ppermute | solution.py:314
  126.2 0.7 copy.57
  126.9 0.9 collective-permute-done.9
  127.8 0.1 select_bitcast_fusion.1
  127.9 1.6 %maximum_convert_fusion = f32[1,2304,256]{2,1,0:T(8,128)} fusion(bf16[1,1152,256]{2,1,0:T(8,128)(2,1)S(1)} %get-tuple-element.31, bf16[1,1152,256]{2,1,0:T(8,128)(2,1)S(1)} %get-tuple-element.30), kind=kLoop, calls=%fused_computation.1 | loop fusion | flops 2359296 | bytes 3538944 | tf_op jit(solution)/shard_map/convert_element_type | solution.py:317
  (39 shorter events, 0.4 us)
Async XLA Ops:
  0.6 19.0 %copy-start = (bf16[1,2304,256]{2,1,0:T(8,128)(2,1)S(1)}, bf16[1,2304,256]{2,1,0:T(8,128)(2,1)}, u32[]{:S(2)}) copy-start(bf16[1,2304,256]{2,1,0:T(8,128)(2,1)} %param.7) | copy-start | bytes 3538948
  1.7 21.0 %copy-start.5 = (bf16[2,2,45,256]{3,1,2,0:T(2,128)(2,1)S(1)}, bf16[2,2,45,256]{3,1,2,0:T(2,128)(2,1)}, u32[]{:S(2)}) copy-start(bf16[2,2,45,256]{3,1,2,0:T(2,128)(2,1)} %param.5) | copy-start | bytes 276484
  1.7 21.0 %collective-permute-start.3 = (bf16[2,1,45,256]{3,2,1,0:T(8,128)(2,1)S(1)}, bf16[2,1,45,256]{3,2,1,0:T(8,128)(2,1)S(1)}, u32[]{:S(2)}, u32[]{:S(2)}) collective-permute-start(bf16[2,1,45,256]{3,2,1,0:T(8,128)(2,1)S(1)} %get-tuple-element.34), channel_id=1, source_target_pairs={{64,0},{96,32},{128,64},{160,96},{192,128},{224,160},{65,1},{97,33... | collective-permute-start | bytes 138248 | tf_op jit(solution)/shard_map/ppermute | solution.py:29
  3.1 19.5 %collective-permute-start = (bf16[2,1,45,256]{3,2,1,0:T(8,128)(2,1)S(1)}, bf16[2,1,45,256]{3,2,1,0:T(8,128)(2,1)S(1)}, u32[]{:S(2)}, u32[]{:S(2)}) collective-permute-start(bf16[2,1,45,256]{3,2,1,0:T(8,128)(2,1)S(1)} %get-tuple-element.35), channel_id=1, source_target_pairs={{0,64},{32,96},{64,128},{96,160},{128,192},{160,224},{1,65},{33,97... | collective-permute-start | bytes 138248 | tf_op jit(solution)/shard_map/ppermute | solution.py:29
  8.9 13.8 %copy-start.4 = (bf16[2,2,45,256]{3,1,2,0:T(2,128)(2,1)S(1)}, bf16[2,2,45,256]{3,1,2,0:T(2,128)(2,1)}, u32[]{:S(2)}) copy-start(bf16[2,2,45,256]{3,1,2,0:T(2,128)(2,1)} %param.6) | copy-start | bytes 276484
  9.0 13.7 %collective-permute-start.2 = (bf16[2,3,45,256]{3,2,1,0:T(8,128)(2,1)S(1)}, bf16[2,3,45,256]{3,2,1,0:T(8,128)(2,1)S(1)}, u32[]{:S(2)}, u32[]{:S(2)}) collective-permute-start(bf16[2,3,45,256]{3,2,1,0:T(8,128)(2,1)S(1)} %get-tuple-element.36), channel_id=1, source_target_pairs={{32,0},{64,32},{96,64},{128,96},{160,128},{192,160},{224,192},{33,... | collective-permute-start | bytes 414728 | tf_op jit(solution)/shard_map/ppermute | solution.py:29
  17.7 4.9 %collective-permute-start.1 = (bf16[2,3,45,256]{3,2,1,0:T(8,128)(2,1)S(1)}, bf16[2,3,45,256]{3,2,1,0:T(8,128)(2,1)S(1)}, u32[]{:S(2)}, u32[]{:S(2)}) collective-permute-start(bf16[2,3,45,256]{3,2,1,0:T(8,128)(2,1)S(1)} %get-tuple-element.37), channel_id=1, source_target_pairs={{0,32},{32,64},{64,96},{96,128},{128,160},{160,192},{192,224},{1,3... | collective-permute-start | bytes 414728 | tf_op jit(solution)/shard_map/ppermute | solution.py:29
  20.5 14.2 %copy-start.6 = (bf16[9,16,3,17]{3,1,2,0:T(8,128)(2,1)S(1)}, bf16[9,16,3,17]{3,1,2,0:T(8,128)(2,1)}, u32[]{:S(2)}) copy-start(bf16[9,16,3,17]{3,1,2,0:T(8,128)(2,1)} %param.8) | copy-start | bytes 44068
  20.5 14.3 %copy-start.7 = (s32[16,3]{0,1:T(4,128)S(1)}, s32[16,3]{0,1:T(4,128)}, u32[]{:S(2)}) copy-start(s32[16,3]{0,1:T(4,128)} %param.9) | copy-start | bytes 580
  20.5 25.3 %collective-permute-start.6 = (bf16[1152,256]{1,0:T(8,128)(2,1)}, bf16[1152,256]{1,0:T(8,128)(2,1)S(1)}, u32[]{:S(2)}, u32[]{:S(2)}) collective-permute-start(bf16[1152,256]{1,0:T(8,128)(2,1)} %dynamic-slice_bitcast_fusion), channel_id=1, source_target_pairs={{0,272},{1,273},{2,274},{3,275},{4,276},{5,277},{6,278},{7,279},{8... | collective-permute-start | bytes 1769480 | tf_op jit(solution)/shard_map/ppermute | solution.py:386
  22.8 12.2 %copy-start.3 = (bf16[2,12,45,256]{3,2,1,0:T(8,128)(2,1)}, bf16[2,12,45,256]{3,2,1,0:T(8,128)(2,1)S(1)}, u32[]{:S(2)}) copy-start(bf16[2,12,45,256]{3,2,1,0:T(8,128)(2,1)S(1)} %slice_dynamic-update-slice_fusion.2) | copy-start | bytes 1658884
  23.8 16.1 %collective-permute-start.5 = (bf16[2,12,24,256]{3,2,1,0:T(8,128)(2,1)}, bf16[2,12,24,256]{3,2,1,0:T(8,128)(2,1)S(1)}, u32[]{:S(2)}, u32[]{:S(2)}) collective-permute-start(bf16[2,12,24,256]{3,2,1,0:T(8,128)(2,1)} %get-tuple-element.32), channel_id=1, source_target_pairs={{0,31},{1,0},{2,1},{3,2},{4,3},{5,4},{6,5},{7,6},{8,7},{9,8},{10,9... | collective-permute-start | bytes 884744 | tf_op jit(solution)/shard_map/ppermute | solution.py:29
  32.8 13.0 %collective-permute-start.4 = (bf16[2,12,24,256]{3,2,1,0:T(8,128)(2,1)}, bf16[2,12,24,256]{3,2,1,0:T(8,128)(2,1)}, u32[]{:S(2)}, u32[]{:S(2)}) collective-permute-start(bf16[2,12,24,256]{3,2,1,0:T(8,128)(2,1)} %get-tuple-element.33), channel_id=1, source_target_pairs={{0,1},{1,2},{2,3},{3,4},{4,5},{5,6},{6,7},{7,8},{8,9},{9,10},{10,1... | collective-permute-start | bytes 884744 | tf_op jit(solution)/shard_map/ppermute | solution.py:29
  37.6 1.0 copy-start.1
  45.8 4.7 %collective-permute-start.7 = (bf16[1152,256]{1,0:T(8,128)(2,1)S(1)}, bf16[1152,256]{1,0:T(8,128)(2,1)}, u32[]{:S(2)}, u32[]{:S(2)}) collective-permute-start(bf16[1152,256]{1,0:T(8,128)(2,1)S(1)} %collective-permute-done.6.other_near), channel_id=1, source_target_pairs={{0,32},{32,0},{64,96},{96,64},{128,160},{160,128},{192,224},{224,1... | collective-permute-start | bytes 1769480 | tf_op jit(solution)/shard_map/ppermute | solution.py:390
  48.5 2.0 %copy-start.2 = (bf16[12,80,640]{2,1,0:T(8,128)(2,1)S(1)}, bf16[12,80,640]{2,1,0:T(8,128)(2,1)}, u32[]{:S(2)}) copy-start(bf16[12,80,640]{2,1,0:T(8,128)(2,1)} %copy-done.1) | copy-start | bytes 3686404
  58.2 3.9 %collective-permute-start.8 = (bf16[1152,256]{1,0:T(8,128)(2,1)S(1)}, bf16[1152,256]{1,0:T(8,128)(2,1)S(1)}, u32[]{:S(2)}, u32[]{:S(2)}) collective-permute-start(bf16[1152,256]{1,0:T(8,128)(2,1)S(1)} %get-tuple-element.21), channel_id=1, source_target_pairs={{0,32},{32,0},{64,96},{96,64},{128,160},{160,128},{192,224},{224,1... | collective-permute-start | bytes 1769480 | tf_op jit(solution)/shard_map/ppermute | solution.py:298
  117.5 10.3 %collective-permute-start.9 = (bf16[1152,256]{1,0:T(8,128)(2,1)S(1)}, bf16[1152,256]{1,0:T(8,128)(2,1)S(1)}, u32[]{:S(2)}, u32[]{:S(2)}) collective-permute-start(bf16[1152,256]{1,0:T(8,128)(2,1)S(1)} %bitcast.31), channel_id=1, source_target_pairs={{0,32},{32,0},{64,96},{96,64},{128,160},{160,128},{192,224},{224,1... | collective-permute-start | bytes 1769480 | tf_op jit(solution)/shard_map/ppermute | solution.py:314

commit v5 on v4

--- a/solution.py
+++ b/solution.py
@@ -346,22 +346,24 @@
 
 def widened(inputs, cotangent):
     lond = inputs.shape[2]
-    both = jnp.concatenate([inputs, cotangent[:, 1:]], axis=1)
-    down = routed(both, "lat", 1, False)
-    both = jnp.concatenate([inputs, cotangent[:, :1]], axis=1)
-    up = routed(both, "lat", -1, False)
-    down_far = routed(inputs[:, 1:], "lat", 2, False)
-    up_far = routed(inputs[:, :1], "lat", -2, False)
+    lats = lax.axis_size("lat")
+    core = lax.axis_index("lat") % 2
+    own = jnp.concatenate([inputs, cotangent], axis=1)
+    mate = lax.ppermute(own, "lat", [(i, i ^ 1) for i in range(lats)])
+    first = jnp.where(core == 0, own, mate)
+    second = jnp.where(core == 0, mate, own)
+    up = routed(
+        jnp.concatenate([first[:, 1:2], second[:, :2], second[:, 3:]], axis=1), "lat", 2, False
+    )
+    down = routed(
+        jnp.concatenate([first[:, :2], second[:, :1], first[:, 2:3]], axis=1), "lat", -2, False
+    )
+    field = jnp.concatenate([up[:, :3], first[:, :2], second[:, :2], down[:, :3]], axis=1)
+    grad = jnp.concatenate([up[:, 3:], first[:, 2:], second[:, 2:], down[:, 3:]], axis=1)
     lines = jnp.concatenate(
         [
-            down_far,
-            down[:, :2],
-            inputs,
-            up[:, :2],
-            up_far,
-            down[:, 2:],
-            cotangent,
-            up[:, 2:],
+            jnp.where(core == 0, field[:, :8], field[:, 2:]),
+            jnp.where(core == 0, grad[:, :4], grad[:, 2:]),
         ],
         axis=1,
     )

time: 130 us -> 129 us (level)
  starting transfers between devices: 43 us -> 38.7 us
  waiting for transfers between devices: 10 us -> 12.9 us
  local copies, waits for them, and re-layouts: 6.54 us -> 5.2 us
    ppermute x6 -> x4, starting transfers between devices: 27.6 us -> 12.8 us  [routed(): return lax.ppermute(block, axis, route)]
    ppermute x0 -> x1, starting transfers between devices: none -> 8.79 us  [widened(): mate = lax.ppermute(own, 'lat', [(i, i ^ 1) for i in range(lats)])]
    slice x3 -> x7, local copies, waits for them, and re-layouts: 2.13 us -> 0.08 us  [the longest x1 0.02 us: widened(): first[:, 1:2]]
    ppermute x1, starting transfers between devices: 2.63 us -> 4.62 us  [shards(): lax.ppermute(other_near, 'lat', [(i, i ^ 1) for i in range(lax.axis_size(...]
    ppermute x6 -> x4, waiting for transfers between devices: 7.19 us -> 9.07 us  [routed(): return lax.ppermute(block, axis, route)]
    unnamed x30 -> x17, local copies, waits for them, and re-layouts: 2.91 us -> 2.73 us
  transfers between devices with their start and end apart: 10 -> 9, of which waited for: 4 -> 6; matrix products, arithmetic and copies ran while one was open for 5% -> 4% of each run, Pallas kernels for 2% -> 2%
where the time goes in v5:
time: 129 us; the launch traced here: 128 us
  blocking collectives  55 us (43%)
  starting transfers between devices  38.7 us (30%)
  waiting for transfers between devices  12.9 us (10%)
  Pallas kernels  9.87 us (8%)
  other arithmetic  5.21 us (4%)
  local copies, waits for them, and re-layouts  5.2 us (4%)
    all_to_all x1, blocking collectives, gathered_sum(): own = lax.all_to_all(own, 'lon', 0, 0, axis_index_groups=apart)  16.3 us
    all_to_all x1, blocking collectives, gathered_sum(): own = lax.all_to_all(own, ('lat', 'lon'), 0, 0, axis_index_groups=near)  14.1 us
    all_to_all x2, blocking collectives, gathered_sum(): own = lax.all_to_all(own, 'lon', 0, 0, axis_index_groups=beside)  14 us
    ppermute x4, starting transfers between devices, routed(): return lax.ppermute(block, axis, route)  12.8 us
    all_to_all x1, blocking collectives, gathered_sum(): lax.all_to_all(own, ('lat', 'lon'), 0, 0, axis_index_groups=near)  10.7 us
    ppermute x4, waiting for transfers between devices, routed(): return lax.ppermute(block, axis, route)  9.07 us
    ppermute x1, starting transfers between devices, widened(): mate = lax.ppermute(own, 'lat', [(i, i ^ 1) for i in range(lats)])  8.79 us
    ppermute x1, starting transfers between devices, gathered_sum(): other = lax.ppermute(own, 'lat', swap)  8.67 us
  transfers between devices with their start and end apart: 9, of which 6 were waited for; matrix products, arithmetic and copies ran while one was open for 4% of the time, Pallas kernels for 2%

profile of v5, /device:TPU:1, one launch (start us, length us, event | category | flops | bytes accessed | tf_op | source)
XLA Modules:
  0.0 128.0 jit_solution(5524429605385641118)
XLA Ops:
  0.6 0.9 copy_dynamic-update-slice_fusion.1
  1.5 0.9 copy_dynamic-update-slice_fusion
  2.5 8.8 %collective-permute-start = (bf16[2,4,45,256]{3,2,1,0:T(8,128)(2,1)S(1)}, bf16[2,4,45,256]{3,2,1,0:T(8,128)(2,1)S(1)}, u32[]{:S(2)}, u32[]{:S(2)}) collective-permute-start(bf16[2,4,45,256]{3,2,1,0:T(8,128)(2,1)S(1)} %copy_dynamic-update-slice_fusion), channel_id=1, source_target_pairs={{0,32},{32,0},{64,96},{96,64},{128,160},{160,128},{192,224},{224,1... | collective-permute-start | bytes 552968 | tf_op jit(solution)/shard_map/ppermute | solution.py:352
  11.3 0.0 copy-start
  11.3 1.0 collective-permute-done
  12.4 1.3 %collective-permute-start.1 = (bf16[2,4,45,256]{3,2,1,0:T(8,128)(2,1)S(1)}, bf16[2,4,45,256]{3,2,1,0:T(8,128)(2,1)S(1)}, u32[]{:S(2)}, u32[]{:S(2)}) collective-permute-start(bf16[2,4,45,256]{3,2,1,0:T(8,128)(2,1)S(1)} %pad_maximum_fusion.6), channel_id=1, source_target_pairs={{0,64},{32,96},{64,128},{96,160},{128,192},{160,224},{1,65},{33,97... | collective-permute-start | bytes 552968 | tf_op jit(solution)/shard_map/ppermute | solution.py:29
  13.8 1.3 %collective-permute-start.2 = (bf16[2,4,45,256]{3,2,1,0:T(8,128)(2,1)S(1)}, bf16[2,4,45,256]{3,2,1,0:T(8,128)(2,1)S(1)}, u32[]{:S(2)}, u32[]{:S(2)}) collective-permute-start(bf16[2,4,45,256]{3,2,1,0:T(8,128)(2,1)S(1)} %pad_maximum_fusion.7), channel_id=1, source_target_pairs={{64,0},{96,32},{128,64},{160,96},{192,128},{224,160},{65,1},{97,33... | collective-permute-start | bytes 552968 | tf_op jit(solution)/shard_map/ppermute | solution.py:29
  15.1 0.9 dynamic-slice_bitcast_fusion
  16.0 1.9 %collective-permute-start.5 = (bf16[1152,256]{1,0:T(8,128)(2,1)}, bf16[1152,256]{1,0:T(8,128)(2,1)S(1)}, u32[]{:S(2)}, u32[]{:S(2)}) collective-permute-start(bf16[1152,256]{1,0:T(8,128)(2,1)} %dynamic-slice_bitcast_fusion), channel_id=1, source_target_pairs={{0,272},{1,273},{2,274},{3,275},{4,276},{5,277},{6,278},{7,279},{8... | collective-permute-start | bytes 1769480 | tf_op jit(solution)/shard_map/ppermute | solution.py:388
  17.9 0.1 collective-permute-done.1
  18.0 3.8 %collective-permute-done.2 = bf16[2,4,45,256]{3,2,1,0:T(8,128)(2,1)S(1)} collective-permute-done((bf16[2,4,45,256]{3,2,1,0:T(8,128)(2,1)S(1)}, bf16[2,4,45,256]{3,2,1,0:T(8,128)(2,1)S(1)}, u32[]{:S(2)}, u32[]{:S(2)}) %collective-permute-start.2) | collective-permute-done | bytes 184352 | tf_op jit(solution)/shard_map/ppermute | solution.py:29
  21.8 0.1 pad_maximum_fusion
  21.9 0.0 copy-start.4
  21.9 0.0 copy-start.5
  22.0 0.9 pad_maximum_fusion.1
  23.0 8.3 %collective-permute-start.4 = (bf16[2,12,24,256]{3,2,1,0:T(8,128)(2,1)}, bf16[2,12,24,256]{3,2,1,0:T(8,128)(2,1)}, u32[]{:S(2)}, u32[]{:S(2)}) collective-permute-start(bf16[2,12,24,256]{3,2,1,0:T(8,128)(2,1)} %get-tuple-element.32), channel_id=1, source_target_pairs={{0,31},{1,0},{2,1},{3,2},{4,3},{5,4},{6,5},{7,6},{8,7},{9,8},{10,9... | collective-permute-start | bytes 884744 | tf_op jit(solution)/shard_map/ppermute | solution.py:29
  31.2 1.9 %collective-permute-start.3 = (bf16[2,12,24,256]{3,2,1,0:T(8,128)(2,1)}, bf16[2,12,24,256]{3,2,1,0:T(8,128)(2,1)}, u32[]{:S(2)}, u32[]{:S(2)}) collective-permute-start(bf16[2,12,24,256]{3,2,1,0:T(8,128)(2,1)} %get-tuple-element.33), channel_id=1, source_target_pairs={{0,1},{1,2},{2,3},{3,4},{4,5},{5,6},{6,7},{7,8},{8,9},{9,10},{10,1... | collective-permute-start | bytes 884744 | tf_op jit(solution)/shard_map/ppermute | solution.py:29
  33.2 0.1 fusion.2
  33.4 0.1 reshape.66.ahead
  33.6 0.1 rev.4
  33.7 0.1 pad.18.clone
  33.8 2.2 %tables.1 = (bf16[54,48,256]{2,1,0:T(8,128)(2,1)S(1)}, bf16[12,80,640]{2,1,0:T(8,128)(2,1)S(1)}) custom-call(f32[6,9,256]{2,1,0:T(8,128)S(1)} %reshape.66.ahead, f32[12,9,128]{2,1,0:T(8,128)S(1)} %bitcast.29), custom_call_target="tpu_custom_call" | custom-call | tf_op jit(solution)/shard_map/tables/pallas_call | solution.py:76
  36.0 0.0 copy-start.1
  36.1 1.0 copy-done.1
  37.1 0.0 collective-permute-done.5.other_near
  37.1 5.2 %collective-permute-done.3 = bf16[2,12,24,256]{3,2,1,0:T(8,128)(2,1)} collective-permute-done((bf16[2,12,24,256]{3,2,1,0:T(8,128)(2,1)}, bf16[2,12,24,256]{3,2,1,0:T(8,128)(2,1)}, u32[]{:S(2)}, u32[]{:S(2)}) %collective-permute-start.3) | collective-permute-done | bytes 294944 | tf_op jit(solution)/shard_map/ppermute | solution.py:29
  42.3 4.6 %collective-permute-start.6 = (bf16[1152,256]{1,0:T(8,128)(2,1)S(1)}, bf16[1152,256]{1,0:T(8,128)(2,1)}, u32[]{:S(2)}, u32[]{:S(2)}) collective-permute-start(bf16[1152,256]{1,0:T(8,128)(2,1)S(1)} %collective-permute-done.5.other_near), channel_id=1, source_target_pairs={{0,32},{32,0},{64,96},{96,64},{128,160},{160,128},{192,224},{224,1... | collective-permute-start | bytes 1769480 | tf_op jit(solution)/shard_map/ppermute | solution.py:392
  46.9 0.0 copy-start.2
  46.9 0.1 pad.25.clone
  47.0 0.1 pad_add_fusion.flags
  47.1 1.9 %maximum_maximum_fusion.field = bf16[2,12,112,256]{3,2,1,0:T(8,128)(2,1)S(1)} fusion(bf16[2,12,24,256]{3,2,1,0:T(8,128)(2,1)} %collective-permute-done.4, bf16[2,4,45,256]{3,2,1,0:T(8,128)(2,1)S(1)} %fusion.1, bf16[2,8,45,256]{3,2,1,0:T(8,128)(2,1)} %copy-done.3, bf16[2,12,24,256]{3,2,1,0:T(8,128)(2,1)} %collective-permute-done.3, bf16[112]{0:T(256)(128)(2,1)S(1)} %pad.25.clone), kind=kLoop, calls=%fused_computation | loop fusion | flops 6881280 | bytes 2519264 | tf_op jit(solution)/shard_map/concatenate | solution.py:378
  49.0 0.0 collective-permute-done.6.other_far
  49.0 7.6 %sphere.1 = (bf16[2,2,45,256]{3,2,1,0:T(8,128)(2,1)S(1)}, f32[1152,256]{1,0:T(8,128)S(1)}, bf16[1152,256]{1,0:T(8,128)(2,1)S(1)}) custom-call(s32[2]{0:T(128)S(1)} %pad_add_fusion.flags, bf16[54,48,256]{2,1,0:T(8,128)(2,1)S(1)} %get-tuple-element.14.table, bf16[12,80,640]{2,1,0:T(8,128)(2,1)S(1)} %copy-done.2, ...), custom_call_target="tpu_custom_call" | custom-call | tf_op jit(solution)/shard_map/sphere/pallas_call | solution.py:251
  56.6 1.9 %collective-permute-start.7 = (bf16[1152,256]{1,0:T(8,128)(2,1)S(1)}, bf16[1152,256]{1,0:T(8,128)(2,1)S(1)}, u32[]{:S(2)}, u32[]{:S(2)}) collective-permute-start(bf16[1152,256]{1,0:T(8,128)(2,1)S(1)} %get-tuple-element.21), channel_id=1, source_target_pairs={{0,32},{32,0},{64,96},{96,64},{128,160},{160,128},{192,224},{224,1... | collective-permute-start | bytes 1769480 | tf_op jit(solution)/shard_map/ppermute | solution.py:298
  58.6 1.9 %collective-permute-done.7 = bf16[1152,256]{1,0:T(8,128)(2,1)S(1)} collective-permute-done((bf16[1152,256]{1,0:T(8,128)(2,1)S(1)}, bf16[1152,256]{1,0:T(8,128)(2,1)S(1)}, u32[]{:S(2)}, u32[]{:S(2)}) %collective-permute-start.7) | collective-permute-done | bytes 589856 | tf_op jit(solution)/shard_map/ppermute | solution.py:298
  60.5 0.1 add_convert_fusion
  60.7 14.1 %all_to_all.25 = bf16[8,144,256]{2,1,0:T(8,128)(2,1)S(1)} all-to-all(bf16[8,144,256]{2,1,0:T(8,128)(2,1)S(1)} %bitcast.32), channel_id=1, replica_groups={{0,16,64,80,128,144,192,208},{1,17,65,81,129,145,193,209},{2,18,66,82,1..., dimensions={0} | all-to-all | bytes 1179648 | tf_op jit(solution)/shard_map/all_to_all | solution.py:300
  74.7 0.1 reduce_sum.36
  74.9 7.0 %all_to_all.26 = bf16[4,72,128]{2,1,0:T(8,128)(2,1)S(1)} all-to-all(bf16[4,72,128]{2,1,0:T(8,128)(2,1)S(1)} %bitcast.34), channel_id=1, replica_groups={{0,1,2,3},{4,5,6,7},{8,9,10,11},{12,13,14,15},{16,17,18,19},{20,21,22,2..., dimensions={0} | all-to-all | bytes 147456 | tf_op jit(solution)/shard_map/all_to_all | solution.py:304
  81.9 16.3 %all_to_all.27 = bf16[4,72,128]{2,1,0:T(8,128)(2,1)S(1)} all-to-all(bf16[4,72,128]{2,1,0:T(8,128)(2,1)S(1)} %broadcast_in_dim.33), channel_id=1, replica_groups={{0,4,8,12},{1,5,9,13},{2,6,10,14},{3,7,11,15},{16,20,24,28},{17,21,25,2..., dimensions={0} | all-to-all | bytes 147456 | tf_op jit(solution)/shard_map/all_to_all | solution.py:307
  98.2 7.0 %all_to_all.28 = bf16[4,72,128]{2,1,0:T(8,128)(2,1)S(1)} all-to-all(bf16[4,72,128]{2,1,0:T(8,128)(2,1)S(1)} %broadcast_in_dim.34), channel_id=1, replica_groups={{0,1,2,3},{4,5,6,7},{8,9,10,11},{12,13,14,15},{16,17,18,19},{20,21,22,2..., dimensions={0} | all-to-all | bytes 147456 | tf_op jit(solution)/shard_map/all_to_all | solution.py:310
  105.2 0.1 copy.32
  105.3 10.7 %all_to_all.29 = bf16[8,144,256]{2,1,0:T(8,128)(2,1)S(1)} all-to-all(bf16[8,144,256]{2,1,0:T(8,128)(2,1)S(1)} %broadcast_in_dim.36), channel_id=1, replica_groups={{0,16,64,80,128,144,192,208},{1,17,65,81,129,145,193,209},{2,18,66,82,1..., dimensions={0} | all-to-all | bytes 1179648 | tf_op jit(solution)/shard_map/all_to_all | solution.py:313
  116.0 8.7 %collective-permute-start.8 = (bf16[1152,256]{1,0:T(8,128)(2,1)S(1)}, bf16[1152,256]{1,0:T(8,128)(2,1)S(1)}, u32[]{:S(2)}, u32[]{:S(2)}) collective-permute-start(bf16[1152,256]{1,0:T(8,128)(2,1)S(1)} %bitcast.31), channel_id=1, source_target_pairs={{0,32},{32,0},{64,96},{96,64},{128,160},{160,128},{192,224},{224,1... | collective-permute-start | bytes 1769480 | tf_op jit(solution)/shard_map/ppermute | solution.py:314
  124.7 0.7 copy.33
  125.4 0.9 collective-permute-done.8
  126.3 0.1 select_bitcast_fusion.1
  126.4 1.6 %maximum_convert_fusion = f32[1,2304,256]{2,1,0:T(8,128)} fusion(bf16[1,1152,256]{2,1,0:T(8,128)(2,1)S(1)} %get-tuple-element.31, bf16[1,1152,256]{2,1,0:T(8,128)(2,1)S(1)} %get-tuple-element.30), kind=kLoop, calls=%fused_computation.1 | loop fusion | flops 2359296 | bytes 3538944 | tf_op jit(solution)/shard_map/convert_element_type | solution.py:317
  (34 shorter events, 0.5 us)
Async XLA Ops:
  2.5 9.8 %collective-permute-start = (bf16[2,4,45,256]{3,2,1,0:T(8,128)(2,1)S(1)}, bf16[2,4,45,256]{3,2,1,0:T(8,128)(2,1)S(1)}, u32[]{:S(2)}, u32[]{:S(2)}) collective-permute-start(bf16[2,4,45,256]{3,2,1,0:T(8,128)(2,1)S(1)} %copy_dynamic-update-slice_fusion), channel_id=1, source_target_pairs={{0,32},{32,0},{64,96},{96,64},{128,160},{160,128},{192,224},{224,1... | collective-permute-start | bytes 552968 | tf_op jit(solution)/shard_map/ppermute | solution.py:352
  11.3 3.8 %copy-start = (bf16[1,2304,256]{2,1,0:T(8,128)(2,1)S(1)}, bf16[1,2304,256]{2,1,0:T(8,128)(2,1)}, u32[]{:S(2)}) copy-start(bf16[1,2304,256]{2,1,0:T(8,128)(2,1)} %param.7) | copy-start | bytes 3538948
  12.4 5.5 %collective-permute-start.1 = (bf16[2,4,45,256]{3,2,1,0:T(8,128)(2,1)S(1)}, bf16[2,4,45,256]{3,2,1,0:T(8,128)(2,1)S(1)}, u32[]{:S(2)}, u32[]{:S(2)}) collective-permute-start(bf16[2,4,45,256]{3,2,1,0:T(8,128)(2,1)S(1)} %pad_maximum_fusion.6), channel_id=1, source_target_pairs={{0,64},{32,96},{64,128},{96,160},{128,192},{160,224},{1,65},{33,97... | collective-permute-start | bytes 552968 | tf_op jit(solution)/shard_map/ppermute | solution.py:29
  13.8 8.0 %collective-permute-start.2 = (bf16[2,4,45,256]{3,2,1,0:T(8,128)(2,1)S(1)}, bf16[2,4,45,256]{3,2,1,0:T(8,128)(2,1)S(1)}, u32[]{:S(2)}, u32[]{:S(2)}) collective-permute-start(bf16[2,4,45,256]{3,2,1,0:T(8,128)(2,1)S(1)} %pad_maximum_fusion.7), channel_id=1, source_target_pairs={{64,0},{96,32},{128,64},{160,96},{192,128},{224,160},{65,1},{97,33... | collective-permute-start | bytes 552968 | tf_op jit(solution)/shard_map/ppermute | solution.py:29
  16.0 21.1 %collective-permute-start.5 = (bf16[1152,256]{1,0:T(8,128)(2,1)}, bf16[1152,256]{1,0:T(8,128)(2,1)S(1)}, u32[]{:S(2)}, u32[]{:S(2)}) collective-permute-start(bf16[1152,256]{1,0:T(8,128)(2,1)} %dynamic-slice_bitcast_fusion), channel_id=1, source_target_pairs={{0,272},{1,273},{2,274},{3,275},{4,276},{5,277},{6,278},{7,279},{8... | collective-permute-start | bytes 1769480 | tf_op jit(solution)/shard_map/ppermute | solution.py:388
  21.9 11.3 %copy-start.4 = (bf16[9,16,3,17]{3,1,2,0:T(8,128)(2,1)S(1)}, bf16[9,16,3,17]{3,1,2,0:T(8,128)(2,1)}, u32[]{:S(2)}) copy-start(bf16[9,16,3,17]{3,1,2,0:T(8,128)(2,1)} %param.8) | copy-start | bytes 44068
  21.9 11.3 %copy-start.5 = (s32[16,3]{0,1:T(4,128)S(1)}, s32[16,3]{0,1:T(4,128)}, u32[]{:S(2)}) copy-start(s32[16,3]{0,1:T(4,128)} %param.9) | copy-start | bytes 580
  21.9 11.5 %copy-start.3 = (bf16[2,8,45,256]{3,2,1,0:T(8,128)(2,1)}, bf16[2,8,45,256]{3,2,1,0:T(8,128)(2,1)S(1)}, u32[]{:S(2)}) copy-start(bf16[2,8,45,256]{3,2,1,0:T(8,128)(2,1)S(1)} %slice_select_fusion) | copy-start | bytes 1105924
  23.0 14.1 %collective-permute-start.4 = (bf16[2,12,24,256]{3,2,1,0:T(8,128)(2,1)}, bf16[2,12,24,256]{3,2,1,0:T(8,128)(2,1)}, u32[]{:S(2)}, u32[]{:S(2)}) collective-permute-start(bf16[2,12,24,256]{3,2,1,0:T(8,128)(2,1)} %get-tuple-element.32), channel_id=1, source_target_pairs={{0,31},{1,0},{2,1},{3,2},{4,3},{5,4},{6,5},{7,6},{8,7},{9,8},{10,9... | collective-permute-start | bytes 884744 | tf_op jit(solution)/shard_map/ppermute | solution.py:29
  31.2 11.0 %collective-permute-start.3 = (bf16[2,12,24,256]{3,2,1,0:T(8,128)(2,1)}, bf16[2,12,24,256]{3,2,1,0:T(8,128)(2,1)}, u32[]{:S(2)}, u32[]{:S(2)}) collective-permute-start(bf16[2,12,24,256]{3,2,1,0:T(8,128)(2,1)} %get-tuple-element.33), channel_id=1, source_target_pairs={{0,1},{1,2},{2,3},{3,4},{4,5},{5,6},{6,7},{7,8},{8,9},{9,10},{10,1... | collective-permute-start | bytes 884744 | tf_op jit(solution)/shard_map/ppermute | solution.py:29
  36.0 1.0 copy-start.1
  42.3 6.7 %collective-permute-start.6 = (bf16[1152,256]{1,0:T(8,128)(2,1)S(1)}, bf16[1152,256]{1,0:T(8,128)(2,1)}, u32[]{:S(2)}, u32[]{:S(2)}) collective-permute-start(bf16[1152,256]{1,0:T(8,128)(2,1)S(1)} %collective-permute-done.5.other_near), channel_id=1, source_target_pairs={{0,32},{32,0},{64,96},{96,64},{128,160},{160,128},{192,224},{224,1... | collective-permute-start | bytes 1769480 | tf_op jit(solution)/shard_map/ppermute | solution.py:392
  46.9 2.1 %copy-start.2 = (bf16[12,80,640]{2,1,0:T(8,128)(2,1)S(1)}, bf16[12,80,640]{2,1,0:T(8,128)(2,1)}, u32[]{:S(2)}) copy-start(bf16[12,80,640]{2,1,0:T(8,128)(2,1)} %copy-done.1) | copy-start | bytes 3686404
  56.6 3.9 %collective-permute-start.7 = (bf16[1152,256]{1,0:T(8,128)(2,1)S(1)}, bf16[1152,256]{1,0:T(8,128)(2,1)S(1)}, u32[]{:S(2)}, u32[]{:S(2)}) collective-permute-start(bf16[1152,256]{1,0:T(8,128)(2,1)S(1)} %get-tuple-element.21), channel_id=1, source_target_pairs={{0,32},{32,0},{64,96},{96,64},{128,160},{160,128},{192,224},{224,1... | collective-permute-start | bytes 1769480 | tf_op jit(solution)/shard_map/ppermute | solution.py:298
  116.0 10.3 %collective-permute-start.8 = (bf16[1152,256]{1,0:T(8,128)(2,1)S(1)}, bf16[1152,256]{1,0:T(8,128)(2,1)S(1)}, u32[]{:S(2)}, u32[]{:S(2)}) collective-permute-start(bf16[1152,256]{1,0:T(8,128)(2,1)S(1)} %bitcast.31), channel_id=1, source_target_pairs={{0,32},{32,0},{64,96},{96,64},{128,160},{160,128},{192,224},{224,1... | collective-permute-start | bytes 1769480 | tf_op jit(solution)/shard_map/ppermute | solution.py:314

commit v6 on v5

--- a/solution.py
+++ b/solution.py
@@ -312,9 +312,11 @@
     own = jnp.broadcast_to(own[None], (columns,) + own.shape)
     own = lax.all_to_all(own, ("lat", "lon"), 0, 0, axis_index_groups=near).reshape(-1, chans)
     other = lax.ppermute(own, "lat", swap)
-    first = jnp.where(core == 0, own, other)
-    second = jnp.where(core == 0, other, own)
-    return jnp.concatenate([first, second], axis=0).astype(jnp.float32)
+    whole = jnp.zeros((2 * half, chans), jnp.float32)
+    whole = lax.dynamic_update_slice_in_dim(whole, own.astype(jnp.float32), core * half, 0)
+    return lax.dynamic_update_slice_in_dim(
+        whole, other.astype(jnp.float32), (1 - core) * half, 0
+    )
 
 
 def tap_rows(psi, band_half, lat_start):
@@ -367,8 +369,8 @@
         ],
         axis=1,
     )
+    right = routed(lines[:, :, :EDGE], "lon", -1, True)
     left = routed(lines[:, :, lond - EDGE :], "lon", 1, True)
-    right = routed(lines[:, :, :EDGE], "lon", -1, True)
     return lines, left, right
 
 

time: 129 us -> 130 us (level)
  blocking collectives: 55 us -> 60.4 us
  waiting for transfers between devices: 12.9 us -> 8.64 us
  local copies, waits for them, and re-layouts: 5.2 us -> 6.75 us
  other arithmetic: 5.21 us -> 3.73 us
    all_to_all x1, blocking collectives: 16.3 us -> 21.5 us  [gathered_sum(): own = lax.all_to_all(own, 'lon', 0, 0, axis_index_groups=apart)]
    ppermute x4, waiting for transfers between devices: 9.07 us -> 5.06 us  [routed(): return lax.ppermute(block, axis, route)]
    convert_element_type x1 -> x0, other arithmetic: 1.59 us -> none  [gathered_sum(): return jnp.concatenate([first, second], axis=0).astype(jnp.float32)]
    unnamed x17 -> x19, local copies, waits for them, and re-layouts: 2.73 us -> 4.13 us
  transfers between devices with their start and end apart: 9 -> 9, of which waited for: 6 -> 7; matrix products, arithmetic and copies ran while one was open for 4% -> 4% of each run, Pallas kernels for 2% -> 2%
where the time goes in v6:
time: 130 us; the launch traced here: 129 us
  blocking collectives  60.4 us (46%)
  starting transfers between devices  38.5 us (30%)
  Pallas kernels  9.88 us (8%)
  waiting for transfers between devices  8.64 us (7%)
  local copies, waits for them, and re-layouts  6.75 us (5%)
  other arithmetic  3.73 us (3%)
    all_to_all x1, blocking collectives, gathered_sum(): own = lax.all_to_all(own, 'lon', 0, 0, axis_index_groups=apart)  21.5 us
    all_to_all x1, blocking collectives, gathered_sum(): own = lax.all_to_all(own, ('lat', 'lon'), 0, 0, axis_index_groups=near)  14.1 us
    all_to_all x2, blocking collectives, gathered_sum(): own = lax.all_to_all(own, 'lon', 0, 0, axis_index_groups=beside)  14.1 us
    ppermute x4, starting transfers between devices, routed(): return lax.ppermute(block, axis, route)  12.8 us
    all_to_all x1, blocking collectives, gathered_sum(): lax.all_to_all(own, ('lat', 'lon'), 0, 0, axis_index_groups=near)  10.7 us
    ppermute x1, starting transfers between devices, widened(): mate = lax.ppermute(own, 'lat', [(i, i ^ 1) for i in range(lats)])  8.79 us
    ppermute x1, starting transfers between devices, gathered_sum(): other = lax.ppermute(own, 'lat', swap)  8.77 us
    pallas_call x1, Pallas kernels, on_device(): pl.pallas_call(device_kernel, out_shape=(jax.ShapeDtypeStruct((2, 2, lond...  7.65 us
  transfers between devices with their start and end apart: 9, of which 7 were waited for; matrix products, arithmetic and copies ran while one was open for 4% of the time, Pallas kernels for 2%

profile of v6, /device:TPU:1, one launch (start us, length us, event | category | flops | bytes accessed | tf_op | source)
XLA Modules:
  0.0 129.0 jit_solution(10280598808778572389)
XLA Ops:
  0.6 0.9 copy_dynamic-update-slice_fusion.1
  1.5 0.9 copy_dynamic-update-slice_fusion
  2.5 8.8 %collective-permute-start = (bf16[2,4,45,256]{3,2,1,0:T(8,128)(2,1)S(1)}, bf16[2,4,45,256]{3,2,1,0:T(8,128)(2,1)S(1)}, u32[]{:S(2)}, u32[]{:S(2)}) collective-permute-start(bf16[2,4,45,256]{3,2,1,0:T(8,128)(2,1)S(1)} %copy_dynamic-update-slice_fusion), channel_id=1, source_target_pairs={{0,32},{32,0},{64,96},{96,64},{128,160},{160,128},{192,224},{224,1... | collective-permute-start | bytes 552968 | tf_op jit(solution)/shard_map/ppermute | solution.py:354
  11.3 0.0 copy-start
  11.3 1.0 collective-permute-done
  12.4 1.3 %collective-permute-start.1 = (bf16[2,4,45,256]{3,2,1,0:T(8,128)(2,1)S(1)}, bf16[2,4,45,256]{3,2,1,0:T(8,128)(2,1)S(1)}, u32[]{:S(2)}, u32[]{:S(2)}) collective-permute-start(bf16[2,4,45,256]{3,2,1,0:T(8,128)(2,1)S(1)} %pad_maximum_fusion.6), channel_id=1, source_target_pairs={{0,64},{32,96},{64,128},{96,160},{128,192},{160,224},{1,65},{33,97... | collective-permute-start | bytes 552968 | tf_op jit(solution)/shard_map/ppermute | solution.py:29
  13.8 1.3 %collective-permute-start.2 = (bf16[2,4,45,256]{3,2,1,0:T(8,128)(2,1)S(1)}, bf16[2,4,45,256]{3,2,1,0:T(8,128)(2,1)S(1)}, u32[]{:S(2)}, u32[]{:S(2)}) collective-permute-start(bf16[2,4,45,256]{3,2,1,0:T(8,128)(2,1)S(1)} %pad_maximum_fusion.7), channel_id=1, source_target_pairs={{64,0},{96,32},{128,64},{160,96},{192,128},{224,160},{65,1},{97,33... | collective-permute-start | bytes 552968 | tf_op jit(solution)/shard_map/ppermute | solution.py:29
  15.1 0.9 dynamic-slice_bitcast_fusion
  16.0 1.9 %collective-permute-start.5 = (bf16[1152,256]{1,0:T(8,128)(2,1)}, bf16[1152,256]{1,0:T(8,128)(2,1)S(1)}, u32[]{:S(2)}, u32[]{:S(2)}) collective-permute-start(bf16[1152,256]{1,0:T(8,128)(2,1)} %dynamic-slice_bitcast_fusion), channel_id=1, source_target_pairs={{0,272},{1,273},{2,274},{3,275},{4,276},{5,277},{6,278},{7,279},{8... | collective-permute-start | bytes 1769480 | tf_op jit(solution)/shard_map/ppermute | solution.py:390
  17.9 0.1 collective-permute-done.1
  18.0 3.8 %collective-permute-done.2 = bf16[2,4,45,256]{3,2,1,0:T(8,128)(2,1)S(1)} collective-permute-done((bf16[2,4,45,256]{3,2,1,0:T(8,128)(2,1)S(1)}, bf16[2,4,45,256]{3,2,1,0:T(8,128)(2,1)S(1)}, u32[]{:S(2)}, u32[]{:S(2)}) %collective-permute-start.2) | collective-permute-done | bytes 184352 | tf_op jit(solution)/shard_map/ppermute | solution.py:29
  21.8 0.1 pad_maximum_fusion
  21.9 0.0 copy-start.5
  22.0 0.9 pad_maximum_fusion.1
  23.0 1.9 %collective-permute-start.3 = (bf16[2,12,24,256]{3,2,1,0:T(8,128)(2,1)}, bf16[2,12,24,256]{3,2,1,0:T(8,128)(2,1)}, u32[]{:S(2)}, u32[]{:S(2)}) collective-permute-start(bf16[2,12,24,256]{3,2,1,0:T(8,128)(2,1)} %get-tuple-element.31), channel_id=1, source_target_pairs={{0,1},{1,2},{2,3},{3,4},{4,5},{5,6},{6,7},{7,8},{8,9},{9,10},{10,1... | collective-permute-start | bytes 884744 | tf_op jit(solution)/shard_map/ppermute | solution.py:29
  24.9 8.3 %collective-permute-start.4 = (bf16[2,12,24,256]{3,2,1,0:T(8,128)(2,1)}, bf16[2,12,24,256]{3,2,1,0:T(8,128)(2,1)}, u32[]{:S(2)}, u32[]{:S(2)}) collective-permute-start(bf16[2,12,24,256]{3,2,1,0:T(8,128)(2,1)} %get-tuple-element.30), channel_id=1, source_target_pairs={{0,31},{1,0},{2,1},{3,2},{4,3},{5,4},{6,5},{7,6},{8,7},{9,8},{10,9... | collective-permute-start | bytes 884744 | tf_op jit(solution)/shard_map/ppermute | solution.py:29
  33.2 0.1 fusion.2
  33.4 0.1 reshape.53.ahead
  33.6 0.1 rev.4
  33.7 0.1 pad.18.clone
  33.8 2.2 %tables.1 = (bf16[54,48,256]{2,1,0:T(8,128)(2,1)S(1)}, bf16[12,80,640]{2,1,0:T(8,128)(2,1)S(1)}) custom-call(f32[6,9,256]{2,1,0:T(8,128)S(1)} %reshape.53.ahead, f32[12,9,128]{2,1,0:T(8,128)S(1)} %bitcast.30), custom_call_target="tpu_custom_call" | custom-call | tf_op jit(solution)/shard_map/tables/pallas_call | solution.py:76
  36.0 0.0 copy-start.1
  36.1 1.0 copy-done.1
  37.1 0.3 collective-permute-done.3
  37.3 0.9 collective-permute-done.4
  38.2 4.3 %collective-permute-start.6 = (bf16[1152,256]{1,0:T(8,128)(2,1)S(1)}, bf16[1152,256]{1,0:T(8,128)(2,1)}, u32[]{:S(2)}, u32[]{:S(2)}) collective-permute-start(bf16[1152,256]{1,0:T(8,128)(2,1)S(1)} %collective-permute-done.5.other_near), channel_id=1, source_target_pairs={{0,32},{32,0},{64,96},{96,64},{128,160},{160,128},{192,224},{224,1... | collective-permute-start | bytes 1769480 | tf_op jit(solution)/shard_map/ppermute | solution.py:394
  42.6 0.0 copy-start.2
  42.6 0.1 pad.23.clone
  42.7 0.1 pad_add_fusion.flags
  42.8 1.9 %maximum_maximum_fusion.field = bf16[2,12,112,256]{3,2,1,0:T(8,128)(2,1)S(1)} fusion(bf16[2,12,24,256]{3,2,1,0:T(8,128)(2,1)} %collective-permute-done.4, bf16[2,4,45,256]{3,2,1,0:T(8,128)(2,1)S(1)} %fusion.1, bf16[2,8,45,256]{3,2,1,0:T(8,128)(2,1)} %copy-done.3, bf16[2,12,24,256]{3,2,1,0:T(8,128)(2,1)} %collective-permute-done.3, bf16[112]{0:T(256)(128)(2,1)S(1)} %pad.23.clone), kind=kLoop, calls=%fused_computation | loop fusion | flops 6881280 | bytes 2519264 | tf_op jit(solution)/shard_map/concatenate | solution.py:380
  44.7 7.7 %sphere.1 = (bf16[2,2,45,256]{3,2,1,0:T(8,128)(2,1)S(1)}, f32[1152,256]{1,0:T(8,128)S(1)}, bf16[1152,256]{1,0:T(8,128)(2,1)S(1)}) custom-call(s32[2]{0:T(128)S(1)} %pad_add_fusion.flags, bf16[54,48,256]{2,1,0:T(8,128)(2,1)S(1)} %get-tuple-element.14.table, bf16[12,80,640]{2,1,0:T(8,128)(2,1)S(1)} %copy-done.2, ...), custom_call_target="tpu_custom_call" | custom-call | tf_op jit(solution)/shard_map/sphere/pallas_call | solution.py:251
  52.3 1.9 %collective-permute-start.7 = (bf16[1152,256]{1,0:T(8,128)(2,1)S(1)}, bf16[1152,256]{1,0:T(8,128)(2,1)S(1)}, u32[]{:S(2)}, u32[]{:S(2)}) collective-permute-start(bf16[1152,256]{1,0:T(8,128)(2,1)S(1)} %get-tuple-element.21), channel_id=1, source_target_pairs={{0,32},{32,0},{64,96},{96,64},{128,160},{160,128},{192,224},{224,1... | collective-permute-start | bytes 1769480 | tf_op jit(solution)/shard_map/ppermute | solution.py:298
  54.3 2.0 %collective-permute-done.7 = bf16[1152,256]{1,0:T(8,128)(2,1)S(1)} collective-permute-done((bf16[1152,256]{1,0:T(8,128)(2,1)S(1)}, bf16[1152,256]{1,0:T(8,128)(2,1)S(1)}, u32[]{:S(2)}, u32[]{:S(2)}) %collective-permute-start.7) | collective-permute-done | bytes 589856 | tf_op jit(solution)/shard_map/ppermute | solution.py:298
  56.2 0.1 add_convert_fusion
  56.4 14.1 %all_to_all.25 = bf16[8,144,256]{2,1,0:T(8,128)(2,1)S(1)} all-to-all(bf16[8,144,256]{2,1,0:T(8,128)(2,1)S(1)} %bitcast.34), channel_id=1, replica_groups={{0,16,64,80,128,144,192,208},{1,17,65,81,129,145,193,209},{2,18,66,82,1..., dimensions={0} | all-to-all | bytes 1179648 | tf_op jit(solution)/shard_map/all_to_all | solution.py:300
  70.5 0.1 reduce_sum.36
  70.6 7.1 %all_to_all.26 = bf16[4,72,128]{2,1,0:T(8,128)(2,1)S(1)} all-to-all(bf16[4,72,128]{2,1,0:T(8,128)(2,1)S(1)} %bitcast.36), channel_id=1, replica_groups={{0,1,2,3},{4,5,6,7},{8,9,10,11},{12,13,14,15},{16,17,18,19},{20,21,22,2..., dimensions={0} | all-to-all | bytes 147456 | tf_op jit(solution)/shard_map/all_to_all | solution.py:304
  77.7 21.5 %all_to_all.27 = bf16[4,72,128]{2,1,0:T(8,128)(2,1)S(1)} all-to-all(bf16[4,72,128]{2,1,0:T(8,128)(2,1)S(1)} %broadcast_in_dim.41), channel_id=1, replica_groups={{0,4,8,12},{1,5,9,13},{2,6,10,14},{3,7,11,15},{16,20,24,28},{17,21,25,2..., dimensions={0} | all-to-all | bytes 147456 | tf_op jit(solution)/shard_map/all_to_all | solution.py:307
  99.3 7.0 %all_to_all.28 = bf16[4,72,128]{2,1,0:T(8,128)(2,1)S(1)} all-to-all(bf16[4,72,128]{2,1,0:T(8,128)(2,1)S(1)} %broadcast_in_dim.42), channel_id=1, replica_groups={{0,1,2,3},{4,5,6,7},{8,9,10,11},{12,13,14,15},{16,17,18,19},{20,21,22,2..., dimensions={0} | all-to-all | bytes 147456 | tf_op jit(solution)/shard_map/all_to_all | solution.py:310
  106.2 0.1 copy.32
  106.4 10.7 %all_to_all.29 = bf16[8,144,256]{2,1,0:T(8,128)(2,1)S(1)} all-to-all(bf16[8,144,256]{2,1,0:T(8,128)(2,1)S(1)} %broadcast_in_dim.44), channel_id=1, replica_groups={{0,16,64,80,128,144,192,208},{1,17,65,81,129,145,193,209},{2,18,66,82,1..., dimensions={0} | all-to-all | bytes 1179648 | tf_op jit(solution)/shard_map/all_to_all | solution.py:313
  117.1 8.8 %collective-permute-start.8 = (bf16[1152,256]{1,0:T(8,128)(2,1)S(1)}, bf16[1152,256]{1,0:T(8,128)(2,1)S(1)}, u32[]{:S(2)}, u32[]{:S(2)}) collective-permute-start(bf16[1152,256]{1,0:T(8,128)(2,1)S(1)} %bitcast.32), channel_id=1, source_target_pairs={{0,32},{32,0},{64,96},{96,64},{128,160},{160,128},{192,224},{224,1... | collective-permute-start | bytes 1769480 | tf_op jit(solution)/shard_map/ppermute | solution.py:314
  125.9 0.7 copy.33
  126.6 0.2 broadcast_in_dim.40
  126.8 0.1 convert_dynamic-update-slice_fusion.1
  126.9 0.6 collective-permute-done.8
  127.5 0.1 convert_dynamic-update-slice_fusion
  127.6 1.4 %copy-done.4 = f32[1,2304,256]{2,1,0:T(8,128)} copy-done((f32[1,2304,256]{2,1,0:T(8,128)}, f32[1,2304,256]{2,1,0:T(8,128)S(1)}, u32[]{:S(2)}) %copy-start.4) | copy-done | bytes 2359320
  (37 shorter events, 0.5 us)
Async XLA Ops:
  2.5 9.8 %collective-permute-start = (bf16[2,4,45,256]{3,2,1,0:T(8,128)(2,1)S(1)}, bf16[2,4,45,256]{3,2,1,0:T(8,128)(2,1)S(1)}, u32[]{:S(2)}, u32[]{:S(2)}) collective-permute-start(bf16[2,4,45,256]{3,2,1,0:T(8,128)(2,1)S(1)} %copy_dynamic-update-slice_fusion), channel_id=1, source_target_pairs={{0,32},{32,0},{64,96},{96,64},{128,160},{160,128},{192,224},{224,1... | collective-permute-start | bytes 552968 | tf_op jit(solution)/shard_map/ppermute | solution.py:354
  11.3 3.8 %copy-start = (bf16[1,2304,256]{2,1,0:T(8,128)(2,1)S(1)}, bf16[1,2304,256]{2,1,0:T(8,128)(2,1)}, u32[]{:S(2)}) copy-start(bf16[1,2304,256]{2,1,0:T(8,128)(2,1)} %param.7) | copy-start | bytes 3538948
  12.4 5.5 %collective-permute-start.1 = (bf16[2,4,45,256]{3,2,1,0:T(8,128)(2,1)S(1)}, bf16[2,4,45,256]{3,2,1,0:T(8,128)(2,1)S(1)}, u32[]{:S(2)}, u32[]{:S(2)}) collective-permute-start(bf16[2,4,45,256]{3,2,1,0:T(8,128)(2,1)S(1)} %pad_maximum_fusion.6), channel_id=1, source_target_pairs={{0,64},{32,96},{64,128},{96,160},{128,192},{160,224},{1,65},{33,97... | collective-permute-start | bytes 552968 | tf_op jit(solution)/shard_map/ppermute | solution.py:29
  13.8 8.0 %collective-permute-start.2 = (bf16[2,4,45,256]{3,2,1,0:T(8,128)(2,1)S(1)}, bf16[2,4,45,256]{3,2,1,0:T(8,128)(2,1)S(1)}, u32[]{:S(2)}, u32[]{:S(2)}) collective-permute-start(bf16[2,4,45,256]{3,2,1,0:T(8,128)(2,1)S(1)} %pad_maximum_fusion.7), channel_id=1, source_target_pairs={{64,0},{96,32},{128,64},{160,96},{192,128},{224,160},{65,1},{97,33... | collective-permute-start | bytes 552968 | tf_op jit(solution)/shard_map/ppermute | solution.py:29
  16.0 21.1 %collective-permute-start.5 = (bf16[1152,256]{1,0:T(8,128)(2,1)}, bf16[1152,256]{1,0:T(8,128)(2,1)S(1)}, u32[]{:S(2)}, u32[]{:S(2)}) collective-permute-start(bf16[1152,256]{1,0:T(8,128)(2,1)} %dynamic-slice_bitcast_fusion), channel_id=1, source_target_pairs={{0,272},{1,273},{2,274},{3,275},{4,276},{5,277},{6,278},{7,279},{8... | collective-permute-start | bytes 1769480 | tf_op jit(solution)/shard_map/ppermute | solution.py:390
  21.9 11.3 %copy-start.5 = (bf16[9,16,3,17]{3,1,2,0:T(8,128)(2,1)S(1)}, bf16[9,16,3,17]{3,1,2,0:T(8,128)(2,1)}, u32[]{:S(2)}) copy-start(bf16[9,16,3,17]{3,1,2,0:T(8,128)(2,1)} %param.8) | copy-start | bytes 44068
  21.9 11.3 %copy-start.6 = (s32[16,3]{0,1:T(4,128)S(1)}, s32[16,3]{0,1:T(4,128)}, u32[]{:S(2)}) copy-start(s32[16,3]{0,1:T(4,128)} %param.9) | copy-start | bytes 580
  21.9 11.5 %copy-start.3 = (bf16[2,8,45,256]{3,2,1,0:T(8,128)(2,1)}, bf16[2,8,45,256]{3,2,1,0:T(8,128)(2,1)S(1)}, u32[]{:S(2)}) copy-start(bf16[2,8,45,256]{3,2,1,0:T(8,128)(2,1)S(1)} %slice_select_fusion) | copy-start | bytes 1105924
  23.0 14.4 %collective-permute-start.3 = (bf16[2,12,24,256]{3,2,1,0:T(8,128)(2,1)}, bf16[2,12,24,256]{3,2,1,0:T(8,128)(2,1)}, u32[]{:S(2)}, u32[]{:S(2)}) collective-permute-start(bf16[2,12,24,256]{3,2,1,0:T(8,128)(2,1)} %get-tuple-element.31), channel_id=1, source_target_pairs={{0,1},{1,2},{2,3},{3,4},{4,5},{5,6},{6,7},{7,8},{8,9},{9,10},{10,1... | collective-permute-start | bytes 884744 | tf_op jit(solution)/shard_map/ppermute | solution.py:29
  24.9 13.4 %collective-permute-start.4 = (bf16[2,12,24,256]{3,2,1,0:T(8,128)(2,1)}, bf16[2,12,24,256]{3,2,1,0:T(8,128)(2,1)}, u32[]{:S(2)}, u32[]{:S(2)}) collective-permute-start(bf16[2,12,24,256]{3,2,1,0:T(8,128)(2,1)} %get-tuple-element.30), channel_id=1, source_target_pairs={{0,31},{1,0},{2,1},{3,2},{4,3},{5,4},{6,5},{7,6},{8,7},{9,8},{10,9... | collective-permute-start | bytes 884744 | tf_op jit(solution)/shard_map/ppermute | solution.py:29
  36.0 1.0 copy-start.1
  38.2 6.4 %collective-permute-start.6 = (bf16[1152,256]{1,0:T(8,128)(2,1)S(1)}, bf16[1152,256]{1,0:T(8,128)(2,1)}, u32[]{:S(2)}, u32[]{:S(2)}) collective-permute-start(bf16[1152,256]{1,0:T(8,128)(2,1)S(1)} %collective-permute-done.5.other_near), channel_id=1, source_target_pairs={{0,32},{32,0},{64,96},{96,64},{128,160},{160,128},{192,224},{224,1... | collective-permute-start | bytes 1769480 | tf_op jit(solution)/shard_map/ppermute | solution.py:394
  42.6 2.1 %copy-start.2 = (bf16[12,80,640]{2,1,0:T(8,128)(2,1)S(1)}, bf16[12,80,640]{2,1,0:T(8,128)(2,1)}, u32[]{:S(2)}) copy-start(bf16[12,80,640]{2,1,0:T(8,128)(2,1)} %copy-done.1) | copy-start | bytes 3686404
  52.3 3.9 %collective-permute-start.7 = (bf16[1152,256]{1,0:T(8,128)(2,1)S(1)}, bf16[1152,256]{1,0:T(8,128)(2,1)S(1)}, u32[]{:S(2)}, u32[]{:S(2)}) collective-permute-start(bf16[1152,256]{1,0:T(8,128)(2,1)S(1)} %get-tuple-element.21), channel_id=1, source_target_pairs={{0,32},{32,0},{64,96},{96,64},{128,160},{160,128},{192,224},{224,1... | collective-permute-start | bytes 1769480 | tf_op jit(solution)/shard_map/ppermute | solution.py:298
  117.1 10.4 %collective-permute-start.8 = (bf16[1152,256]{1,0:T(8,128)(2,1)S(1)}, bf16[1152,256]{1,0:T(8,128)(2,1)S(1)}, u32[]{:S(2)}, u32[]{:S(2)}) collective-permute-start(bf16[1152,256]{1,0:T(8,128)(2,1)S(1)} %bitcast.32), channel_id=1, source_target_pairs={{0,32},{32,0},{64,96},{96,64},{128,160},{160,128},{192,224},{224,1... | collective-permute-start | bytes 1769480 | tf_op jit(solution)/shard_map/ppermute | solution.py:314
  127.6 1.4 %copy-start.4 = (f32[1,2304,256]{2,1,0:T(8,128)}, f32[1,2304,256]{2,1,0:T(8,128)S(1)}, u32[]{:S(2)}) copy-start(f32[1,2304,256]{2,1,0:T(8,128)S(1)} %convert_dynamic-update-slice_fusion) | copy-start | bytes 7077892
